TPU v7x, 256 devices: a whole 4x4x8 slice. The times are simulated.
256 devices in a mesh: fiber: 64 (over z, y_lo, x), seg: 4 (over y_hi, core).
Axes of the slice: x: 4, y: 4 (y_hi: 2, y_lo: 2; y = y_hi * 2 + y_lo), z: 8, core: 2. Of those that a mesh axis runs over, the one named last changes fastest.
Arguments:
- raw_strain: bfloat16 [64, 8192, 2048], P('seg', 'fiber'), may hold values from -6 to 6
- fir_taps: float32 [31], replicated, may hold values from -1 to 1
- good_mask: int32 [64, 8192], P('seg', 'fiber'), may hold values from 0 to 1, as said below
Outputs:
- stacked_spectra: float32 [144, 8192, 2, 128], P('seg', 'fiber')
Inputs may be any that keep to these rules, and one draw needn't show every extreme that they name: `good_mask`: 0 or 1; some channels are 0 in every segment.
All inputs are finite; a program needn't handle non-finite values.
Results may differ from a plain program's by a relative error of at most 0.005.
Values may be sent and summed in bfloat16 or wider, within the bound.
No kernel may reach another device: no remote copies, remote signals or barrier semaphores. Data moves between devices by JAX's collectives and lax.ppermute only.
A program may use at most 192 MiB of HBM per device.

v0:
```python
import functools
import math

import jax
import jax.numpy as jnp
import numpy as np
from jax import lax
from jax.experimental import pallas as pl
from jax.experimental.pallas import tpu as pltpu
from jax.sharding import PartitionSpec as P

NF = 144
LOW = 16
SMOOTH = 4
LAGS = 128
EDGE = 16
HALF = 15

epsilon = 1e-06
water_share = 0.1

GRID = ("fiber", "seg")
VMEM = 56 * 1024 * 1024
F32 = jnp.float32
BF16 = jnp.bfloat16


def basis_rows(samples):
    times = np.arange(samples, dtype=np.int64)
    bins = np.arange(NF, dtype=np.int64) + LOW
    phase_index = bins[:, None] * times[None, :] % samples
    angles = phase_index.astype(np.float32) * np.float32(2.0 * math.pi / samples)
    rows = np.concatenate([np.cos(angles), -np.sin(angles)], axis=0)
    return jnp.asarray(rows, dtype=BF16)


def filter_band(taps, count, first, shape):
    offset = lax.broadcasted_iota(jnp.int32, shape, 0) - lax.broadcasted_iota(jnp.int32, shape, 1)
    band = jnp.zeros(shape, F32)
    for tap in range(count):
        band = jnp.where(offset == tap - first - HALF, taps[tap], band)
    return band


NT = (((1,), (1,)), ((), ()))
TN = (((0,), (0,)), ((), ()))


def dot(a, b, dims=(((1,), (0,)), ((), ()))):
    return lax.dot_general(a, b, dims, preferred_element_type=F32)


def edge_kernel(basis, first, last, head, tail):
    rows = first.shape[0] * EDGE
    samples = first.shape[2]
    head[...] = dot(basis[...], first[...].reshape(rows, samples), NT).astype(BF16)
    tail[...] = dot(basis[...], last[...].reshape(rows, samples), NT).astype(BF16)


def edge_spectra(basis, raw):
    segs, channels, samples = raw.shape
    out = jax.ShapeDtypeStruct((2 * NF, segs * EDGE), BF16)
    return pl.pallas_call(
        edge_kernel,
        grid=(1,),
        in_specs=[
            pl.BlockSpec(basis.shape, lambda i: (0, 0)),
            pl.BlockSpec((segs, EDGE, samples), lambda i: (0, 0, 0)),
            pl.BlockSpec((segs, EDGE, samples), lambda i: (0, channels // EDGE - 1, 0)),
        ],
        out_specs=[pl.BlockSpec(out.shape, lambda i: (0, 0))] * 2,
        out_shape=[out, out],
        compiler_params=pltpu.CompilerParams(vmem_limit_bytes=VMEM),
        name="edge_spectra",
    )(basis, raw, raw)


def main_kernel(segs, count, basis, raw, taps, filtered, high, low):
    step = pl.program_id(0)

    @pl.when(step == 0)
    def _():
        band = filter_band(taps, count, 0, high.shape)
        high[...] = band.astype(BF16)
        low[...] = (band - high[...].astype(F32)).astype(BF16)

    pair, channels, samples = raw.shape
    spectra = dot(basis[...], raw[...].reshape(pair * channels, samples), NT)
    for at in range(pair):
        part = spectra[:, at * channels : (at + 1) * channels]
        top = part.astype(BF16)
        rest = (part - top.astype(F32)).astype(BF16)
        sums = dot(top, high[...]) + dot(rest, high[...]) + dot(top, low[...])
        filtered[pl.ds(step * pair + at, 2 * NF, stride=segs), :] = sums


def main_spectra(basis, raw, taps):
    segs, channels, samples = raw.shape
    pair = 2
    return pl.pallas_call(
        functools.partial(main_kernel, segs, taps.shape[0]),
        grid=(segs // pair,),
        in_specs=[
            pl.BlockSpec(basis.shape, lambda i: (0, 0)),
            pl.BlockSpec((pair, channels, samples), lambda i: (i, 0, 0)),
            pl.BlockSpec(memory_space=pltpu.SMEM),
        ],
        out_specs=pl.BlockSpec((2 * NF * segs, channels), lambda i: (0, 0)),
        out_shape=jax.ShapeDtypeStruct((2 * NF * segs, channels), F32),
        scratch_shapes=[pltpu.VMEM((channels, channels), BF16)] * 2,
        compiler_params=pltpu.CompilerParams(vmem_limit_bytes=VMEM),
        name="main_spectra",
    )(basis, raw, taps)


def whiten_kernel(parts, count, me, taps, filtered, left, right, mask, *refs):
    outs, (total, powers) = refs[:parts], refs[parts:]
    segs, channels = mask.shape
    rows = segs * EDGE
    share = NF // parts
    owner = lax.broadcasted_iota(jnp.int32, (rows, channels), 0) // EDGE
    band_left = filter_band(taps, count, -EDGE, (EDGE, channels))
    band_right = filter_band(taps, count, channels, (EDGE, channels))
    wide_left = jnp.concatenate([band_left] * segs, axis=0)
    wide_right = jnp.concatenate([band_right] * segs, axis=0)
    for seg in range(segs):
        here = owner == seg
        sums = dot(left[...], jnp.where(here, wide_left, 0.0).astype(BF16))
        sums += dot(right[...], jnp.where(here, wide_right, 0.0).astype(BF16))
        at = pl.ds(seg, 2 * NF, stride=segs)
        total[at, :] = sums
    powers[0:SMOOTH] = jnp.zeros((SMOOTH, segs, channels), F32)
    powers[SMOOTH + NF :] = jnp.zeros((SMOOTH, segs, channels), F32)
    block = 12

    def square(step, water):
        first = pl.multiple_of(step * (block * segs), segs)
        second = pl.multiple_of(first + NF * segs, segs)
        real = total[pl.ds(first, block * segs), :] + filtered[pl.ds(first, block * segs), :]
        imag = total[pl.ds(second, block * segs), :] + filtered[pl.ds(second, block * segs), :]
        total[pl.ds(first, block * segs), :] = real
        total[pl.ds(second, block * segs), :] = imag
        power = (real * real + imag * imag).reshape(block, segs, channels)
        powers[pl.ds(step * block + SMOOTH, block)] = power
        return water + power.sum(0)

    water = lax.fori_loop(0, NF // block, square, jnp.zeros((segs, channels), F32))
    floor = water * (water_share / NF) + epsilon
    good = mask[...].astype(F32)
    for k in range(parts):
        start = (me[0] ^ k) * share
        out = outs[k]

        def spread(step, carry, start=start, out=out):
            bin_at = start + step * block
            cells = powers[pl.ds(bin_at, block + 2 * SMOOTH)]
            two = cells[:-1] + cells[1:]
            four = two[:-2] + two[2:]
            eight = four[:-4] + four[4:]
            nine = eight[:block] + cells[2 * SMOOTH :]
            scaled = good * lax.rsqrt(nine * (1.0 / (2 * SMOOTH + 1)) + floor)
            first = pl.multiple_of(bin_at * segs, segs)
            second = pl.multiple_of(first + NF * segs, segs)
            real = total[pl.ds(first, block * segs), :].reshape(block, segs, channels) * scaled
            imag = total[pl.ds(second, block * segs), :].reshape(block, segs, channels) * scaled
            both = jnp.concatenate([real[:, None], imag[:, None]], axis=1).astype(BF16)
            at = pl.multiple_of(step * (block * 2 * segs), segs)
            out[pl.ds(at, block * 2 * segs), :] = both.reshape(block * 2 * segs, channels)
            return carry

        lax.fori_loop(0, share // block, spread, 0)
        out[share * 2 * segs :, :] = good.astype(BF16)


def whitened_parts(parts, me, taps, filtered, left, right, mask):
    segs, channels = mask.shape
    rows = NF // parts * 2 * segs + segs
    whole = pl.BlockSpec(memory_space=pltpu.VMEM)
    return pl.pallas_call(
        functools.partial(whiten_kernel, parts, taps.shape[0]),
        in_specs=[pl.BlockSpec(memory_space=pltpu.SMEM)] * 2 + [whole] * 4,
        out_specs=[whole] * parts,
        out_shape=[jax.ShapeDtypeStruct((rows, channels), BF16)] * parts,
        scratch_shapes=[
            pltpu.VMEM((2 * NF * segs, channels), F32),
            pltpu.VMEM((NF + 2 * SMOOTH, segs, channels), F32),
        ],
        compiler_params=pltpu.CompilerParams(vmem_limit_bytes=VMEM),
        name="whiten",
    )(me, taps, filtered, left, right, mask)


def gram_kernel(parts, segs, bins, *refs):
    own, later, own_mask, later_mask = (refs[i * parts : (i + 1) * parts] for i in range(4))
    out, scale = refs[4 * parts :]
    channels = own[0].shape[1]
    row = lax.broadcasted_iota(jnp.int32, (channels, channels), 0)
    column = lax.broadcasted_iota(jnp.int32, (channels, channels), 1)
    ahead = column > row
    skew = (row + column + 1) % channels

    @pl.when(pl.program_id(0) == 0)
    def _():
        mine = jnp.concatenate([ref[...] for ref in own_mask], axis=0)
        theirs = jnp.concatenate([ref[...] for ref in later_mask], axis=0)
        count = jnp.where(ahead, dot(mine, mine, TN), dot(mine, theirs, TN))
        scale[...] = 1.0 / jnp.maximum(count, 1.0)

    for at in range(bins):
        here = [ref[at * 2 * segs : (at + 1) * 2 * segs, :] for ref in own]
        mine = jnp.concatenate(here, axis=0)
        turned = jnp.concatenate(
            [piece for cells in here for piece in (-cells[segs:], cells[:segs])], axis=0
        )
        theirs = jnp.concatenate(
            [ref[at * 2 * segs : (at + 1) * 2 * segs, :] for ref in later], axis=0
        )
        gram = dot(
            jnp.concatenate([mine, turned], axis=1), jnp.concatenate([mine, theirs], axis=1), TN
        )
        for part in range(2):
            rows = gram[part * channels : (part + 1) * channels]
            band = jnp.where(ahead, rows[:, :channels], rows[:, channels:]) * scale[...]
            band = jnp.take_along_axis(band, skew, axis=1, mode="promise_in_bounds")
            out[at, pl.ds(part, channels, stride=2), :] = band


def stacked(parts, segs, own, later):
    channels = own[0].shape[1]
    share = NF // parts
    bins = 4
    cells = pl.BlockSpec((bins * 2 * segs, channels), lambda i: (i, 0))
    flags = pl.BlockSpec((segs, channels), lambda i: (share * 2, 0))
    return pl.pallas_call(
        functools.partial(gram_kernel, parts, segs, bins),
        grid=(share // bins,),
        in_specs=[cells] * (2 * parts) + [flags] * (2 * parts),
        out_specs=pl.BlockSpec((bins, 2 * channels, LAGS), lambda i: (i, 0, 0)),
        out_shape=jax.ShapeDtypeStruct((share, 2 * channels, LAGS), F32),
        scratch_shapes=[pltpu.VMEM((channels, channels), F32)],
        compiler_params=pltpu.CompilerParams(vmem_limit_bytes=VMEM),
        name="gram",
    )(*own, *later, *own, *later)


def on_device(fibers, parts, raw_strain, fir_taps, good_mask):
    segs, channels, samples = raw_strain.shape
    basis = basis_rows(samples)
    me = lax.axis_index("seg").astype(jnp.int32)
    head, tail = edge_spectra(basis, raw_strain)
    left = lax.ppermute(tail, "fiber", [(i, i + 1) for i in range(fibers - 1)])
    right = lax.ppermute(head, "fiber", [(i + 1, i) for i in range(fibers - 1)])
    filtered = main_spectra(basis, raw_strain, fir_taps)
    mine = whitened_parts(parts, me[None], fir_taps, filtered, left, right, good_mask)
    own = [mine[0]]
    for k in range(1, parts):
        own.append(lax.ppermute(mine[k], "seg", [(i, i ^ k) for i in range(parts)]))
    later = [
        lax.ppermute(cells, "fiber", [(i + 1, i) for i in range(fibers - 1)]) for cells in own
    ]
    out = stacked(parts, segs, own, later)
    return out.reshape(out.shape[0], channels, 2, LAGS)


def solution(mesh):
    return jax.shard_map(
        functools.partial(on_device, mesh.shape["fiber"], mesh.shape["seg"]),
        mesh=mesh,
        in_specs=(P("seg", "fiber", None), P(), P("seg", "fiber")),
        out_specs=P("seg", "fiber", None, None),
        check_vma=False,
    )
```

profile of v0, /device:TPU:126, one launch (start us, length us, event | category | flops | bytes accessed | tf_op | source)
XLA Modules:
  0.0 96.6 jit_solution(1475925864009211423)
XLA Ops:
  0.0 3.4 %edge_spectra.1 = (bf16[288,256]{1,0:T(8,128)(2,1)}, bf16[288,256]{1,0:T(8,128)(2,1)}) custom-call(bf16[288,2048]{1,0:T(8,128)(2,1)} %constant.6.clone.basis, bf16[16,128,2048]{2,1,0:T(8,128)(2,1)} %last.1, bf16[16,128,2048]{2,1,0:T(8,128)(2,1)} %last.1), custom_call_target="tpu_custom_call" | custom-call | tf_op jit(solution)/shard_map/edge_spectra/pallas_call | solution.py:63
  3.4 5.1 %collective-permute-start = (bf16[288,256]{1,0:T(8,128)(2,1)}, bf16[288,256]{1,0:T(8,128)(2,1)S(1)}, u32[]{:S(2)}, u32[]{:S(2)}) collective-permute-start(bf16[288,256]{1,0:T(8,128)(2,1)} %get-tuple-element.11), channel_id=1, source_target_pairs={{0,4},{4,8},{8,12},{12,16},{16,20},{20,24},{24,28},{28,32},{32,36}... | collective-permute-start | bytes 442376 | tf_op jit(solution)/shard_map/ppermute | solution.py:251
  8.5 1.9 %collective-permute-start.1 = (bf16[288,256]{1,0:T(8,128)(2,1)}, bf16[288,256]{1,0:T(8,128)(2,1)S(1)}, u32[]{:S(2)}, u32[]{:S(2)}) collective-permute-start(bf16[288,256]{1,0:T(8,128)(2,1)} %get-tuple-element.12), channel_id=1, source_target_pairs={{4,0},{8,4},{12,8},{16,12},{20,16},{24,20},{28,24},{32,28},{36,32}... | collective-permute-start | bytes 442376 | tf_op jit(solution)/shard_map/ppermute | solution.py:252
  10.5 11.9 %main_spectra.1.filtered = f32[4608,128]{1,0:T(8,128)} custom-call(bf16[288,2048]{1,0:T(8,128)(2,1)} %constant.6.clone.basis, bf16[16,128,2048]{2,1,0:T(8,128)(2,1)} %last.1, f32[31]{0:T(128)} %taps.3), custom_call_target="tpu_custom_call" | custom-call | tf_op jit(solution)/shard_map/main_spectra/pallas_call | solution.py:100
  22.4 0.0 collective-permute-done.left
  22.4 0.0 copy-start.7
  22.4 0.0 collective-permute-done.1.right
  22.4 0.0 copy-start.8
  22.4 0.6 copy-done.7
  23.0 0.1 copy-done.8
  23.1 5.2 %whiten.1 = (bf16[1168,128]{1,0:T(8,128)(2,1)}, bf16[1168,128]{1,0:T(8,128)(2,1)}, bf16[1168,128]{1,0:T(8,128)(2,1)}, bf16[1168,128]{1,0:T(8,128)(2,1)}) custom-call(s32[1]{0:T(128)} %bitcast.me, f32[31]{0:T(128)} %taps.3, f32[4608,128]{1,0:T(8,128)} %main_spectra.1.filtered, bf16[288,256]{1,0:T(8,128)(2,1)} %copy-done.7, bf16[288,256]{1,0:T(8,128)(2,1)} %copy-done.8, ...), custom_call_target="tpu_custom_call" | custom-call | tf_op jit(solution)/shard_map/whiten/pallas_call | solution.py:179
  28.3 0.0 collective-permute-start.2
  28.3 0.9 collective-permute-start.3
  29.2 2.4 %collective-permute-start.4 = (bf16[1168,128]{1,0:T(8,128)(2,1)}, bf16[1168,128]{1,0:T(8,128)(2,1)S(1)}, u32[]{:S(2)}, u32[]{:S(2)}) collective-permute-start(bf16[1168,128]{1,0:T(8,128)(2,1)} %get-tuple-element.16), channel_id=1, source_target_pairs={{0,3},{1,2},{2,1},{3,0},{4,7},{5,6},{6,5},{7,4},{8,11},{9,10},{10,... | collective-permute-start | bytes 897032 | tf_op jit(solution)/shard_map/ppermute | solution.py:257
  31.6 1.9 %collective-permute-start.5 = (bf16[1168,128]{1,0:T(8,128)(2,1)}, bf16[1168,128]{1,0:T(8,128)(2,1)S(1)}, u32[]{:S(2)}, u32[]{:S(2)}) collective-permute-start(bf16[1168,128]{1,0:T(8,128)(2,1)} %get-tuple-element.13.refs_0_.refs_8_), channel_id=1, source_target_pairs={{4,0},{8,4},{12,8},{16,12},{20,16},{24,20},{28,24},{32,28},{36,32}... | collective-permute-start | bytes 897032 | tf_op jit(solution)/shard_map/ppermute | solution.py:259
  33.6 0.0 collective-permute-done.2.refs_1_.refs_9_
  33.6 0.0 copy-start
  33.6 2.0 %collective-permute-start.6 = (bf16[1168,128]{1,0:T(8,128)(2,1)S(1)}, bf16[1168,128]{1,0:T(8,128)(2,1)S(1)}, u32[]{:S(2)}, u32[]{:S(2)}) collective-permute-start(bf16[1168,128]{1,0:T(8,128)(2,1)S(1)} %collective-permute-done.2.refs_1_.refs_9_), channel_id=1, source_target_pairs={{4,0},{8,4},{12,8},{16,12},{20,16},{24,20},{28,24},{32,28},{36,32}... | collective-permute-start | bytes 897032 | tf_op jit(solution)/shard_map/ppermute | solution.py:259
  35.6 23.5 %collective-permute-done.3.refs_2_.refs_10_ = bf16[1168,128]{1,0:T(8,128)(2,1)S(1)} collective-permute-done((bf16[1168,128]{1,0:T(8,128)(2,1)}, bf16[1168,128]{1,0:T(8,128)(2,1)S(1)}, u32[]{:S(2)}, u32[]{:S(2)}) %collective-permute-start.3) | collective-permute-done | bytes 299040 | tf_op jit(solution)/shard_map/ppermute | solution.py:257
  59.1 0.0 copy-start.1
  59.1 1.9 %collective-permute-start.7 = (bf16[1168,128]{1,0:T(8,128)(2,1)S(1)}, bf16[1168,128]{1,0:T(8,128)(2,1)S(1)}, u32[]{:S(2)}, u32[]{:S(2)}) collective-permute-start(bf16[1168,128]{1,0:T(8,128)(2,1)S(1)} %collective-permute-done.3.refs_2_.refs_10_), channel_id=1, source_target_pairs={{4,0},{8,4},{12,8},{16,12},{20,16},{24,20},{28,24},{32,28},{36,32}... | collective-permute-start | bytes 897032 | tf_op jit(solution)/shard_map/ppermute | solution.py:259
  61.0 10.1 %collective-permute-done.4.refs_3_.refs_11_ = bf16[1168,128]{1,0:T(8,128)(2,1)S(1)} collective-permute-done((bf16[1168,128]{1,0:T(8,128)(2,1)}, bf16[1168,128]{1,0:T(8,128)(2,1)S(1)}, u32[]{:S(2)}, u32[]{:S(2)}) %collective-permute-start.4) | collective-permute-done | bytes 299040 | tf_op jit(solution)/shard_map/ppermute | solution.py:257
  71.2 0.0 copy-start.2
  71.2 1.9 %collective-permute-start.8 = (bf16[1168,128]{1,0:T(8,128)(2,1)S(1)}, bf16[1168,128]{1,0:T(8,128)(2,1)S(1)}, u32[]{:S(2)}, u32[]{:S(2)}) collective-permute-start(bf16[1168,128]{1,0:T(8,128)(2,1)S(1)} %collective-permute-done.4.refs_3_.refs_11_), channel_id=1, source_target_pairs={{4,0},{8,4},{12,8},{16,12},{20,16},{24,20},{28,24},{32,28},{36,32}... | collective-permute-start | bytes 897032 | tf_op jit(solution)/shard_map/ppermute | solution.py:259
  73.1 0.0 collective-permute-done.5.refs_4_.refs_12_
  73.1 0.0 copy-start.3
  73.1 0.0 collective-permute-done.6.refs_5_.refs_13_
  73.1 0.0 copy-start.4
  73.1 0.4 collective-permute-done.7.refs_6_.refs_14_
  73.6 0.0 copy-start.5
  73.6 13.2 %collective-permute-done.8.refs_7_.refs_15_ = bf16[1168,128]{1,0:T(8,128)(2,1)S(1)} collective-permute-done((bf16[1168,128]{1,0:T(8,128)(2,1)S(1)}, bf16[1168,128]{1,0:T(8,128)(2,1)S(1)}, u32[]{:S(2)}, u32[]{:S(2)}) %collective-permute-start.8) | collective-permute-done | bytes 299040 | tf_op jit(solution)/shard_map/ppermute | solution.py:259
  86.8 0.0 copy-done
  86.8 0.0 copy-done.1
  86.8 0.0 copy-done.2
  86.8 0.0 copy-done.3
  86.8 0.0 copy-done.4
  86.8 0.0 copy-done.5
  86.8 0.0 copy-start.6
  86.8 0.7 copy-done.6
  87.5 9.1 %gram.1 = f32[36,256,128]{2,1,0:T(8,128)} custom-call(bf16[1168,128]{1,0:T(8,128)(2,1)} %get-tuple-element.13.refs_0_.refs_8_, bf16[1168,128]{1,0:T(8,128)(2,1)} %copy-done, bf16[1168,128]{1,0:T(8,128)(2,1)} %copy-done.1, bf16[1168,128]{1,0:T(8,128)(2,1)} %copy-done.2, bf16[1168,128]{1,0:T(8,128)(2,1)} %copy-done.3, bf16[1168,128]{1,0:T(8,128)(2,1)} %copy-done.4, ...), custom_call_target="tpu_custom_call" | custom-call | tf_op jit(solution)/shard_map/gram/pallas_call | solution.py:234
Async XLA Ops:
  3.4 19.0 %collective-permute-start = (bf16[288,256]{1,0:T(8,128)(2,1)}, bf16[288,256]{1,0:T(8,128)(2,1)S(1)}, u32[]{:S(2)}, u32[]{:S(2)}) collective-permute-start(bf16[288,256]{1,0:T(8,128)(2,1)} %get-tuple-element.11), channel_id=1, source_target_pairs={{0,4},{4,8},{8,12},{12,16},{16,20},{20,24},{24,28},{28,32},{32,36}... | collective-permute-start | bytes 442376 | tf_op jit(solution)/shard_map/ppermute | solution.py:251
  8.5 13.9 %collective-permute-start.1 = (bf16[288,256]{1,0:T(8,128)(2,1)}, bf16[288,256]{1,0:T(8,128)(2,1)S(1)}, u32[]{:S(2)}, u32[]{:S(2)}) collective-permute-start(bf16[288,256]{1,0:T(8,128)(2,1)} %get-tuple-element.12), channel_id=1, source_target_pairs={{4,0},{8,4},{12,8},{16,12},{20,16},{24,20},{28,24},{32,28},{36,32}... | collective-permute-start | bytes 442376 | tf_op jit(solution)/shard_map/ppermute | solution.py:252
  22.4 0.7 copy-start.7
  22.4 0.7 copy-start.8
  28.3 5.3 %collective-permute-start.2 = (bf16[1168,128]{1,0:T(8,128)(2,1)}, bf16[1168,128]{1,0:T(8,128)(2,1)S(1)}, u32[]{:S(2)}, u32[]{:S(2)}) collective-permute-start(bf16[1168,128]{1,0:T(8,128)(2,1)} %get-tuple-element.14), channel_id=1, source_target_pairs={{0,1},{1,0},{2,3},{3,2},{4,5},{5,4},{6,7},{7,6},{8,9},{9,8},{10,11... | collective-permute-start | bytes 897032 | tf_op jit(solution)/shard_map/ppermute | solution.py:257
  28.3 30.8 %collective-permute-start.3 = (bf16[1168,128]{1,0:T(8,128)(2,1)}, bf16[1168,128]{1,0:T(8,128)(2,1)S(1)}, u32[]{:S(2)}, u32[]{:S(2)}) collective-permute-start(bf16[1168,128]{1,0:T(8,128)(2,1)} %get-tuple-element.15), channel_id=1, source_target_pairs={{0,2},{1,3},{2,0},{3,1},{4,6},{5,7},{6,4},{7,5},{8,10},{9,11},{10,... | collective-permute-start | bytes 897032 | tf_op jit(solution)/shard_map/ppermute | solution.py:257
  29.2 41.9 %collective-permute-start.4 = (bf16[1168,128]{1,0:T(8,128)(2,1)}, bf16[1168,128]{1,0:T(8,128)(2,1)S(1)}, u32[]{:S(2)}, u32[]{:S(2)}) collective-permute-start(bf16[1168,128]{1,0:T(8,128)(2,1)} %get-tuple-element.16), channel_id=1, source_target_pairs={{0,3},{1,2},{2,1},{3,0},{4,7},{5,6},{6,5},{7,4},{8,11},{9,10},{10,... | collective-permute-start | bytes 897032 | tf_op jit(solution)/shard_map/ppermute | solution.py:257
  31.6 41.4 %collective-permute-start.5 = (bf16[1168,128]{1,0:T(8,128)(2,1)}, bf16[1168,128]{1,0:T(8,128)(2,1)S(1)}, u32[]{:S(2)}, u32[]{:S(2)}) collective-permute-start(bf16[1168,128]{1,0:T(8,128)(2,1)} %get-tuple-element.13.refs_0_.refs_8_), channel_id=1, source_target_pairs={{4,0},{8,4},{12,8},{16,12},{20,16},{24,20},{28,24},{32,28},{36,32}... | collective-permute-start | bytes 897032 | tf_op jit(solution)/shard_map/ppermute | solution.py:259
  33.6 53.2 %copy-start = (bf16[1168,128]{1,0:T(8,128)(2,1)}, bf16[1168,128]{1,0:T(8,128)(2,1)S(1)}, u32[]{:S(2)}) copy-start(bf16[1168,128]{1,0:T(8,128)(2,1)S(1)} %collective-permute-done.2.refs_1_.refs_9_) | copy-start | bytes 897028
  33.6 39.5 %collective-permute-start.6 = (bf16[1168,128]{1,0:T(8,128)(2,1)S(1)}, bf16[1168,128]{1,0:T(8,128)(2,1)S(1)}, u32[]{:S(2)}, u32[]{:S(2)}) collective-permute-start(bf16[1168,128]{1,0:T(8,128)(2,1)S(1)} %collective-permute-done.2.refs_1_.refs_9_), channel_id=1, source_target_pairs={{4,0},{8,4},{12,8},{16,12},{20,16},{24,20},{28,24},{32,28},{36,32}... | collective-permute-start | bytes 897032 | tf_op jit(solution)/shard_map/ppermute | solution.py:259
  59.1 27.7 %copy-start.1 = (bf16[1168,128]{1,0:T(8,128)(2,1)}, bf16[1168,128]{1,0:T(8,128)(2,1)S(1)}, u32[]{:S(2)}) copy-start(bf16[1168,128]{1,0:T(8,128)(2,1)S(1)} %collective-permute-done.3.refs_2_.refs_10_) | copy-start | bytes 897028
  59.1 14.4 %collective-permute-start.7 = (bf16[1168,128]{1,0:T(8,128)(2,1)S(1)}, bf16[1168,128]{1,0:T(8,128)(2,1)S(1)}, u32[]{:S(2)}, u32[]{:S(2)}) collective-permute-start(bf16[1168,128]{1,0:T(8,128)(2,1)S(1)} %collective-permute-done.3.refs_2_.refs_10_), channel_id=1, source_target_pairs={{4,0},{8,4},{12,8},{16,12},{20,16},{24,20},{28,24},{32,28},{36,32}... | collective-permute-start | bytes 897032 | tf_op jit(solution)/shard_map/ppermute | solution.py:259
  71.2 15.6 %copy-start.2 = (bf16[1168,128]{1,0:T(8,128)(2,1)}, bf16[1168,128]{1,0:T(8,128)(2,1)S(1)}, u32[]{:S(2)}) copy-start(bf16[1168,128]{1,0:T(8,128)(2,1)S(1)} %collective-permute-done.4.refs_3_.refs_11_) | copy-start | bytes 897028
  71.2 15.6 %collective-permute-start.8 = (bf16[1168,128]{1,0:T(8,128)(2,1)S(1)}, bf16[1168,128]{1,0:T(8,128)(2,1)S(1)}, u32[]{:S(2)}, u32[]{:S(2)}) collective-permute-start(bf16[1168,128]{1,0:T(8,128)(2,1)S(1)} %collective-permute-done.4.refs_3_.refs_11_), channel_id=1, source_target_pairs={{4,0},{8,4},{12,8},{16,12},{20,16},{24,20},{28,24},{32,28},{36,32}... | collective-permute-start | bytes 897032 | tf_op jit(solution)/shard_map/ppermute | solution.py:259
  73.1 13.7 %copy-start.3 = (bf16[1168,128]{1,0:T(8,128)(2,1)}, bf16[1168,128]{1,0:T(8,128)(2,1)S(1)}, u32[]{:S(2)}) copy-start(bf16[1168,128]{1,0:T(8,128)(2,1)S(1)} %collective-permute-done.5.refs_4_.refs_12_) | copy-start | bytes 897028
  73.1 13.7 %copy-start.4 = (bf16[1168,128]{1,0:T(8,128)(2,1)}, bf16[1168,128]{1,0:T(8,128)(2,1)S(1)}, u32[]{:S(2)}) copy-start(bf16[1168,128]{1,0:T(8,128)(2,1)S(1)} %collective-permute-done.6.refs_5_.refs_13_) | copy-start | bytes 897028
  73.6 13.2 %copy-start.5 = (bf16[1168,128]{1,0:T(8,128)(2,1)}, bf16[1168,128]{1,0:T(8,128)(2,1)S(1)}, u32[]{:S(2)}) copy-start(bf16[1168,128]{1,0:T(8,128)(2,1)S(1)} %collective-permute-done.7.refs_6_.refs_14_) | copy-start | bytes 897028
  86.8 0.7 copy-start.6
where the time goes:
time: 97.8 us; the launch traced here: 96.6 us
  waiting for transfers between devices  47.3 us (48%)
  Pallas kernels  29.6 us (30%)
  starting transfers between devices  18.2 us (19%)
  local copies, waits for them, and re-layouts  1.43 us (1%)
    ppermute x3, waiting for transfers between devices, on_device(): own.append(lax.ppermute(mine[k], 'seg', [(i, i ^ k) for i in range(parts)]))  33.6 us
    ppermute x4, waiting for transfers between devices, on_device(): lax.ppermute(cells, 'fiber', [(i + 1, i) for i in range(fibers - 1)])  13.7 us
    pallas_call x1, Pallas kernels, main_spectra(): pl.pallas_call(functools.partial(main_kernel, segs, taps.shape[0]), grid=...  11.9 us
    pallas_call x1, Pallas kernels, stacked(): pl.pallas_call(functools.partial(gram_kernel, parts, segs, bins), grid=(s...  9.06 us
    ppermute x4, starting transfers between devices, on_device(): lax.ppermute(cells, 'fiber', [(i + 1, i) for i in range(fibers - 1)])  7.77 us
    pallas_call x1, Pallas kernels, whitened_parts(): pl.pallas_call(functools.partial(whiten_kernel, parts, taps.shape[0]), in...  5.18 us
    ppermute x1, starting transfers between devices, on_device(): left = lax.ppermute(tail, 'fiber', [(i, i + 1) for i in range(fibers - 1)])  5.12 us
    pallas_call x1, Pallas kernels, edge_spectra(): pl.pallas_call(edge_kernel, grid=(1,), in_specs=[pl.BlockSpec(basis.shape...  3.41 us
  transfers between devices with their start and end apart: 9, of which 4 were waited for; matrix products, arithmetic and copies ran while one was open for 0% of the time, Pallas kernels for 12%

commit v1 on v0

--- a/solution.py
+++ b/solution.py
@@ -75,22 +75,30 @@
     )(basis, raw, raw)
 
 
-def main_kernel(segs, count, basis, raw, taps, filtered, high, low):
+def main_kernel(segs, count, basis, raw, taps, filtered, both):
     step = pl.program_id(0)
+    pair, channels, samples = raw.shape
 
     @pl.when(step == 0)
     def _():
-        band = filter_band(taps, count, 0, high.shape)
-        high[...] = band.astype(BF16)
-        low[...] = (band - high[...].astype(F32)).astype(BF16)
-
-    pair, channels, samples = raw.shape
+        band = filter_band(taps, count, 0, (channels, channels))
+        high = band.astype(BF16)
+        low = (band - high.astype(F32)).astype(BF16)
+        both[...] = jnp.concatenate(
+            [
+                jnp.concatenate([high, low], axis=1),
+                jnp.concatenate([high, jnp.zeros_like(high)], axis=1),
+            ],
+            axis=0,
+        )
+
     spectra = dot(basis[...], raw[...].reshape(pair * channels, samples), NT)
     for at in range(pair):
         part = spectra[:, at * channels : (at + 1) * channels]
         top = part.astype(BF16)
         rest = (part - top.astype(F32)).astype(BF16)
-        sums = dot(top, high[...]) + dot(rest, high[...]) + dot(top, low[...])
+        sums = dot(jnp.concatenate([top, rest], axis=1), both[...])
+        sums = sums[:, :channels] + sums[:, channels:]
         filtered[pl.ds(step * pair + at, 2 * NF, stride=segs), :] = sums
 
 
@@ -107,7 +115,7 @@
         ],
         out_specs=pl.BlockSpec((2 * NF * segs, channels), lambda i: (0, 0)),
         out_shape=jax.ShapeDtypeStruct((2 * NF * segs, channels), F32),
-        scratch_shapes=[pltpu.VMEM((channels, channels), BF16)] * 2,
+        scratch_shapes=[pltpu.VMEM((2 * channels, 2 * channels), BF16)],
         compiler_params=pltpu.CompilerParams(vmem_limit_bytes=VMEM),
         name="main_spectra",
     )(basis, raw, taps)
@@ -255,9 +263,14 @@
     own = [mine[0]]
     for k in range(1, parts):
         own.append(lax.ppermute(mine[k], "seg", [(i, i ^ k) for i in range(parts)]))
-    later = [
-        lax.ppermute(cells, "fiber", [(i + 1, i) for i in range(fibers - 1)]) for cells in own
-    ]
+    later = []
+    for k in range(parts):
+        pairs = [
+            ((i + 1) * parts + (j ^ k), i * parts + j)
+            for i in range(fibers - 1)
+            for j in range(parts)
+        ]
+        later.append(lax.ppermute(mine[k], GRID, pairs))
     out = stacked(parts, segs, own, later)
     return out.reshape(out.shape[0], channels, 2, LAGS)
 

time: 97.8 us -> 83.7 us (0.86)
  the two profiles are of different devices: /device:TPU:126 before, /device:TPU:103 now
where the time goes in v1:
time: 83.7 us; the launch traced here: 82.5 us
  Pallas kernels  28.9 us (35%)
  waiting for transfers between devices  27.5 us (33%)
  starting transfers between devices  24.6 us (29%)
  local copies, waits for them, and re-layouts  1.45 us (2%)
    ppermute x3, waiting for transfers between devices, on_device(): own.append(lax.ppermute(mine[k], 'seg', [(i, i ^ k) for i in range(parts)]))  20.2 us
    ppermute x4, starting transfers between devices, on_device(): later.append(lax.ppermute(mine[k], GRID, pairs))  19.1 us
    pallas_call x1, Pallas kernels, main_spectra(): pl.pallas_call(functools.partial(main_kernel, segs, taps.shape[0]), grid=...  11.2 us
    pallas_call x1, Pallas kernels, stacked(): pl.pallas_call(functools.partial(gram_kernel, parts, segs, bins), grid=(s...  9.06 us
    ppermute x4, waiting for transfers between devices, on_device(): later.append(lax.ppermute(mine[k], GRID, pairs))  7.24 us
    pallas_call x1, Pallas kernels, whitened_parts(): pl.pallas_call(functools.partial(whiten_kernel, parts, taps.shape[0]), in...  5.18 us
    pallas_call x1, Pallas kernels, edge_spectra(): pl.pallas_call(edge_kernel, grid=(1,), in_specs=[pl.BlockSpec(basis.shape...  3.41 us
    ppermute x1, starting transfers between devices, on_device(): left = lax.ppermute(tail, 'fiber', [(i, i + 1) for i in range(fibers - 1)])  3.11 us
  transfers between devices with their start and end apart: 9, of which 4 were waited for; matrix products, arithmetic and copies ran while one was open for 0% of the time, Pallas kernels for 14%

profile of v1, /device:TPU:103, one launch (start us, length us, event | category | flops | bytes accessed | tf_op | source)
XLA Modules:
  0.0 82.5 jit_solution(18274237665209509187)
XLA Ops:
  0.0 3.4 %edge_spectra.1 = (bf16[288,256]{1,0:T(8,128)(2,1)}, bf16[288,256]{1,0:T(8,128)(2,1)}) custom-call(bf16[288,2048]{1,0:T(8,128)(2,1)} %constant.6.clone.basis, bf16[16,128,2048]{2,1,0:T(8,128)(2,1)} %last.1, bf16[16,128,2048]{2,1,0:T(8,128)(2,1)} %last.1), custom_call_target="tpu_custom_call" | custom-call | tf_op jit(solution)/shard_map/edge_spectra/pallas_call | solution.py:63
  3.4 3.1 %collective-permute-start = (bf16[288,256]{1,0:T(8,128)(2,1)}, bf16[288,256]{1,0:T(8,128)(2,1)S(1)}, u32[]{:S(2)}, u32[]{:S(2)}) collective-permute-start(bf16[288,256]{1,0:T(8,128)(2,1)} %get-tuple-element.11), channel_id=1, source_target_pairs={{0,4},{4,8},{8,12},{12,16},{16,20},{20,24},{24,28},{28,32},{32,36}... | collective-permute-start | bytes 442376 | tf_op jit(solution)/shard_map/ppermute | solution.py:259
  6.5 2.2 %collective-permute-start.1 = (bf16[288,256]{1,0:T(8,128)(2,1)}, bf16[288,256]{1,0:T(8,128)(2,1)S(1)}, u32[]{:S(2)}, u32[]{:S(2)}) collective-permute-start(bf16[288,256]{1,0:T(8,128)(2,1)} %get-tuple-element.12), channel_id=1, source_target_pairs={{4,0},{8,4},{12,8},{16,12},{20,16},{24,20},{28,24},{32,28},{36,32}... | collective-permute-start | bytes 442376 | tf_op jit(solution)/shard_map/ppermute | solution.py:260
  8.7 11.2 %main_spectra.1.filtered = f32[4608,128]{1,0:T(8,128)} custom-call(bf16[288,2048]{1,0:T(8,128)(2,1)} %constant.6.clone.basis, bf16[16,128,2048]{2,1,0:T(8,128)(2,1)} %last.1, f32[31]{0:T(128)} %taps.3), custom_call_target="tpu_custom_call" | custom-call | tf_op jit(solution)/shard_map/main_spectra/pallas_call | solution.py:108
  19.9 0.0 collective-permute-done.left
  20.0 0.0 copy-start.7
  20.0 0.0 collective-permute-done.1.right
  20.0 0.0 copy-start.8
  20.0 0.6 copy-done.7
  20.6 0.1 copy-done.8
  20.7 5.2 %whiten.1 = (bf16[1168,128]{1,0:T(8,128)(2,1)}, bf16[1168,128]{1,0:T(8,128)(2,1)}, bf16[1168,128]{1,0:T(8,128)(2,1)}, bf16[1168,128]{1,0:T(8,128)(2,1)}) custom-call(s32[1]{0:T(128)} %bitcast.me, f32[31]{0:T(128)} %taps.3, f32[4608,128]{1,0:T(8,128)} %main_spectra.1.filtered, bf16[288,256]{1,0:T(8,128)(2,1)} %copy-done.7, bf16[288,256]{1,0:T(8,128)(2,1)} %copy-done.8, ...), custom_call_target="tpu_custom_call" | custom-call | tf_op jit(solution)/shard_map/whiten/pallas_call | solution.py:187
  25.9 2.4 %collective-permute-start.5 = (bf16[1168,128]{1,0:T(8,128)(2,1)}, bf16[1168,128]{1,0:T(8,128)(2,1)S(1)}, u32[]{:S(2)}, u32[]{:S(2)}) collective-permute-start(bf16[1168,128]{1,0:T(8,128)(2,1)} %get-tuple-element.13.refs_0_.refs_8_), channel_id=1, source_target_pairs={{4,0},{5,1},{6,2},{7,3},{8,4},{9,5},{10,6},{11,7},{12,8},{13,9},{1... | collective-permute-start | bytes 897032 | tf_op jit(solution)/shard_map/ppermute | solution.py:273
  28.3 3.6 %collective-permute-start.6 = (bf16[1168,128]{1,0:T(8,128)(2,1)}, bf16[1168,128]{1,0:T(8,128)(2,1)S(1)}, u32[]{:S(2)}, u32[]{:S(2)}) collective-permute-start(bf16[1168,128]{1,0:T(8,128)(2,1)} %get-tuple-element.14), channel_id=1, source_target_pairs={{5,0},{4,1},{7,2},{6,3},{9,4},{8,5},{11,6},{10,7},{13,8},{12,9},{1... | collective-permute-start | bytes 897032 | tf_op jit(solution)/shard_map/ppermute | solution.py:273
  31.9 0.1 collective-permute-start.2
  32.0 7.8 %collective-permute-start.7 = (bf16[1168,128]{1,0:T(8,128)(2,1)}, bf16[1168,128]{1,0:T(8,128)(2,1)S(1)}, u32[]{:S(2)}, u32[]{:S(2)}) collective-permute-start(bf16[1168,128]{1,0:T(8,128)(2,1)} %get-tuple-element.15), channel_id=1, source_target_pairs={{6,0},{7,1},{4,2},{5,3},{10,4},{11,5},{8,6},{9,7},{14,8},{15,9},{1... | collective-permute-start | bytes 897032 | tf_op jit(solution)/shard_map/ppermute | solution.py:273
  39.8 0.1 collective-permute-start.3
  39.9 0.0 collective-permute-done.5.refs_4_.refs_12_
  39.9 0.0 copy-start
  39.9 5.2 %collective-permute-start.8 = (bf16[1168,128]{1,0:T(8,128)(2,1)}, bf16[1168,128]{1,0:T(8,128)(2,1)S(1)}, u32[]{:S(2)}, u32[]{:S(2)}) collective-permute-start(bf16[1168,128]{1,0:T(8,128)(2,1)} %get-tuple-element.16), channel_id=1, source_target_pairs={{7,0},{6,1},{5,2},{4,3},{11,4},{10,5},{9,6},{8,7},{15,8},{14,9},{1... | collective-permute-start | bytes 897032 | tf_op jit(solution)/shard_map/ppermute | solution.py:273
  45.2 1.9 %collective-permute-done.6.refs_5_.refs_13_ = bf16[1168,128]{1,0:T(8,128)(2,1)S(1)} collective-permute-done((bf16[1168,128]{1,0:T(8,128)(2,1)}, bf16[1168,128]{1,0:T(8,128)(2,1)S(1)}, u32[]{:S(2)}, u32[]{:S(2)}) %collective-permute-start.6) | collective-permute-done | bytes 299040 | tf_op jit(solution)/shard_map/ppermute | solution.py:273
  47.1 0.0 copy-start.1
  47.1 0.1 collective-permute-start.4
  47.1 0.0 collective-permute-done.2.refs_1_.refs_9_
  47.1 0.0 copy-start.2
  47.1 5.4 %collective-permute-done.7.refs_6_.refs_14_ = bf16[1168,128]{1,0:T(8,128)(2,1)S(1)} collective-permute-done((bf16[1168,128]{1,0:T(8,128)(2,1)}, bf16[1168,128]{1,0:T(8,128)(2,1)S(1)}, u32[]{:S(2)}, u32[]{:S(2)}) %collective-permute-start.7) | collective-permute-done | bytes 299040 | tf_op jit(solution)/shard_map/ppermute | solution.py:273
  52.5 0.0 copy-start.3
  52.5 13.6 %collective-permute-done.3.refs_2_.refs_10_ = bf16[1168,128]{1,0:T(8,128)(2,1)S(1)} collective-permute-done((bf16[1168,128]{1,0:T(8,128)(2,1)}, bf16[1168,128]{1,0:T(8,128)(2,1)S(1)}, u32[]{:S(2)}, u32[]{:S(2)}) %collective-permute-start.3) | collective-permute-done | bytes 299040 | tf_op jit(solution)/shard_map/ppermute | solution.py:265
  66.1 0.0 copy-start.4
  66.1 0.0 collective-permute-done.8.refs_7_.refs_15_
  66.1 0.0 copy-start.5
  66.1 6.6 %collective-permute-done.4.refs_3_.refs_11_ = bf16[1168,128]{1,0:T(8,128)(2,1)S(1)} collective-permute-done((bf16[1168,128]{1,0:T(8,128)(2,1)}, bf16[1168,128]{1,0:T(8,128)(2,1)S(1)}, u32[]{:S(2)}, u32[]{:S(2)}) %collective-permute-start.4) | collective-permute-done | bytes 299040 | tf_op jit(solution)/shard_map/ppermute | solution.py:265
  72.7 0.0 copy-done
  72.7 0.0 copy-done.1
  72.7 0.0 copy-done.2
  72.7 0.0 copy-done.3
  72.7 0.0 copy-done.4
  72.7 0.0 copy-done.5
  72.7 0.0 copy-start.6
  72.8 0.7 copy-done.6
  73.5 9.1 %gram.1 = f32[36,256,128]{2,1,0:T(8,128)} custom-call(bf16[1168,128]{1,0:T(8,128)(2,1)} %get-tuple-element.13.refs_0_.refs_8_, bf16[1168,128]{1,0:T(8,128)(2,1)} %copy-done.2, bf16[1168,128]{1,0:T(8,128)(2,1)} %copy-done.4, bf16[1168,128]{1,0:T(8,128)(2,1)} %copy-done.6, bf16[1168,128]{1,0:T(8,128)(2,1)} %copy-done, bf16[1168,128]{1,0:T(8,128)(2,1)} %copy-done.1, ...), custom_call_target="tpu_custom_call" | custom-call | tf_op jit(solution)/shard_map/gram/pallas_call | solution.py:242
Async XLA Ops:
  3.4 16.5 %collective-permute-start = (bf16[288,256]{1,0:T(8,128)(2,1)}, bf16[288,256]{1,0:T(8,128)(2,1)S(1)}, u32[]{:S(2)}, u32[]{:S(2)}) collective-permute-start(bf16[288,256]{1,0:T(8,128)(2,1)} %get-tuple-element.11), channel_id=1, source_target_pairs={{0,4},{4,8},{8,12},{12,16},{16,20},{20,24},{24,28},{28,32},{32,36}... | collective-permute-start | bytes 442376 | tf_op jit(solution)/shard_map/ppermute | solution.py:259
  6.5 13.4 %collective-permute-start.1 = (bf16[288,256]{1,0:T(8,128)(2,1)}, bf16[288,256]{1,0:T(8,128)(2,1)S(1)}, u32[]{:S(2)}, u32[]{:S(2)}) collective-permute-start(bf16[288,256]{1,0:T(8,128)(2,1)} %get-tuple-element.12), channel_id=1, source_target_pairs={{4,0},{8,4},{12,8},{16,12},{20,16},{24,20},{28,24},{32,28},{36,32}... | collective-permute-start | bytes 442376 | tf_op jit(solution)/shard_map/ppermute | solution.py:260
  20.0 0.6 copy-start.7
  20.0 0.7 copy-start.8
  25.9 14.1 %collective-permute-start.5 = (bf16[1168,128]{1,0:T(8,128)(2,1)}, bf16[1168,128]{1,0:T(8,128)(2,1)S(1)}, u32[]{:S(2)}, u32[]{:S(2)}) collective-permute-start(bf16[1168,128]{1,0:T(8,128)(2,1)} %get-tuple-element.13.refs_0_.refs_8_), channel_id=1, source_target_pairs={{4,0},{5,1},{6,2},{7,3},{8,4},{9,5},{10,6},{11,7},{12,8},{13,9},{1... | collective-permute-start | bytes 897032 | tf_op jit(solution)/shard_map/ppermute | solution.py:273
  28.3 18.8 %collective-permute-start.6 = (bf16[1168,128]{1,0:T(8,128)(2,1)}, bf16[1168,128]{1,0:T(8,128)(2,1)S(1)}, u32[]{:S(2)}, u32[]{:S(2)}) collective-permute-start(bf16[1168,128]{1,0:T(8,128)(2,1)} %get-tuple-element.14), channel_id=1, source_target_pairs={{5,0},{4,1},{7,2},{6,3},{9,4},{8,5},{11,6},{10,7},{13,8},{12,9},{1... | collective-permute-start | bytes 897032 | tf_op jit(solution)/shard_map/ppermute | solution.py:273
  31.9 15.2 %collective-permute-start.2 = (bf16[1168,128]{1,0:T(8,128)(2,1)}, bf16[1168,128]{1,0:T(8,128)(2,1)S(1)}, u32[]{:S(2)}, u32[]{:S(2)}) collective-permute-start(bf16[1168,128]{1,0:T(8,128)(2,1)} %get-tuple-element.14), channel_id=1, source_target_pairs={{0,1},{1,0},{2,3},{3,2},{4,5},{5,4},{6,7},{7,6},{8,9},{9,8},{10,11... | collective-permute-start | bytes 897032 | tf_op jit(solution)/shard_map/ppermute | solution.py:265
  32.0 20.5 %collective-permute-start.7 = (bf16[1168,128]{1,0:T(8,128)(2,1)}, bf16[1168,128]{1,0:T(8,128)(2,1)S(1)}, u32[]{:S(2)}, u32[]{:S(2)}) collective-permute-start(bf16[1168,128]{1,0:T(8,128)(2,1)} %get-tuple-element.15), channel_id=1, source_target_pairs={{6,0},{7,1},{4,2},{5,3},{10,4},{11,5},{8,6},{9,7},{14,8},{15,9},{1... | collective-permute-start | bytes 897032 | tf_op jit(solution)/shard_map/ppermute | solution.py:273
  39.8 26.2 %collective-permute-start.3 = (bf16[1168,128]{1,0:T(8,128)(2,1)}, bf16[1168,128]{1,0:T(8,128)(2,1)S(1)}, u32[]{:S(2)}, u32[]{:S(2)}) collective-permute-start(bf16[1168,128]{1,0:T(8,128)(2,1)} %get-tuple-element.15), channel_id=1, source_target_pairs={{0,2},{1,3},{2,0},{3,1},{4,6},{5,7},{6,4},{7,5},{8,10},{9,11},{10,... | collective-permute-start | bytes 897032 | tf_op jit(solution)/shard_map/ppermute | solution.py:265
  39.9 32.8 %copy-start = (bf16[1168,128]{1,0:T(8,128)(2,1)}, bf16[1168,128]{1,0:T(8,128)(2,1)S(1)}, u32[]{:S(2)}) copy-start(bf16[1168,128]{1,0:T(8,128)(2,1)S(1)} %collective-permute-done.5.refs_4_.refs_12_) | copy-start | bytes 897028
  39.9 26.1 %collective-permute-start.8 = (bf16[1168,128]{1,0:T(8,128)(2,1)}, bf16[1168,128]{1,0:T(8,128)(2,1)S(1)}, u32[]{:S(2)}, u32[]{:S(2)}) collective-permute-start(bf16[1168,128]{1,0:T(8,128)(2,1)} %get-tuple-element.16), channel_id=1, source_target_pairs={{7,0},{6,1},{5,2},{4,3},{11,4},{10,5},{9,6},{8,7},{15,8},{14,9},{1... | collective-permute-start | bytes 897032 | tf_op jit(solution)/shard_map/ppermute | solution.py:273
  47.1 25.6 %copy-start.1 = (bf16[1168,128]{1,0:T(8,128)(2,1)}, bf16[1168,128]{1,0:T(8,128)(2,1)S(1)}, u32[]{:S(2)}) copy-start(bf16[1168,128]{1,0:T(8,128)(2,1)S(1)} %collective-permute-done.6.refs_5_.refs_13_) | copy-start | bytes 897028
  47.1 25.6 %collective-permute-start.4 = (bf16[1168,128]{1,0:T(8,128)(2,1)}, bf16[1168,128]{1,0:T(8,128)(2,1)S(1)}, u32[]{:S(2)}, u32[]{:S(2)}) collective-permute-start(bf16[1168,128]{1,0:T(8,128)(2,1)} %get-tuple-element.16), channel_id=1, source_target_pairs={{0,3},{1,2},{2,1},{3,0},{4,7},{5,6},{6,5},{7,4},{8,11},{9,10},{10,... | collective-permute-start | bytes 897032 | tf_op jit(solution)/shard_map/ppermute | solution.py:265
  47.1 25.6 %copy-start.2 = (bf16[1168,128]{1,0:T(8,128)(2,1)}, bf16[1168,128]{1,0:T(8,128)(2,1)S(1)}, u32[]{:S(2)}) copy-start(bf16[1168,128]{1,0:T(8,128)(2,1)S(1)} %collective-permute-done.2.refs_1_.refs_9_) | copy-start | bytes 897028
  52.5 20.2 %copy-start.3 = (bf16[1168,128]{1,0:T(8,128)(2,1)}, bf16[1168,128]{1,0:T(8,128)(2,1)S(1)}, u32[]{:S(2)}) copy-start(bf16[1168,128]{1,0:T(8,128)(2,1)S(1)} %collective-permute-done.7.refs_6_.refs_14_) | copy-start | bytes 897028
  66.1 6.7 %copy-start.4 = (bf16[1168,128]{1,0:T(8,128)(2,1)}, bf16[1168,128]{1,0:T(8,128)(2,1)S(1)}, u32[]{:S(2)}) copy-start(bf16[1168,128]{1,0:T(8,128)(2,1)S(1)} %collective-permute-done.3.refs_2_.refs_10_) | copy-start | bytes 897028
  66.1 6.7 %copy-start.5 = (bf16[1168,128]{1,0:T(8,128)(2,1)}, bf16[1168,128]{1,0:T(8,128)(2,1)S(1)}, u32[]{:S(2)}) copy-start(bf16[1168,128]{1,0:T(8,128)(2,1)S(1)} %collective-permute-done.8.refs_7_.refs_15_) | copy-start | bytes 897028
  72.7 0.7 copy-start.6

commit v2 on v0

v2 whole, which is shorter than its diff:
```python
import functools
import math

import jax
import jax.numpy as jnp
import numpy as np
from jax import lax
from jax.experimental import pallas as pl
from jax.experimental.pallas import tpu as pltpu
from jax.sharding import PartitionSpec as P

NF = 144
LOW = 16
SMOOTH = 4
LAGS = 128
EDGE = 16
HALF = 15

epsilon = 1e-06
water_share = 0.1

GRID = ("fiber", "seg")
VMEM = 24 * 1024 * 1024
STREAM = 50 * 1024 * 1024
F32 = jnp.float32
BF16 = jnp.bfloat16


def basis_rows(samples):
    times = np.arange(samples, dtype=np.int64)
    bins = np.arange(NF, dtype=np.int64) + LOW
    phase_index = bins[:, None] * times[None, :] % samples
    angles = phase_index.astype(np.float32) * np.float32(2.0 * math.pi / samples)
    rows = np.concatenate([np.cos(angles), -np.sin(angles)], axis=0)
    return jnp.asarray(rows, dtype=BF16)


def filter_band(taps, count, first, shape):
    offset = lax.broadcasted_iota(jnp.int32, shape, 0) - lax.broadcasted_iota(jnp.int32, shape, 1)
    band = jnp.zeros(shape, F32)
    for tap in range(count):
        band = jnp.where(offset == tap - first - HALF, taps[tap], band)
    return band


NT = (((1,), (1,)), ((), ()))
TN = (((0,), (0,)), ((), ()))


def dot(a, b, dims=(((1,), (0,)), ((), ()))):
    return lax.dot_general(a, b, dims, preferred_element_type=F32)


WHOLE = pl.BlockSpec(memory_space=pltpu.VMEM)
SCALARS = pl.BlockSpec(memory_space=pltpu.SMEM)
ANYWHERE = pl.BlockSpec(memory_space=pl.ANY)


def edge_kernel(raw, basis, head, tail, cells, sems):
    segs, channels, samples = raw.shape
    copies = [
        pltpu.make_async_copy(raw.at[:, pl.ds(first, EDGE), :], cells.at[at], sems.at[at])
        for at, first in enumerate((channels - EDGE, 0))
    ]
    for copy in copies:
        copy.start()
    for at, out in enumerate((tail, head)):
        copies[at].wait()
        out[...] = dot(basis[...], cells[at].reshape(segs * EDGE, samples), NT).astype(BF16)


def edge_spectra(basis, raw):
    segs, channels, samples = raw.shape
    out = jax.ShapeDtypeStruct((2 * NF, segs * EDGE), BF16)
    return pl.pallas_call(
        edge_kernel,
        in_specs=[ANYWHERE, WHOLE],
        out_specs=[WHOLE] * 2,
        out_shape=[out, out],
        scratch_shapes=[
            pltpu.VMEM((2, segs, EDGE, samples), BF16),
            pltpu.SemaphoreType.DMA((2,)),
        ],
        compiler_params=pltpu.CompilerParams(vmem_limit_bytes=STREAM),
        name="edge_spectra",
    )(raw, basis)


def main_kernel(pair, count, raw, basis, taps, filtered, cells, both, sems):
    segs, channels, samples = raw.shape
    copies = [
        pltpu.make_async_copy(
            raw.at[pl.ds(at * pair, pair)], cells.at[pl.ds(at * pair, pair)], sems.at[at]
        )
        for at in range(segs // pair)
    ]
    for copy in copies:
        copy.start()
    band = filter_band(taps, count, 0, (channels, channels))
    high = band.astype(BF16)
    low = (band - high.astype(F32)).astype(BF16)
    both[...] = jnp.concatenate(
        [
            jnp.concatenate([high, low], axis=1),
            jnp.concatenate([high, jnp.zeros_like(high)], axis=1),
        ],
        axis=0,
    )
    for step in range(segs // pair):
        copies[step].wait()
        block = cells[step * pair : (step + 1) * pair].reshape(pair * channels, samples)
        spectra = dot(basis[...], block, NT)
        for at in range(pair):
            part = spectra[:, at * channels : (at + 1) * channels]
            top = part.astype(BF16)
            rest = (part - top.astype(F32)).astype(BF16)
            sums = dot(jnp.concatenate([top, rest], axis=1), both[...])
            sums = sums[:, :channels] + sums[:, channels:]
            filtered[pl.ds(step * pair + at, 2 * NF, stride=segs), :] = sums


def main_spectra(basis, raw, taps):
    segs, channels, samples = raw.shape
    pair = 2
    return pl.pallas_call(
        functools.partial(main_kernel, pair, taps.shape[0]),
        in_specs=[ANYWHERE, WHOLE, SCALARS],
        out_specs=WHOLE,
        out_shape=jax.ShapeDtypeStruct((2 * NF * segs, channels), F32),
        scratch_shapes=[
            pltpu.VMEM((segs, channels, samples), BF16),
            pltpu.VMEM((2 * channels, 2 * channels), BF16),
            pltpu.SemaphoreType.DMA((segs // pair,)),
        ],
        compiler_params=pltpu.CompilerParams(vmem_limit_bytes=STREAM),
        name="main_spectra",
    )(raw, basis, taps)


def whiten_kernel(parts, count, me, taps, filtered, left, right, mask, *refs):
    near, far, other, total, powers = refs
    segs, channels = mask.shape
    height = near.shape[0]
    places = [(near, 0), (other, 0), (far, 0), (other, height)]
    rows = segs * EDGE
    share = NF // parts
    owner = lax.broadcasted_iota(jnp.int32, (rows, channels), 0) // EDGE
    band_left = filter_band(taps, count, -EDGE, (EDGE, channels))
    band_right = filter_band(taps, count, channels, (EDGE, channels))
    wide_left = jnp.concatenate([band_left] * segs, axis=0)
    wide_right = jnp.concatenate([band_right] * segs, axis=0)
    for seg in range(segs):
        here = owner == seg
        sums = dot(left[...], jnp.where(here, wide_left, 0.0).astype(BF16))
        sums += dot(right[...], jnp.where(here, wide_right, 0.0).astype(BF16))
        at = pl.ds(seg, 2 * NF, stride=segs)
        total[at, :] = sums
    powers[0:SMOOTH] = jnp.zeros((SMOOTH, segs, channels), F32)
    powers[SMOOTH + NF :] = jnp.zeros((SMOOTH, segs, channels), F32)
    block = 12

    def square(step, water):
        first = pl.multiple_of(step * (block * segs), segs)
        second = pl.multiple_of(first + NF * segs, segs)
        real = total[pl.ds(first, block * segs), :] + filtered[pl.ds(first, block * segs), :]
        imag = total[pl.ds(second, block * segs), :] + filtered[pl.ds(second, block * segs), :]
        total[pl.ds(first, block * segs), :] = real
        total[pl.ds(second, block * segs), :] = imag
        power = (real * real + imag * imag).reshape(block, segs, channels)
        powers[pl.ds(step * block + SMOOTH, block)] = power
        return water + power.sum(0)

    water = lax.fori_loop(0, NF // block, square, jnp.zeros((segs, channels), F32))
    floor = water * (water_share / NF) + epsilon
    good = mask[...].astype(F32)
    for k in range(parts):
        start = (me[0] ^ k) * share
        out, base = places[k]

        def spread(step, carry, start=start, out=out, base=base):
            bin_at = start + step * block
            cells = powers[pl.ds(bin_at, block + 2 * SMOOTH)]
            two = cells[:-1] + cells[1:]
            four = two[:-2] + two[2:]
            eight = four[:-4] + four[4:]
            nine = eight[:block] + cells[2 * SMOOTH :]
            scaled = good * lax.rsqrt(nine * (1.0 / (2 * SMOOTH + 1)) + floor)
            first = pl.multiple_of(bin_at * segs, segs)
            second = pl.multiple_of(first + NF * segs, segs)
            real = total[pl.ds(first, block * segs), :].reshape(block, segs, channels) * scaled
            imag = total[pl.ds(second, block * segs), :].reshape(block, segs, channels) * scaled
            both = jnp.concatenate([real[:, None], imag[:, None]], axis=1).astype(BF16)
            at = pl.multiple_of(base + step * (block * 2 * segs), segs)
            out[pl.ds(at, block * 2 * segs), :] = both.reshape(block * 2 * segs, channels)
            return carry

        lax.fori_loop(0, share // block, spread, 0)
        out[base + share * 2 * segs : base + height, :] = good.astype(BF16)


def whitened_parts(parts, me, taps, filtered, left, right, mask):
    segs, channels = mask.shape
    rows = NF // parts * 2 * segs + segs
    return pl.pallas_call(
        functools.partial(whiten_kernel, parts, taps.shape[0]),
        in_specs=[SCALARS] * 2 + [WHOLE] * 4,
        out_specs=[WHOLE] * 3,
        out_shape=[jax.ShapeDtypeStruct((height, channels), BF16) for height in (rows, rows, 2 * rows)],
        scratch_shapes=[
            pltpu.VMEM((2 * NF * segs, channels), F32),
            pltpu.VMEM((NF + 2 * SMOOTH, segs, channels), F32),
        ],
        compiler_params=pltpu.CompilerParams(vmem_limit_bytes=VMEM),
        name="whiten",
    )(me, taps, filtered, left, right, mask)


def gram_kernel(segs, bins, *refs):
    own, later, (out, cells, sems) = refs[:2], refs[2:4], refs[4:]
    channels = own[0].shape[1]
    height = own[0].shape[0] // 2
    share = out.shape[0]
    row = lax.broadcasted_iota(jnp.int32, (channels, channels), 0)
    column = lax.broadcasted_iota(jnp.int32, (channels, channels), 1)
    ahead = column > row
    skew = (row + column + 1) % channels
    offsets = [(ref, base) for ref in range(2) for base in (0, height)]

    def pieces(side, first, size):
        return [side[ref][pl.ds(base + first, size), :] for ref, base in offsets]

    mine = jnp.concatenate(pieces(own, height - segs, segs), axis=0)
    theirs = jnp.concatenate(pieces(later, height - segs, segs), axis=0)
    count = jnp.where(ahead, dot(mine, mine, TN), dot(mine, theirs, TN))
    scale = 1.0 / jnp.maximum(count, 1.0)

    def group(step, carry):
        for at in range(bins):
            bin_at = step * bins + at
            first = pl.multiple_of(bin_at * (2 * segs), 2 * segs)
            here = pieces(own, first, 2 * segs)
            mine = jnp.concatenate(here, axis=0)
            turned = jnp.concatenate(
                [piece for part in here for piece in (-part[segs:], part[:segs])], axis=0
            )
            theirs = jnp.concatenate(pieces(later, first, 2 * segs), axis=0)
            gram = dot(
                jnp.concatenate([mine, turned], axis=1), jnp.concatenate([mine, theirs], axis=1), TN
            )
            for part in range(2):
                rows = gram[part * channels : (part + 1) * channels]
                band = jnp.where(ahead, rows[:, :channels], rows[:, channels:]) * scale
                band = jnp.take_along_axis(band, skew, axis=1, mode="promise_in_bounds")
                cells[bin_at, pl.ds(part, channels, stride=2), :] = band
        at = pl.ds(step * bins, bins)
        pltpu.make_async_copy(cells.at[at], out.at[at], sems.at[step]).start()
        return carry

    lax.fori_loop(0, share // bins, group, 0)
    for step in range(share // bins):
        at = pl.ds(step * bins, bins)
        pltpu.make_async_copy(cells.at[at], out.at[at], sems.at[step]).wait()


def stacked(parts, segs, own, later):
    channels = own[0].shape[1]
    share = NF // parts
    bins = 4
    shape = (share, 2 * channels, LAGS)
    return pl.pallas_call(
        functools.partial(gram_kernel, segs, bins),
        in_specs=[WHOLE] * 4,
        out_specs=ANYWHERE,
        out_shape=jax.ShapeDtypeStruct(shape, F32),
        scratch_shapes=[pltpu.VMEM(shape, F32), pltpu.SemaphoreType.DMA((share // bins,))],
        compiler_params=pltpu.CompilerParams(vmem_limit_bytes=VMEM),
        name="gram",
    )(*own, *later)


def on_device(fibers, parts, raw_strain, fir_taps, good_mask):
    segs, channels, samples = raw_strain.shape
    basis = basis_rows(samples)
    me = lax.axis_index("seg").astype(jnp.int32)
    head, tail = edge_spectra(basis, raw_strain)
    left = lax.ppermute(tail, "fiber", [(i, i + 1) for i in range(fibers - 1)])
    right = lax.ppermute(head, "fiber", [(i + 1, i) for i in range(fibers - 1)])
    filtered = main_spectra(basis, raw_strain, fir_taps)
    near, far, other = whitened_parts(
        parts, me[None], fir_taps, filtered, left, right, good_mask
    )
    rows = near.shape[0]
    swapped = lax.ppermute(other, "seg", [(j, j ^ 1) for j in range(parts)])
    near = jnp.concatenate([near, swapped[:rows]], axis=0)
    far = jnp.concatenate([far, swapped[rows:]], axis=0)

    def following(cells, flip):
        pairs = [
            ((i + 1) * parts + (j ^ flip), i * parts + j)
            for i in range(fibers - 1)
            for j in range(parts)
        ]
        return lax.ppermute(cells, GRID, pairs)

    later_far = following(far, 2)
    own_far = lax.ppermute(far, "seg", [(j, j ^ 2) for j in range(parts)])
    later_near = following(near, 0)
    out = stacked(parts, segs, (near, own_far), (later_near, later_far))
    return out.reshape(out.shape[0], channels, 2, LAGS)


def solution(mesh):
    return jax.shard_map(
        functools.partial(on_device, mesh.shape["fiber"], mesh.shape["seg"]),
        mesh=mesh,
        in_specs=(P("seg", "fiber", None), P(), P("seg", "fiber")),
        out_specs=P("seg", "fiber", None, None),
        check_vma=False,
    )
```

time: 97.8 us -> 78.6 us (0.80)
  the two profiles are of different devices: /device:TPU:126 before, /device:TPU:110 now
where the time goes in v2:
time: 78.6 us; the launch traced here: 77.6 us
  waiting for transfers between devices  39.9 us (51%)
  Pallas kernels  22 us (28%)
  starting transfers between devices  14.2 us (18%)
  local copies, waits for them, and re-layouts  1.32 us (2%)
    ppermute x2, waiting for transfers between devices, following(): return lax.ppermute(cells, GRID, pairs)  35.8 us
    pallas_call x1, Pallas kernels, main_spectra(): pl.pallas_call(functools.partial(main_kernel, pair, taps.shape[0]), in_sp...  10.1 us
    ppermute x2, starting transfers between devices, following(): return lax.ppermute(cells, GRID, pairs)  6 us
    pallas_call x1, Pallas kernels, stacked(): pl.pallas_call(functools.partial(gram_kernel, segs, bins), in_specs=[WHOL...  5.91 us
    ppermute x1, starting transfers between devices, on_device(): left = lax.ppermute(tail, 'fiber', [(i, i + 1) for i in range(fibers - 1)])  4.84 us
    pallas_call x1, Pallas kernels, whitened_parts(): pl.pallas_call(functools.partial(whiten_kernel, parts, taps.shape[0]), in...  3.1 us
    pallas_call x1, Pallas kernels, edge_spectra(): pl.pallas_call(edge_kernel, in_specs=[ANYWHERE, WHOLE], out_specs=[WHOLE]...  2.92 us
    ppermute x1, waiting for transfers between devices, on_device(): own_far = lax.ppermute(far, 'seg', [(j, j ^ 2) for j in range(parts)])  2.09 us
  transfers between devices with their start and end apart: 6, of which 4 were waited for; matrix products, arithmetic and copies ran while one was open for 0% of the time, Pallas kernels for 13%

profile of v2, /device:TPU:110, one launch (start us, length us, event | category | flops | bytes accessed | tf_op | source)
XLA Modules:
  0.0 77.6 jit_solution(8302725640535872022)
XLA Ops:
  0.0 0.0 copy-start
  0.0 1.3 %copy-done = bf16[288,2048]{1,0:T(8,128)(2,1)S(1)} copy-done((bf16[288,2048]{1,0:T(8,128)(2,1)S(1)}, bf16[288,2048]{1,0:T(8,128)(2,1)}, u32[]{:S(2)}) %copy-start) | copy-done | bytes 1179672
  1.3 0.0 copy-start.1
  1.3 0.0 copy-start.3
  1.3 2.9 %edge_spectra.1 = (bf16[288,256]{1,0:T(8,128)(2,1)S(1)}, bf16[288,256]{1,0:T(8,128)(2,1)S(1)}) custom-call(bf16[16,128,2048]{2,1,0:T(8,128)(2,1)} %raw.3, bf16[288,2048]{1,0:T(8,128)(2,1)S(1)} %copy-done), custom_call_target="tpu_custom_call" | custom-call | tf_op jit(solution)/shard_map/edge_spectra/pallas_call | solution.py:75
  4.2 4.8 %collective-permute-start = (bf16[288,256]{1,0:T(8,128)(2,1)S(1)}, bf16[288,256]{1,0:T(8,128)(2,1)S(1)}, u32[]{:S(2)}, u32[]{:S(2)}) collective-permute-start(bf16[288,256]{1,0:T(8,128)(2,1)S(1)} %get-tuple-element.10), channel_id=1, source_target_pairs={{0,4},{4,8},{8,12},{12,16},{16,20},{20,24},{24,28},{28,32},{32,36}... | collective-permute-start | bytes 442376 | tf_op jit(solution)/shard_map/ppermute | solution.py:286
  9.0 1.9 %collective-permute-start.1 = (bf16[288,256]{1,0:T(8,128)(2,1)S(1)}, bf16[288,256]{1,0:T(8,128)(2,1)S(1)}, u32[]{:S(2)}, u32[]{:S(2)}) collective-permute-start(bf16[288,256]{1,0:T(8,128)(2,1)S(1)} %get-tuple-element.11), channel_id=1, source_target_pairs={{4,0},{8,4},{12,8},{16,12},{20,16},{24,20},{28,24},{32,28},{36,32}... | collective-permute-start | bytes 442376 | tf_op jit(solution)/shard_map/ppermute | solution.py:287
  11.0 0.0 copy-done.1
  11.0 0.0 copy-done.3
  11.0 0.0 copy-start.2
  11.0 10.1 %main_spectra.1.filtered = f32[4608,128]{1,0:T(8,128)S(1)} custom-call(bf16[16,128,2048]{2,1,0:T(8,128)(2,1)} %raw.3, bf16[288,2048]{1,0:T(8,128)(2,1)S(1)} %copy-done.1, f32[31]{0:T(128)S(1)} %copy-done.3), custom_call_target="tpu_custom_call" | custom-call | tf_op jit(solution)/shard_map/main_spectra/pallas_call | solution.py:125
  21.1 0.0 collective-permute-done.left
  21.1 0.0 collective-permute-done.1.right
  21.1 0.0 copy-done.2
  21.1 3.1 %whiten.1 = (bf16[1168,128]{1,0:T(8,128)(2,1)S(1)}, bf16[1168,128]{1,0:T(8,128)(2,1)S(1)}, bf16[2336,128]{1,0:T(8,128)(2,1)S(1)}) custom-call(s32[1]{0:T(128)} %bitcast.me, f32[31]{0:T(128)S(1)} %copy-done.3, f32[4608,128]{1,0:T(8,128)S(1)} %main_spectra.1.filtered, bf16[288,256]{1,0:T(8,128)(2,1)S(1)} %collective-permute-done.left, ...), custom_call_target="tpu_custom_call" | custom-call | tf_op jit(solution)/shard_map/whiten/pallas_call | solution.py:204
  24.2 0.1 collective-permute-start.2
  24.3 2.0 %collective-permute-done.2 = bf16[2336,128]{1,0:T(8,128)(2,1)S(1)} collective-permute-done((bf16[2336,128]{1,0:T(8,128)(2,1)S(1)}, bf16[2336,128]{1,0:T(8,128)(2,1)S(1)}, u32[]{:S(2)}, u32[]{:S(2)}) %collective-permute-start.2) | collective-permute-done | bytes 598048 | tf_op jit(solution)/shard_map/ppermute | solution.py:293
  26.4 1.9 %collective-permute-start.4 = (bf16[2336,128]{1,0:T(8,128)(2,1)S(1)}, bf16[2336,128]{1,0:T(8,128)(2,1)S(1)}, u32[]{:S(2)}, u32[]{:S(2)}) collective-permute-start(bf16[2336,128]{1,0:T(8,128)(2,1)S(1)} %pad_maximum_fusion.refs_0_), channel_id=1, source_target_pairs={{4,0},{5,1},{6,2},{7,3},{8,4},{9,5},{10,6},{11,7},{12,8},{13,9},{1... | collective-permute-start | bytes 1794056 | tf_op jit(solution)/shard_map/ppermute | solution.py:303
  28.4 4.1 %collective-permute-start.5 = (bf16[2336,128]{1,0:T(8,128)(2,1)S(1)}, bf16[2336,128]{1,0:T(8,128)(2,1)S(1)}, u32[]{:S(2)}, u32[]{:S(2)}) collective-permute-start(bf16[2336,128]{1,0:T(8,128)(2,1)S(1)} %pad_maximum_fusion.1), channel_id=1, source_target_pairs={{6,0},{7,1},{4,2},{5,3},{10,4},{11,5},{8,6},{9,7},{14,8},{15,9},{1... | collective-permute-start | bytes 1794056 | tf_op jit(solution)/shard_map/ppermute | solution.py:303
  32.5 1.3 %collective-permute-start.3 = (bf16[2336,128]{1,0:T(8,128)(2,1)S(1)}, bf16[2336,128]{1,0:T(8,128)(2,1)S(1)}, u32[]{:S(2)}, u32[]{:S(2)}) collective-permute-start(bf16[2336,128]{1,0:T(8,128)(2,1)S(1)} %pad_maximum_fusion.1), channel_id=1, source_target_pairs={{0,2},{1,3},{2,0},{3,1},{4,6},{5,7},{6,4},{7,5},{8,10},{9,11},{10,... | collective-permute-start | bytes 1794056 | tf_op jit(solution)/shard_map/ppermute | solution.py:306
  33.8 15.1 %collective-permute-done.4.refs_2_ = bf16[2336,128]{1,0:T(8,128)(2,1)S(1)} collective-permute-done((bf16[2336,128]{1,0:T(8,128)(2,1)S(1)}, bf16[2336,128]{1,0:T(8,128)(2,1)S(1)}, u32[]{:S(2)}, u32[]{:S(2)}) %collective-permute-start.4) | collective-permute-done | bytes 598048 | tf_op jit(solution)/shard_map/ppermute | solution.py:303
  48.9 20.7 %collective-permute-done.5.refs_3_ = bf16[2336,128]{1,0:T(8,128)(2,1)S(1)} collective-permute-done((bf16[2336,128]{1,0:T(8,128)(2,1)S(1)}, bf16[2336,128]{1,0:T(8,128)(2,1)S(1)}, u32[]{:S(2)}, u32[]{:S(2)}) %collective-permute-start.5) | collective-permute-done | bytes 598048 | tf_op jit(solution)/shard_map/ppermute | solution.py:303
  69.6 2.1 %collective-permute-done.3.refs_1_ = bf16[2336,128]{1,0:T(8,128)(2,1)S(1)} collective-permute-done((bf16[2336,128]{1,0:T(8,128)(2,1)S(1)}, bf16[2336,128]{1,0:T(8,128)(2,1)S(1)}, u32[]{:S(2)}, u32[]{:S(2)}) %collective-permute-start.3) | collective-permute-done | bytes 598048 | tf_op jit(solution)/shard_map/ppermute | solution.py:306
  71.7 5.9 %gram.1 = f32[36,256,128]{2,1,0:T(8,128)} custom-call(bf16[2336,128]{1,0:T(8,128)(2,1)S(1)} %pad_maximum_fusion.refs_0_, bf16[2336,128]{1,0:T(8,128)(2,1)S(1)} %collective-permute-done.3.refs_1_, bf16[2336,128]{1,0:T(8,128)(2,1)S(1)} %collective-permute-done.4.refs_2_, bf16[2336,128]{1,0:T(8,128)(2,1)S(1)} %collective-permute-done.5.refs_3_), custom_call_target="tpu_custom_call" | custom-call | tf_op jit(solution)/shard_map/gram/pallas_call | solution.py:270
  (3 shorter events, 0.1 us)
Async XLA Ops:
  0.0 1.3 %copy-start = (bf16[288,2048]{1,0:T(8,128)(2,1)S(1)}, bf16[288,2048]{1,0:T(8,128)(2,1)}, u32[]{:S(2)}) copy-start(bf16[288,2048]{1,0:T(8,128)(2,1)} %constant.6.clone.basis) | copy-start | bytes 3538948
  1.3 9.7 %copy-start.1 = (bf16[288,2048]{1,0:T(8,128)(2,1)S(1)}, bf16[288,2048]{1,0:T(8,128)(2,1)}, u32[]{:S(2)}) copy-start(bf16[288,2048]{1,0:T(8,128)(2,1)} %constant.6.clone.basis) | copy-start | bytes 3538948
  1.3 9.7 %copy-start.3 = (f32[31]{0:T(128)S(1)}, f32[31]{0:T(128)}, u32[]{:S(2)}) copy-start(f32[31]{0:T(128)} %taps.3) | copy-start | bytes 376
  4.2 16.9 %collective-permute-start = (bf16[288,256]{1,0:T(8,128)(2,1)S(1)}, bf16[288,256]{1,0:T(8,128)(2,1)S(1)}, u32[]{:S(2)}, u32[]{:S(2)}) collective-permute-start(bf16[288,256]{1,0:T(8,128)(2,1)S(1)} %get-tuple-element.10), channel_id=1, source_target_pairs={{0,4},{4,8},{8,12},{12,16},{16,20},{20,24},{24,28},{28,32},{32,36}... | collective-permute-start | bytes 442376 | tf_op jit(solution)/shard_map/ppermute | solution.py:286
  9.0 12.0 %collective-permute-start.1 = (bf16[288,256]{1,0:T(8,128)(2,1)S(1)}, bf16[288,256]{1,0:T(8,128)(2,1)S(1)}, u32[]{:S(2)}, u32[]{:S(2)}) collective-permute-start(bf16[288,256]{1,0:T(8,128)(2,1)S(1)} %get-tuple-element.11), channel_id=1, source_target_pairs={{4,0},{8,4},{12,8},{16,12},{20,16},{24,20},{28,24},{32,28},{36,32}... | collective-permute-start | bytes 442376 | tf_op jit(solution)/shard_map/ppermute | solution.py:287
  11.0 10.1 %copy-start.2 = (s32[16,128]{1,0:T(8,128)S(1)}, s32[16,128]{1,0:T(8,128)}, u32[]{:S(2)}) copy-start(s32[16,128]{1,0:T(8,128)} %mask.1) | copy-start | bytes 24580
  24.2 2.1 %collective-permute-start.2 = (bf16[2336,128]{1,0:T(8,128)(2,1)S(1)}, bf16[2336,128]{1,0:T(8,128)(2,1)S(1)}, u32[]{:S(2)}, u32[]{:S(2)}) collective-permute-start(bf16[2336,128]{1,0:T(8,128)(2,1)S(1)} %get-tuple-element.13), channel_id=1, source_target_pairs={{0,1},{1,0},{2,3},{3,2},{4,5},{5,4},{6,7},{7,6},{8,9},{9,8},{10,11... | collective-permute-start | bytes 1794056 | tf_op jit(solution)/shard_map/ppermute | solution.py:293
  26.4 22.5 %collective-permute-start.4 = (bf16[2336,128]{1,0:T(8,128)(2,1)S(1)}, bf16[2336,128]{1,0:T(8,128)(2,1)S(1)}, u32[]{:S(2)}, u32[]{:S(2)}) collective-permute-start(bf16[2336,128]{1,0:T(8,128)(2,1)S(1)} %pad_maximum_fusion.refs_0_), channel_id=1, source_target_pairs={{4,0},{5,1},{6,2},{7,3},{8,4},{9,5},{10,6},{11,7},{12,8},{13,9},{1... | collective-permute-start | bytes 1794056 | tf_op jit(solution)/shard_map/ppermute | solution.py:303
  28.4 41.2 %collective-permute-start.5 = (bf16[2336,128]{1,0:T(8,128)(2,1)S(1)}, bf16[2336,128]{1,0:T(8,128)(2,1)S(1)}, u32[]{:S(2)}, u32[]{:S(2)}) collective-permute-start(bf16[2336,128]{1,0:T(8,128)(2,1)S(1)} %pad_maximum_fusion.1), channel_id=1, source_target_pairs={{6,0},{7,1},{4,2},{5,3},{10,4},{11,5},{8,6},{9,7},{14,8},{15,9},{1... | collective-permute-start | bytes 1794056 | tf_op jit(solution)/shard_map/ppermute | solution.py:303
  32.5 39.2 %collective-permute-start.3 = (bf16[2336,128]{1,0:T(8,128)(2,1)S(1)}, bf16[2336,128]{1,0:T(8,128)(2,1)S(1)}, u32[]{:S(2)}, u32[]{:S(2)}) collective-permute-start(bf16[2336,128]{1,0:T(8,128)(2,1)S(1)} %pad_maximum_fusion.1), channel_id=1, source_target_pairs={{0,2},{1,3},{2,0},{3,1},{4,6},{5,7},{6,4},{7,5},{8,10},{9,11},{10,... | collective-permute-start | bytes 1794056 | tf_op jit(solution)/shard_map/ppermute | solution.py:306

commit v3 on v2

--- a/solution.py
+++ b/solution.py
@@ -56,17 +56,10 @@
 ANYWHERE = pl.BlockSpec(memory_space=pl.ANY)
 
 
-def edge_kernel(raw, basis, head, tail, cells, sems):
-    segs, channels, samples = raw.shape
-    copies = [
-        pltpu.make_async_copy(raw.at[:, pl.ds(first, EDGE), :], cells.at[at], sems.at[at])
-        for at, first in enumerate((channels - EDGE, 0))
-    ]
-    for copy in copies:
-        copy.start()
-    for at, out in enumerate((tail, head)):
-        copies[at].wait()
-        out[...] = dot(basis[...], cells[at].reshape(segs * EDGE, samples), NT).astype(BF16)
+def edge_kernel(first, last, basis, head, tail):
+    for cells, out in ((last, tail), (first, head)):
+        segs, width, samples = cells.shape
+        out[...] = dot(basis[...], cells[...].reshape(segs * width, samples), NT).astype(BF16)
 
 
 def edge_spectra(basis, raw):
@@ -74,28 +67,16 @@
     out = jax.ShapeDtypeStruct((2 * NF, segs * EDGE), BF16)
     return pl.pallas_call(
         edge_kernel,
-        in_specs=[ANYWHERE, WHOLE],
+        in_specs=[WHOLE] * 3,
         out_specs=[WHOLE] * 2,
         out_shape=[out, out],
-        scratch_shapes=[
-            pltpu.VMEM((2, segs, EDGE, samples), BF16),
-            pltpu.SemaphoreType.DMA((2,)),
-        ],
-        compiler_params=pltpu.CompilerParams(vmem_limit_bytes=STREAM),
+        compiler_params=pltpu.CompilerParams(vmem_limit_bytes=VMEM),
         name="edge_spectra",
-    )(raw, basis)
-
-
-def main_kernel(pair, count, raw, basis, taps, filtered, cells, both, sems):
+    )(raw[:, :EDGE], raw[:, channels - EDGE :], basis)
+
+
+def main_kernel(pair, count, raw, basis, taps, filtered, both):
     segs, channels, samples = raw.shape
-    copies = [
-        pltpu.make_async_copy(
-            raw.at[pl.ds(at * pair, pair)], cells.at[pl.ds(at * pair, pair)], sems.at[at]
-        )
-        for at in range(segs // pair)
-    ]
-    for copy in copies:
-        copy.start()
     band = filter_band(taps, count, 0, (channels, channels))
     high = band.astype(BF16)
     low = (band - high.astype(F32)).astype(BF16)
@@ -107,8 +88,7 @@
         axis=0,
     )
     for step in range(segs // pair):
-        copies[step].wait()
-        block = cells[step * pair : (step + 1) * pair].reshape(pair * channels, samples)
+        block = raw[step * pair : (step + 1) * pair].reshape(pair * channels, samples)
         spectra = dot(basis[...], block, NT)
         for at in range(pair):
             part = spectra[:, at * channels : (at + 1) * channels]
@@ -121,40 +101,34 @@
 
 def main_spectra(basis, raw, taps):
     segs, channels, samples = raw.shape
-    pair = 2
     return pl.pallas_call(
-        functools.partial(main_kernel, pair, taps.shape[0]),
-        in_specs=[ANYWHERE, WHOLE, SCALARS],
+        functools.partial(main_kernel, 4, taps.shape[0]),
+        in_specs=[WHOLE, WHOLE, SCALARS],
         out_specs=WHOLE,
         out_shape=jax.ShapeDtypeStruct((2 * NF * segs, channels), F32),
-        scratch_shapes=[
-            pltpu.VMEM((segs, channels, samples), BF16),
-            pltpu.VMEM((2 * channels, 2 * channels), BF16),
-            pltpu.SemaphoreType.DMA((segs // pair,)),
-        ],
-        compiler_params=pltpu.CompilerParams(vmem_limit_bytes=STREAM),
+        scratch_shapes=[pltpu.VMEM((2 * channels, 2 * channels), BF16)],
+        compiler_params=pltpu.CompilerParams(vmem_limit_bytes=VMEM),
         name="main_spectra",
     )(raw, basis, taps)
 
 
 def whiten_kernel(parts, count, me, taps, filtered, left, right, mask, *refs):
     near, far, other, total, powers = refs
-    segs, channels = mask.shape
+    segs, channels = powers.shape[1:]
     height = near.shape[0]
     places = [(near, 0), (other, 0), (far, 0), (other, height)]
-    rows = segs * EDGE
     share = NF // parts
-    owner = lax.broadcasted_iota(jnp.int32, (rows, channels), 0) // EDGE
-    band_left = filter_band(taps, count, -EDGE, (EDGE, channels))
-    band_right = filter_band(taps, count, channels, (EDGE, channels))
-    wide_left = jnp.concatenate([band_left] * segs, axis=0)
-    wide_right = jnp.concatenate([band_right] * segs, axis=0)
+    width = segs * EDGE
+    owner = lax.broadcasted_iota(jnp.int32, (2 * width, channels), 0) // EDGE % segs
+    wide = jnp.concatenate(
+        [filter_band(taps, count, -EDGE, (EDGE, channels))] * segs
+        + [filter_band(taps, count, channels, (EDGE, channels))] * segs,
+        axis=0,
+    )
+    sides = jnp.concatenate([left[...], right[...]], axis=1)
     for seg in range(segs):
-        here = owner == seg
-        sums = dot(left[...], jnp.where(here, wide_left, 0.0).astype(BF16))
-        sums += dot(right[...], jnp.where(here, wide_right, 0.0).astype(BF16))
         at = pl.ds(seg, 2 * NF, stride=segs)
-        total[at, :] = sums
+        total[at, :] = dot(sides, jnp.where(owner == seg, wide, 0.0).astype(BF16))
     powers[0:SMOOTH] = jnp.zeros((SMOOTH, segs, channels), F32)
     powers[SMOOTH + NF :] = jnp.zeros((SMOOTH, segs, channels), F32)
     block = 12
@@ -189,9 +163,9 @@
             second = pl.multiple_of(first + NF * segs, segs)
             real = total[pl.ds(first, block * segs), :].reshape(block, segs, channels) * scaled
             imag = total[pl.ds(second, block * segs), :].reshape(block, segs, channels) * scaled
-            both = jnp.concatenate([real[:, None], imag[:, None]], axis=1).astype(BF16)
-            at = pl.multiple_of(base + step * (block * 2 * segs), segs)
-            out[pl.ds(at, block * 2 * segs), :] = both.reshape(block * 2 * segs, channels)
+            both = jnp.concatenate([real[:, None], imag[:, None]], axis=1)
+            at = pl.multiple_of(base + step * (block * 2 * segs), 2 * segs)
+            out[pl.ds(at, block * 2 * segs), :] = both.reshape(block * 2 * segs, channels).astype(BF16)
             return carry
 
         lax.fori_loop(0, share // block, spread, 0)
@@ -215,67 +189,82 @@
     )(me, taps, filtered, left, right, mask)
 
 
-def gram_kernel(segs, bins, *refs):
-    own, later, (out, cells, sems) = refs[:2], refs[2:4], refs[4:]
-    channels = own[0].shape[1]
-    height = own[0].shape[0] // 2
-    share = out.shape[0]
+def gram_kernel(segs, bins, last, *refs):
+    own, later = refs[:2]
+    if last:
+        before, before_count, out, cells, sems = refs[2:]
+    else:
+        cells, count_out = refs[2:]
+    channels = own.shape[1]
+    height = own.shape[0] // 2
+    share = cells.shape[0]
     row = lax.broadcasted_iota(jnp.int32, (channels, channels), 0)
     column = lax.broadcasted_iota(jnp.int32, (channels, channels), 1)
     ahead = column > row
     skew = (row + column + 1) % channels
-    offsets = [(ref, base) for ref in range(2) for base in (0, height)]
 
     def pieces(side, first, size):
-        return [side[ref][pl.ds(base + first, size), :] for ref, base in offsets]
-
-    mine = jnp.concatenate(pieces(own, height - segs, segs), axis=0)
-    theirs = jnp.concatenate(pieces(later, height - segs, segs), axis=0)
+        rows = [side[pl.ds(base + first, size), :] for base in (0, height)]
+        return jnp.concatenate(rows, axis=0)
+
+    mine = pieces(own, height - segs, segs)
+    theirs = pieces(later, height - segs, segs)
     count = jnp.where(ahead, dot(mine, mine, TN), dot(mine, theirs, TN))
-    scale = 1.0 / jnp.maximum(count, 1.0)
+    if last:
+        scale = 1.0 / jnp.maximum(count + before_count[...], 1.0)
+    else:
+        count_out[...] = count
 
     def group(step, carry):
         for at in range(bins):
             bin_at = step * bins + at
             first = pl.multiple_of(bin_at * (2 * segs), 2 * segs)
-            here = pieces(own, first, 2 * segs)
-            mine = jnp.concatenate(here, axis=0)
-            turned = jnp.concatenate(
-                [piece for part in here for piece in (-part[segs:], part[:segs])], axis=0
-            )
-            theirs = jnp.concatenate(pieces(later, first, 2 * segs), axis=0)
+            mine = pieces(own, first, 2 * segs)
+            theirs = pieces(later, first, 2 * segs)
+            split = mine.astype(F32).reshape(mine.shape[0] // (2 * segs), 2, segs, channels)
+            turned = jnp.concatenate([-split[:, 1:], split[:, :1]], axis=1)
+            turned = turned.reshape(mine.shape).astype(BF16)
             gram = dot(
                 jnp.concatenate([mine, turned], axis=1), jnp.concatenate([mine, theirs], axis=1), TN
             )
             for part in range(2):
                 rows = gram[part * channels : (part + 1) * channels]
-                band = jnp.where(ahead, rows[:, :channels], rows[:, channels:]) * scale
-                band = jnp.take_along_axis(band, skew, axis=1, mode="promise_in_bounds")
-                cells[bin_at, pl.ds(part, channels, stride=2), :] = band
-        at = pl.ds(step * bins, bins)
-        pltpu.make_async_copy(cells.at[at], out.at[at], sems.at[step]).start()
+                band = jnp.where(ahead, rows[:, :channels], rows[:, channels:])
+                if last:
+                    band = (band + before[bin_at, part * channels : (part + 1) * channels, :]) * scale
+                    band = jnp.take_along_axis(band, skew, axis=1, mode="promise_in_bounds")
+                    cells[bin_at, pl.ds(part, channels, stride=2), :] = band
+                else:
+                    cells[bin_at, part * channels : (part + 1) * channels, :] = band
+        if last:
+            at = pl.ds(step * bins, bins)
+            pltpu.make_async_copy(cells.at[at], out.at[at], sems.at[step]).start()
         return carry
 
     lax.fori_loop(0, share // bins, group, 0)
-    for step in range(share // bins):
-        at = pl.ds(step * bins, bins)
-        pltpu.make_async_copy(cells.at[at], out.at[at], sems.at[step]).wait()
-
-
-def stacked(parts, segs, own, later):
-    channels = own[0].shape[1]
+    if last:
+        for step in range(share // bins):
+            at = pl.ds(step * bins, bins)
+            pltpu.make_async_copy(cells.at[at], out.at[at], sems.at[step]).wait()
+
+
+def stacked(parts, segs, own, later, before=()):
+    channels = own.shape[1]
     share = NF // parts
     bins = 4
-    shape = (share, 2 * channels, LAGS)
+    last = bool(before)
+    sums = jax.ShapeDtypeStruct((share, 2 * channels, LAGS), F32)
+    count = jax.ShapeDtypeStruct((channels, channels), F32)
+    scratch = [pltpu.VMEM(sums.shape, F32), pltpu.SemaphoreType.DMA((share // bins,))]
     return pl.pallas_call(
-        functools.partial(gram_kernel, segs, bins),
-        in_specs=[WHOLE] * 4,
-        out_specs=ANYWHERE,
-        out_shape=jax.ShapeDtypeStruct(shape, F32),
-        scratch_shapes=[pltpu.VMEM(shape, F32), pltpu.SemaphoreType.DMA((share // bins,))],
+        functools.partial(gram_kernel, segs, bins, last),
+        in_specs=[WHOLE] * (2 + len(before)),
+        out_specs=ANYWHERE if last else [WHOLE] * 2,
+        out_shape=sums if last else [sums, count],
+        scratch_shapes=scratch if last else [],
         compiler_params=pltpu.CompilerParams(vmem_limit_bytes=VMEM),
         name="gram",
-    )(*own, *later)
+    )(own, later, *before)
 
 
 def on_device(fibers, parts, raw_strain, fir_taps, good_mask):
@@ -305,7 +294,8 @@
     later_far = following(far, 2)
     own_far = lax.ppermute(far, "seg", [(j, j ^ 2) for j in range(parts)])
     later_near = following(near, 0)
-    out = stacked(parts, segs, (near, own_far), (later_near, later_far))
+    before = stacked(parts, segs, near, later_near)
+    out = stacked(parts, segs, own_far, later_far, before)
     return out.reshape(out.shape[0], channels, 2, LAGS)
 
 

time: 78.6 us -> 75.4 us (0.959)
  Pallas kernels: 22 us -> 18 us
  local copies, waits for them, and re-layouts: 1.32 us -> 5.32 us
  waiting for transfers between devices: 39.9 us -> 37.5 us
  starting transfers between devices: 14.2 us -> 13.4 us
    pallas_call x3 -> x4, Pallas kernels: 18.9 us -> 14.9 us  [the longest x2 9.65 us: stacked(): pl.pallas_call(functools.partial(gram_kernel, segs, bins, last), in_specs...]
    ppermute x2, waiting for transfers between devices: 35.8 us -> 33 us  [following(): return lax.ppermute(cells, GRID, pairs)]
    unnamed x8, local copies, waits for them, and re-layouts: 1.28 us -> 3.4 us
    slice x1 -> x2, local copies, waits for them, and re-layouts: 0.04 us -> 1.92 us  [the longest x1 1.88 us: edge_spectra(): raw[:, channels - EDGE:]]
    ppermute x1, waiting for transfers between devices: 0.01 us -> 1.66 us  [on_device(): right = lax.ppermute(head, 'fiber', [(i + 1, i) for i in range(fibers - 1)])]
    ppermute x2, starting transfers between devices: 6 us -> 4.36 us  [following(): return lax.ppermute(cells, GRID, pairs)]
    ppermute x1, waiting for transfers between devices: 2.09 us -> 0.84 us  [on_device(): own_far = lax.ppermute(far, 'seg', [(j, j ^ 2) for j in range(parts)])]
    ppermute x1, starting transfers between devices: 1.32 us -> 2.16 us  [on_device(): own_far = lax.ppermute(far, 'seg', [(j, j ^ 2) for j in range(parts)])]
  transfers between devices with their start and end apart: 6 -> 6, of which waited for: 4 -> 5; matrix products, arithmetic and copies ran while one was open for 0% -> 0% of each run, Pallas kernels for 13% -> 10%
where the time goes in v3:
time: 75.4 us; the launch traced here: 74.4 us
  waiting for transfers between devices  37.5 us (50%)
  Pallas kernels  18 us (24%)
  starting transfers between devices  13.4 us (18%)
  local copies, waits for them, and re-layouts  5.32 us (7%)
    ppermute x2, waiting for transfers between devices, following(): return lax.ppermute(cells, GRID, pairs)  33 us
    pallas_call x2, Pallas kernels, stacked(): pl.pallas_call(functools.partial(gram_kernel, segs, bins, last), in_specs...  9.65 us
    ppermute x1, starting transfers between devices, on_device(): left = lax.ppermute(tail, 'fiber', [(i, i + 1) for i in range(fibers - 1)])  4.84 us
    pallas_call x1, Pallas kernels, main_spectra(): pl.pallas_call(functools.partial(main_kernel, 4, taps.shape[0]), in_specs...  4.41 us
    ppermute x2, starting transfers between devices, following(): return lax.ppermute(cells, GRID, pairs)  4.36 us
    unnamed x8, local copies, waits for them, and re-layouts  3.4 us
    pallas_call x1, Pallas kernels, whitened_parts(): pl.pallas_call(functools.partial(whiten_kernel, parts, taps.shape[0]), in...  3.1 us
    ppermute x1, starting transfers between devices, on_device(): own_far = lax.ppermute(far, 'seg', [(j, j ^ 2) for j in range(parts)])  2.16 us
  transfers between devices with their start and end apart: 6, of which 5 were waited for; matrix products, arithmetic and copies ran while one was open for 0% of the time, Pallas kernels for 10%

profile of v3, /device:TPU:110, one launch (start us, length us, event | category | flops | bytes accessed | tf_op | source)
XLA Modules:
  0.0 74.4 jit_solution(17332120564710743343)
XLA Ops:
  0.0 0.0 copy-start.1
  0.0 1.9 %fusion = (bf16[16,16,2048]{2,1,0:T(8,128)(2,1)S(1)}, bf16[16,16,2048]{2,1,0:T(8,128)(2,1)S(1)}) fusion(bf16[16,128,2048]{2,1,0:T(8,128)(2,1)} %raw.1), kind=kLoop, calls=%fused_computation.2 | loop fusion | bytes 4194304 | tf_op jit(solution)/shard_map/slice | solution.py:75
  1.9 0.0 copy-done.1
  1.9 0.0 copy-start.3
  1.9 0.8 %edge_spectra.1 = (bf16[288,256]{1,0:T(8,128)(2,1)S(1)}, bf16[288,256]{1,0:T(8,128)(2,1)S(1)}) custom-call(bf16[16,16,2048]{2,1,0:T(8,128)(2,1)S(1)} %get-tuple-element.20.first, bf16[16,16,2048]{2,1,0:T(8,128)(2,1)S(1)} %get-tuple-element.19.last, bf16[288,2048]{1,0:T(8,128)(2,1)S(1)} %copy-done.1), custom_call_target="tpu_custom_call" | custom-call | tf_op jit(solution)/shard_map/edge_spectra/pallas_call | solution.py:68
  2.7 4.8 %collective-permute-start = (bf16[288,256]{1,0:T(8,128)(2,1)S(1)}, bf16[288,256]{1,0:T(8,128)(2,1)S(1)}, u32[]{:S(2)}, u32[]{:S(2)}) collective-permute-start(bf16[288,256]{1,0:T(8,128)(2,1)S(1)} %get-tuple-element.12), channel_id=1, source_target_pairs={{0,4},{4,8},{8,12},{12,16},{16,20},{20,24},{24,28},{28,32},{32,36}... | collective-permute-start | bytes 442376 | tf_op jit(solution)/shard_map/ppermute | solution.py:275
  7.6 1.9 %collective-permute-start.1 = (bf16[288,256]{1,0:T(8,128)(2,1)S(1)}, bf16[288,256]{1,0:T(8,128)(2,1)S(1)}, u32[]{:S(2)}, u32[]{:S(2)}) collective-permute-start(bf16[288,256]{1,0:T(8,128)(2,1)S(1)} %get-tuple-element.13), channel_id=1, source_target_pairs={{4,0},{8,4},{12,8},{16,12},{20,16},{24,20},{28,24},{32,28},{36,32}... | collective-permute-start | bytes 442376 | tf_op jit(solution)/shard_map/ppermute | solution.py:276
  9.5 0.0 copy-done.3
  9.5 0.0 copy-start
  9.5 3.4 %copy-done = bf16[16,128,2048]{2,1,0:T(8,128)(2,1)S(1)} copy-done((bf16[16,128,2048]{2,1,0:T(8,128)(2,1)S(1)}, bf16[16,128,2048]{2,1,0:T(8,128)(2,1)}, u32[]{:S(2)}) %copy-start) | copy-done | bytes 8388632
  12.9 0.0 copy-start.2
  12.9 4.4 %main_spectra.1.filtered = f32[4608,128]{1,0:T(8,128)S(1)} custom-call(bf16[16,128,2048]{2,1,0:T(8,128)(2,1)S(1)} %copy-done, bf16[288,2048]{1,0:T(8,128)(2,1)S(1)} %copy-done.1, f32[31]{0:T(128)S(1)} %copy-done.3), custom_call_target="tpu_custom_call" | custom-call | tf_op jit(solution)/shard_map/main_spectra/pallas_call | solution.py:104
  17.3 0.0 collective-permute-done.left
  17.3 1.7 %collective-permute-done.1.right = bf16[288,256]{1,0:T(8,128)(2,1)S(1)} collective-permute-done((bf16[288,256]{1,0:T(8,128)(2,1)S(1)}, bf16[288,256]{1,0:T(8,128)(2,1)S(1)}, u32[]{:S(2)}, u32[]{:S(2)}) %collective-permute-start.1) | collective-permute-done | bytes 147488 | tf_op jit(solution)/shard_map/ppermute | solution.py:276
  19.0 0.0 copy-done.2
  19.0 3.1 %whiten.1 = (bf16[1168,128]{1,0:T(8,128)(2,1)S(1)}, bf16[1168,128]{1,0:T(8,128)(2,1)S(1)}, bf16[2336,128]{1,0:T(8,128)(2,1)S(1)}) custom-call(s32[1]{0:T(128)} %bitcast.me, f32[31]{0:T(128)S(1)} %copy-done.3, f32[4608,128]{1,0:T(8,128)S(1)} %main_spectra.1.filtered, bf16[288,256]{1,0:T(8,128)(2,1)S(1)} %collective-permute-done.left, ...), custom_call_target="tpu_custom_call" | custom-call | tf_op jit(solution)/shard_map/whiten/pallas_call | solution.py:178
  22.1 0.1 collective-permute-start.2
  22.2 2.0 %collective-permute-done.2 = bf16[2336,128]{1,0:T(8,128)(2,1)S(1)} collective-permute-done((bf16[2336,128]{1,0:T(8,128)(2,1)S(1)}, bf16[2336,128]{1,0:T(8,128)(2,1)S(1)}, u32[]{:S(2)}, u32[]{:S(2)}) %collective-permute-start.2) | collective-permute-done | bytes 598048 | tf_op jit(solution)/shard_map/ppermute | solution.py:282
  24.3 1.9 %collective-permute-start.5 = (bf16[2336,128]{1,0:T(8,128)(2,1)S(1)}, bf16[2336,128]{1,0:T(8,128)(2,1)S(1)}, u32[]{:S(2)}, u32[]{:S(2)}) collective-permute-start(bf16[2336,128]{1,0:T(8,128)(2,1)S(1)} %pad_maximum_fusion.1.refs_0_), channel_id=1, source_target_pairs={{4,0},{5,1},{6,2},{7,3},{8,4},{9,5},{10,6},{11,7},{12,8},{13,9},{1... | collective-permute-start | bytes 1794056 | tf_op jit(solution)/shard_map/ppermute | solution.py:292
  26.3 2.4 %collective-permute-start.4 = (bf16[2336,128]{1,0:T(8,128)(2,1)S(1)}, bf16[2336,128]{1,0:T(8,128)(2,1)S(1)}, u32[]{:S(2)}, u32[]{:S(2)}) collective-permute-start(bf16[2336,128]{1,0:T(8,128)(2,1)S(1)} %pad_maximum_fusion), channel_id=1, source_target_pairs={{6,0},{7,1},{4,2},{5,3},{10,4},{11,5},{8,6},{9,7},{14,8},{15,9},{1... | collective-permute-start | bytes 1794056 | tf_op jit(solution)/shard_map/ppermute | solution.py:292
  28.7 2.2 %collective-permute-start.3 = (bf16[2336,128]{1,0:T(8,128)(2,1)S(1)}, bf16[2336,128]{1,0:T(8,128)(2,1)S(1)}, u32[]{:S(2)}, u32[]{:S(2)}) collective-permute-start(bf16[2336,128]{1,0:T(8,128)(2,1)S(1)} %pad_maximum_fusion), channel_id=1, source_target_pairs={{0,2},{1,3},{2,0},{3,1},{4,6},{5,7},{6,4},{7,5},{8,10},{9,11},{10,... | collective-permute-start | bytes 1794056 | tf_op jit(solution)/shard_map/ppermute | solution.py:295
  30.9 15.9 %collective-permute-done.5.refs_1_ = bf16[2336,128]{1,0:T(8,128)(2,1)S(1)} collective-permute-done((bf16[2336,128]{1,0:T(8,128)(2,1)S(1)}, bf16[2336,128]{1,0:T(8,128)(2,1)S(1)}, u32[]{:S(2)}, u32[]{:S(2)}) %collective-permute-start.5) | collective-permute-done | bytes 598048 | tf_op jit(solution)/shard_map/ppermute | solution.py:292
  46.8 3.2 %gram.2 = (f32[36,256,128]{2,1,0:T(8,128)S(1)}, f32[128,128]{1,0:T(8,128)S(1)}) custom-call(bf16[2336,128]{1,0:T(8,128)(2,1)S(1)} %pad_maximum_fusion.1.refs_0_, bf16[2336,128]{1,0:T(8,128)(2,1)S(1)} %collective-permute-done.5.refs_1_), custom_call_target="tpu_custom_call" | custom-call | tf_op jit(solution)/shard_map/gram/pallas_call | solution.py:259
  50.0 17.1 %collective-permute-done.4.refs_1_ = bf16[2336,128]{1,0:T(8,128)(2,1)S(1)} collective-permute-done((bf16[2336,128]{1,0:T(8,128)(2,1)S(1)}, bf16[2336,128]{1,0:T(8,128)(2,1)S(1)}, u32[]{:S(2)}, u32[]{:S(2)}) %collective-permute-start.4) | collective-permute-done | bytes 598048 | tf_op jit(solution)/shard_map/ppermute | solution.py:292
  67.1 0.8 %collective-permute-done.3.refs_0_ = bf16[2336,128]{1,0:T(8,128)(2,1)S(1)} collective-permute-done((bf16[2336,128]{1,0:T(8,128)(2,1)S(1)}, bf16[2336,128]{1,0:T(8,128)(2,1)S(1)}, u32[]{:S(2)}, u32[]{:S(2)}) %collective-permute-start.3) | collective-permute-done | bytes 598048 | tf_op jit(solution)/shard_map/ppermute | solution.py:295
  67.9 6.5 %gram.3 = f32[36,256,128]{2,1,0:T(8,128)} custom-call(bf16[2336,128]{1,0:T(8,128)(2,1)S(1)} %collective-permute-done.3.refs_0_, bf16[2336,128]{1,0:T(8,128)(2,1)S(1)} %collective-permute-done.4.refs_1_, f32[36,256,128]{2,1,0:T(8,128)S(1)} %get-tuple-element.17.refs_2_, f32[128,128]{1,0:T(8,128)S(1)} %get-tuple-element.18.refs_3_), custom_call_target="tpu_custom_call" | custom-call | tf_op jit(solution)/shard_map/gram/pallas_call | solution.py:259
  (3 shorter events, 0.1 us)
Async XLA Ops:
  0.0 1.9 %copy-start.1 = (bf16[288,2048]{1,0:T(8,128)(2,1)S(1)}, bf16[288,2048]{1,0:T(8,128)(2,1)}, u32[]{:S(2)}) copy-start(bf16[288,2048]{1,0:T(8,128)(2,1)} %constant.6.clone.basis) | copy-start | bytes 3538948
  1.9 7.6 %copy-start.3 = (f32[31]{0:T(128)S(1)}, f32[31]{0:T(128)}, u32[]{:S(2)}) copy-start(f32[31]{0:T(128)} %taps.3) | copy-start | bytes 376
  2.7 14.6 %collective-permute-start = (bf16[288,256]{1,0:T(8,128)(2,1)S(1)}, bf16[288,256]{1,0:T(8,128)(2,1)S(1)}, u32[]{:S(2)}, u32[]{:S(2)}) collective-permute-start(bf16[288,256]{1,0:T(8,128)(2,1)S(1)} %get-tuple-element.12), channel_id=1, source_target_pairs={{0,4},{4,8},{8,12},{12,16},{16,20},{20,24},{24,28},{28,32},{32,36}... | collective-permute-start | bytes 442376 | tf_op jit(solution)/shard_map/ppermute | solution.py:275
  7.6 11.4 %collective-permute-start.1 = (bf16[288,256]{1,0:T(8,128)(2,1)S(1)}, bf16[288,256]{1,0:T(8,128)(2,1)S(1)}, u32[]{:S(2)}, u32[]{:S(2)}) collective-permute-start(bf16[288,256]{1,0:T(8,128)(2,1)S(1)} %get-tuple-element.13), channel_id=1, source_target_pairs={{4,0},{8,4},{12,8},{16,12},{20,16},{24,20},{28,24},{32,28},{36,32}... | collective-permute-start | bytes 442376 | tf_op jit(solution)/shard_map/ppermute | solution.py:276
  9.5 3.4 %copy-start = (bf16[16,128,2048]{2,1,0:T(8,128)(2,1)S(1)}, bf16[16,128,2048]{2,1,0:T(8,128)(2,1)}, u32[]{:S(2)}) copy-start(bf16[16,128,2048]{2,1,0:T(8,128)(2,1)} %raw.1) | copy-start | bytes 25165828
  12.9 6.1 %copy-start.2 = (s32[16,128]{1,0:T(8,128)S(1)}, s32[16,128]{1,0:T(8,128)}, u32[]{:S(2)}) copy-start(s32[16,128]{1,0:T(8,128)} %mask.1) | copy-start | bytes 24580
  22.1 2.1 %collective-permute-start.2 = (bf16[2336,128]{1,0:T(8,128)(2,1)S(1)}, bf16[2336,128]{1,0:T(8,128)(2,1)S(1)}, u32[]{:S(2)}, u32[]{:S(2)}) collective-permute-start(bf16[2336,128]{1,0:T(8,128)(2,1)S(1)} %get-tuple-element.15), channel_id=1, source_target_pairs={{0,1},{1,0},{2,3},{3,2},{4,5},{5,4},{6,7},{7,6},{8,9},{9,8},{10,11... | collective-permute-start | bytes 1794056 | tf_op jit(solution)/shard_map/ppermute | solution.py:282
  24.3 22.5 %collective-permute-start.5 = (bf16[2336,128]{1,0:T(8,128)(2,1)S(1)}, bf16[2336,128]{1,0:T(8,128)(2,1)S(1)}, u32[]{:S(2)}, u32[]{:S(2)}) collective-permute-start(bf16[2336,128]{1,0:T(8,128)(2,1)S(1)} %pad_maximum_fusion.1.refs_0_), channel_id=1, source_target_pairs={{4,0},{5,1},{6,2},{7,3},{8,4},{9,5},{10,6},{11,7},{12,8},{13,9},{1... | collective-permute-start | bytes 1794056 | tf_op jit(solution)/shard_map/ppermute | solution.py:292
  26.3 40.8 %collective-permute-start.4 = (bf16[2336,128]{1,0:T(8,128)(2,1)S(1)}, bf16[2336,128]{1,0:T(8,128)(2,1)S(1)}, u32[]{:S(2)}, u32[]{:S(2)}) collective-permute-start(bf16[2336,128]{1,0:T(8,128)(2,1)S(1)} %pad_maximum_fusion), channel_id=1, source_target_pairs={{6,0},{7,1},{4,2},{5,3},{10,4},{11,5},{8,6},{9,7},{14,8},{15,9},{1... | collective-permute-start | bytes 1794056 | tf_op jit(solution)/shard_map/ppermute | solution.py:292
  28.7 39.2 %collective-permute-start.3 = (bf16[2336,128]{1,0:T(8,128)(2,1)S(1)}, bf16[2336,128]{1,0:T(8,128)(2,1)S(1)}, u32[]{:S(2)}, u32[]{:S(2)}) collective-permute-start(bf16[2336,128]{1,0:T(8,128)(2,1)S(1)} %pad_maximum_fusion), channel_id=1, source_target_pairs={{0,2},{1,3},{2,0},{3,1},{4,6},{5,7},{6,4},{7,5},{8,10},{9,11},{10,... | collective-permute-start | bytes 1794056 | tf_op jit(solution)/shard_map/ppermute | solution.py:295

commit v4 on v3

--- a/solution.py
+++ b/solution.py
@@ -71,6 +71,7 @@
         out_specs=[WHOLE] * 2,
         out_shape=[out, out],
         compiler_params=pltpu.CompilerParams(vmem_limit_bytes=VMEM),
+        cost_estimate=pl.CostEstimate(flops=1, bytes_accessed=1, transcendentals=0),
         name="edge_spectra",
     )(raw[:, :EDGE], raw[:, channels - EDGE :], basis)
 
@@ -189,82 +190,103 @@
     )(me, taps, filtered, left, right, mask)
 
 
-def gram_kernel(segs, bins, last, *refs):
-    own, later = refs[:2]
-    if last:
-        before, before_count, out, cells, sems = refs[2:]
-    else:
-        cells, count_out = refs[2:]
-    channels = own.shape[1]
-    height = own.shape[0] // 2
-    share = cells.shape[0]
-    row = lax.broadcasted_iota(jnp.int32, (channels, channels), 0)
-    column = lax.broadcasted_iota(jnp.int32, (channels, channels), 1)
-    ahead = column > row
-    skew = (row + column + 1) % channels
-
-    def pieces(side, first, size):
-        rows = [side[pl.ds(base + first, size), :] for base in (0, height)]
-        return jnp.concatenate(rows, axis=0)
-
-    mine = pieces(own, height - segs, segs)
-    theirs = pieces(later, height - segs, segs)
-    count = jnp.where(ahead, dot(mine, mine, TN), dot(mine, theirs, TN))
-    if last:
-        scale = 1.0 / jnp.maximum(count + before_count[...], 1.0)
-    else:
-        count_out[...] = count
+def pieces(arrays, first, size):
+    height = arrays[0].shape[0] // 2
+    rows = [ref[pl.ds(base + first, size), :] for ref in arrays for base in (0, height)]
+    return jnp.concatenate(rows, axis=0)
+
+
+def own_kernel(segs, bins, near, far, rows, sums, count):
+    own = (near, far)
+    channels = near.shape[1]
+    height = near.shape[0] // 2
+    share = rows.shape[0]
+    flags = pieces(own, height - segs, segs)
+    count[...] = dot(flags, flags, TN)
 
     def group(step, carry):
         for at in range(bins):
             bin_at = step * bins + at
             first = pl.multiple_of(bin_at * (2 * segs), 2 * segs)
             mine = pieces(own, first, 2 * segs)
-            theirs = pieces(later, first, 2 * segs)
-            split = mine.astype(F32).reshape(mine.shape[0] // (2 * segs), 2, segs, channels)
-            turned = jnp.concatenate([-split[:, 1:], split[:, :1]], axis=1)
-            turned = turned.reshape(mine.shape).astype(BF16)
-            gram = dot(
-                jnp.concatenate([mine, turned], axis=1), jnp.concatenate([mine, theirs], axis=1), TN
-            )
+            split = mine.reshape(mine.shape[0] // (2 * segs), 2, segs, channels)
+            turned = jnp.concatenate([-split[:, 1:], split[:, :1]], axis=1).reshape(mine.shape)
+            both = jnp.concatenate([mine.T, turned.T], axis=0)
+            rows[bin_at] = both
+            sums[bin_at] = dot(both, mine)
+        return carry
+
+    lax.fori_loop(0, share // bins, group, 0)
+
+
+def own_gram(parts, segs, near, far):
+    channels = near.shape[1]
+    share = NF // parts
+    return pl.pallas_call(
+        functools.partial(own_kernel, segs, 12),
+        in_specs=[WHOLE] * 2,
+        out_specs=[WHOLE] * 3,
+        out_shape=[
+            jax.ShapeDtypeStruct((share, 2 * channels, 2 * parts * segs), BF16),
+            jax.ShapeDtypeStruct((share, 2 * channels, channels), F32),
+            jax.ShapeDtypeStruct((channels, channels), F32),
+        ],
+        compiler_params=pltpu.CompilerParams(vmem_limit_bytes=VMEM),
+        name="own_gram",
+    )(near, far)
+
+
+def gram_kernel(segs, bins, batch, later_far, later_near, near, far, rows, sums, own_count, out, cells, sems):
+    later = (later_near, later_far)
+    channels = near.shape[1]
+    height = near.shape[0] // 2
+    share = rows.shape[0]
+    row = lax.broadcasted_iota(jnp.int32, (channels, channels), 0)
+    column = lax.broadcasted_iota(jnp.int32, (channels, channels), 1)
+    ahead = column > row
+    skew = (row + column + 1) % channels
+    mine = pieces((near, far), height - segs, segs)
+    theirs = pieces(later, height - segs, segs)
+    count = jnp.where(ahead, own_count[...], dot(mine, theirs, TN))
+    scale = 1.0 / jnp.maximum(count, 1.0)
+
+    def group(step, carry):
+        for at in range(bins):
+            bin_at = step * bins + at
+            first = pl.multiple_of(bin_at * (2 * segs), 2 * segs)
+            gram = dot(rows[bin_at], pieces(later, first, 2 * segs))
             for part in range(2):
-                rows = gram[part * channels : (part + 1) * channels]
-                band = jnp.where(ahead, rows[:, :channels], rows[:, channels:])
-                if last:
-                    band = (band + before[bin_at, part * channels : (part + 1) * channels, :]) * scale
-                    band = jnp.take_along_axis(band, skew, axis=1, mode="promise_in_bounds")
-                    cells[bin_at, pl.ds(part, channels, stride=2), :] = band
-                else:
-                    cells[bin_at, part * channels : (part + 1) * channels, :] = band
-        if last:
-            at = pl.ds(step * bins, bins)
-            pltpu.make_async_copy(cells.at[at], out.at[at], sems.at[step]).start()
+                half = slice(part * channels, (part + 1) * channels)
+                band = jnp.where(ahead, sums[bin_at, half, :], gram[half]) * scale
+                band = jnp.take_along_axis(band, skew, axis=1, mode="promise_in_bounds")
+                cells[bin_at, pl.ds(part, channels, stride=2), :] = band
+            if at % batch == batch - 1:
+                done = step * (bins // batch) + at // batch
+                there = pl.ds(done * batch, batch)
+                pltpu.make_async_copy(cells.at[there], out.at[there], sems.at[done]).start()
         return carry
 
     lax.fori_loop(0, share // bins, group, 0)
-    if last:
-        for step in range(share // bins):
-            at = pl.ds(step * bins, bins)
-            pltpu.make_async_copy(cells.at[at], out.at[at], sems.at[step]).wait()
-
-
-def stacked(parts, segs, own, later, before=()):
-    channels = own.shape[1]
+    for done in range(share // batch):
+        there = pl.ds(done * batch, batch)
+        pltpu.make_async_copy(cells.at[there], out.at[there], sems.at[done]).wait()
+
+
+def stacked(parts, segs, near, later_near, far, later_far):
+    channels = near.shape[1]
     share = NF // parts
-    bins = 4
-    last = bool(before)
-    sums = jax.ShapeDtypeStruct((share, 2 * channels, LAGS), F32)
-    count = jax.ShapeDtypeStruct((channels, channels), F32)
-    scratch = [pltpu.VMEM(sums.shape, F32), pltpu.SemaphoreType.DMA((share // bins,))]
-    return pl.pallas_call(
-        functools.partial(gram_kernel, segs, bins, last),
-        in_specs=[WHOLE] * (2 + len(before)),
-        out_specs=ANYWHERE if last else [WHOLE] * 2,
-        out_shape=sums if last else [sums, count],
-        scratch_shapes=scratch if last else [],
+    batch = 4
+    shape = (share, 2 * channels, LAGS)
+    rows, sums, count = own_gram(parts, segs, near, far)
+    return pl.pallas_call(
+        functools.partial(gram_kernel, segs, 12, batch),
+        in_specs=[WHOLE] * 7,
+        out_specs=ANYWHERE,
+        out_shape=jax.ShapeDtypeStruct(shape, F32),
+        scratch_shapes=[pltpu.VMEM(shape, F32), pltpu.SemaphoreType.DMA((share // batch,))],
         compiler_params=pltpu.CompilerParams(vmem_limit_bytes=VMEM),
         name="gram",
-    )(own, later, *before)
+    )(later_far, later_near, near, far, rows, sums, count)
 
 
 def on_device(fibers, parts, raw_strain, fir_taps, good_mask):
@@ -294,8 +316,7 @@
     later_far = following(far, 2)
     own_far = lax.ppermute(far, "seg", [(j, j ^ 2) for j in range(parts)])
     later_near = following(near, 0)
-    before = stacked(parts, segs, near, later_near)
-    out = stacked(parts, segs, own_far, later_far, before)
+    out = stacked(parts, segs, near, later_near, own_far, later_far)
     return out.reshape(out.shape[0], channels, 2, LAGS)
 
 

time: 75.4 us -> 71.9 us (0.954); the launches traced: 74.4 us -> 71.7 us
  Pallas kernels: 18 us -> 14.7 us
    ppermute x1, waiting for transfers between devices: 0.84 us -> 30 us  [on_device(): own_far = lax.ppermute(far, 'seg', [(j, j ^ 2) for j in range(parts)])]
    ppermute x2, waiting for transfers between devices: 33 us -> 4.48 us  [following(): return lax.ppermute(cells, GRID, pairs)]
    pallas_call x2, Pallas kernels: 9.65 us -> 6.34 us  [the longest x1 4.96 us: stacked(): pl.pallas_call(functools.partial(gram_kernel, segs, 12, batch), in_specs=...]
  transfers between devices with their start and end apart: 6 -> 6, of which waited for: 5 -> 4; matrix products, arithmetic and copies ran while one was open for 0% -> 0% of each run, Pallas kernels for 10% -> 8%
where the time goes in v4:
time: 71.9 us; the launch traced here: 71.7 us
  waiting for transfers between devices  38.1 us (53%)
  Pallas kernels  14.7 us (20%)
  starting transfers between devices  13.4 us (19%)
  local copies, waits for them, and re-layouts  5.32 us (7%)
    ppermute x1, waiting for transfers between devices, on_device(): own_far = lax.ppermute(far, 'seg', [(j, j ^ 2) for j in range(parts)])  30 us
    pallas_call x1, Pallas kernels, stacked(): pl.pallas_call(functools.partial(gram_kernel, segs, 12, batch), in_specs=...  4.96 us
    ppermute x1, starting transfers between devices, on_device(): left = lax.ppermute(tail, 'fiber', [(i, i + 1) for i in range(fibers - 1)])  4.84 us
    ppermute x2, waiting for transfers between devices, following(): return lax.ppermute(cells, GRID, pairs)  4.48 us
    pallas_call x1, Pallas kernels, main_spectra(): pl.pallas_call(functools.partial(main_kernel, 4, taps.shape[0]), in_specs...  4.41 us
    ppermute x2, starting transfers between devices, following(): return lax.ppermute(cells, GRID, pairs)  3.83 us
    unnamed x8, local copies, waits for them, and re-layouts  3.4 us
    pallas_call x1, Pallas kernels, whitened_parts(): pl.pallas_call(functools.partial(whiten_kernel, parts, taps.shape[0]), in...  3.1 us
  transfers between devices with their start and end apart: 6, of which 4 were waited for; matrix products, arithmetic and copies ran while one was open for 0% of the time, Pallas kernels for 8%

profile of v4, /device:TPU:110, one launch (start us, length us, event | category | flops | bytes accessed | tf_op | source)
XLA Modules:
  0.0 71.7 jit_solution(7589127148092871634)
XLA Ops:
  0.0 0.0 copy-start.1
  0.0 1.9 %fusion = (bf16[16,16,2048]{2,1,0:T(8,128)(2,1)S(1)}, bf16[16,16,2048]{2,1,0:T(8,128)(2,1)S(1)}) fusion(bf16[16,128,2048]{2,1,0:T(8,128)(2,1)} %raw.1), kind=kLoop, calls=%fused_computation.2 | loop fusion | bytes 4194304 | tf_op jit(solution)/shard_map/slice | solution.py:76
  1.9 0.0 copy-done.1
  1.9 0.0 copy-start.3
  1.9 0.8 %edge_spectra.1 = (bf16[288,256]{1,0:T(8,128)(2,1)S(1)}, bf16[288,256]{1,0:T(8,128)(2,1)S(1)}) custom-call(bf16[16,16,2048]{2,1,0:T(8,128)(2,1)S(1)} %get-tuple-element.22.first, bf16[16,16,2048]{2,1,0:T(8,128)(2,1)S(1)} %get-tuple-element.21.last, bf16[288,2048]{1,0:T(8,128)(2,1)S(1)} %copy-done.1), custom_call_target="tpu_custom_call" | custom-call | flops 1 | bytes 1 | tf_op jit(solution)/shard_map/edge_spectra/pallas_call | solution.py:68
  2.7 4.8 %collective-permute-start = (bf16[288,256]{1,0:T(8,128)(2,1)S(1)}, bf16[288,256]{1,0:T(8,128)(2,1)S(1)}, u32[]{:S(2)}, u32[]{:S(2)}) collective-permute-start(bf16[288,256]{1,0:T(8,128)(2,1)S(1)} %get-tuple-element.13), channel_id=1, source_target_pairs={{0,4},{4,8},{8,12},{12,16},{16,20},{20,24},{24,28},{28,32},{32,36}... | collective-permute-start | bytes 442376 | tf_op jit(solution)/shard_map/ppermute | solution.py:297
  7.6 1.9 %collective-permute-start.1 = (bf16[288,256]{1,0:T(8,128)(2,1)S(1)}, bf16[288,256]{1,0:T(8,128)(2,1)S(1)}, u32[]{:S(2)}, u32[]{:S(2)}) collective-permute-start(bf16[288,256]{1,0:T(8,128)(2,1)S(1)} %get-tuple-element.14), channel_id=1, source_target_pairs={{4,0},{8,4},{12,8},{16,12},{20,16},{24,20},{28,24},{32,28},{36,32}... | collective-permute-start | bytes 442376 | tf_op jit(solution)/shard_map/ppermute | solution.py:298
  9.5 0.0 copy-done.3
  9.5 0.0 copy-start
  9.5 3.4 %copy-done = bf16[16,128,2048]{2,1,0:T(8,128)(2,1)S(1)} copy-done((bf16[16,128,2048]{2,1,0:T(8,128)(2,1)S(1)}, bf16[16,128,2048]{2,1,0:T(8,128)(2,1)}, u32[]{:S(2)}) %copy-start) | copy-done | bytes 8388632
  12.9 0.0 copy-start.2
  12.9 4.4 %main_spectra.1.filtered = f32[4608,128]{1,0:T(8,128)S(1)} custom-call(bf16[16,128,2048]{2,1,0:T(8,128)(2,1)S(1)} %copy-done, bf16[288,2048]{1,0:T(8,128)(2,1)S(1)} %copy-done.1, f32[31]{0:T(128)S(1)} %copy-done.3), custom_call_target="tpu_custom_call" | custom-call | tf_op jit(solution)/shard_map/main_spectra/pallas_call | solution.py:105
  17.3 0.0 collective-permute-done.left
  17.3 1.7 %collective-permute-done.1.right = bf16[288,256]{1,0:T(8,128)(2,1)S(1)} collective-permute-done((bf16[288,256]{1,0:T(8,128)(2,1)S(1)}, bf16[288,256]{1,0:T(8,128)(2,1)S(1)}, u32[]{:S(2)}, u32[]{:S(2)}) %collective-permute-start.1) | collective-permute-done | bytes 147488 | tf_op jit(solution)/shard_map/ppermute | solution.py:298
  19.0 0.0 copy-done.2
  19.0 3.1 %whiten.1 = (bf16[1168,128]{1,0:T(8,128)(2,1)S(1)}, bf16[1168,128]{1,0:T(8,128)(2,1)S(1)}, bf16[2336,128]{1,0:T(8,128)(2,1)S(1)}) custom-call(s32[1]{0:T(128)} %bitcast.me, f32[31]{0:T(128)S(1)} %copy-done.3, f32[4608,128]{1,0:T(8,128)S(1)} %main_spectra.1.filtered, bf16[288,256]{1,0:T(8,128)(2,1)S(1)} %collective-permute-done.left, ...), custom_call_target="tpu_custom_call" | custom-call | tf_op jit(solution)/shard_map/whiten/pallas_call | solution.py:179
  22.1 0.1 collective-permute-start.2
  22.2 2.0 %collective-permute-done.2 = bf16[2336,128]{1,0:T(8,128)(2,1)S(1)} collective-permute-done((bf16[2336,128]{1,0:T(8,128)(2,1)S(1)}, bf16[2336,128]{1,0:T(8,128)(2,1)S(1)}, u32[]{:S(2)}, u32[]{:S(2)}) %collective-permute-start.2) | collective-permute-done | bytes 598048 | tf_op jit(solution)/shard_map/ppermute | solution.py:304
  24.3 2.7 %collective-permute-start.5 = (bf16[2336,128]{1,0:T(8,128)(2,1)S(1)}, bf16[2336,128]{1,0:T(8,128)(2,1)S(1)}, u32[]{:S(2)}, u32[]{:S(2)}) collective-permute-start(bf16[2336,128]{1,0:T(8,128)(2,1)S(1)} %pad_maximum_fusion), channel_id=1, source_target_pairs={{0,2},{1,3},{2,0},{3,1},{4,6},{5,7},{6,4},{7,5},{8,10},{9,11},{10,... | collective-permute-start | bytes 1794056 | tf_op jit(solution)/shard_map/ppermute | solution.py:317
  27.0 1.9 %collective-permute-start.3 = (bf16[2336,128]{1,0:T(8,128)(2,1)S(1)}, bf16[2336,128]{1,0:T(8,128)(2,1)S(1)}, u32[]{:S(2)}, u32[]{:S(2)}) collective-permute-start(bf16[2336,128]{1,0:T(8,128)(2,1)S(1)} %pad_maximum_fusion), channel_id=1, source_target_pairs={{6,0},{7,1},{4,2},{5,3},{10,4},{11,5},{8,6},{9,7},{14,8},{15,9},{1... | collective-permute-start | bytes 1794056 | tf_op jit(solution)/shard_map/ppermute | solution.py:314
  28.9 1.9 %collective-permute-start.4 = (bf16[2336,128]{1,0:T(8,128)(2,1)S(1)}, bf16[2336,128]{1,0:T(8,128)(2,1)S(1)}, u32[]{:S(2)}, u32[]{:S(2)}) collective-permute-start(bf16[2336,128]{1,0:T(8,128)(2,1)S(1)} %pad_maximum_fusion.1.near), channel_id=1, source_target_pairs={{4,0},{5,1},{6,2},{7,3},{8,4},{9,5},{10,6},{11,7},{12,8},{13,9},{1... | collective-permute-start | bytes 1794056 | tf_op jit(solution)/shard_map/ppermute | solution.py:314
  30.9 30.0 %collective-permute-done.5.far = bf16[2336,128]{1,0:T(8,128)(2,1)S(1)} collective-permute-done((bf16[2336,128]{1,0:T(8,128)(2,1)S(1)}, bf16[2336,128]{1,0:T(8,128)(2,1)S(1)}, u32[]{:S(2)}, u32[]{:S(2)}) %collective-permute-start.5) | collective-permute-done | bytes 598048 | tf_op jit(solution)/shard_map/ppermute | solution.py:317
  60.9 1.4 %own_gram.1 = (bf16[36,256,128]{2,1,0:T(8,128)(2,1)S(1)}, f32[36,256,128]{2,1,0:T(8,128)S(1)}, f32[128,128]{1,0:T(8,128)S(1)}) custom-call(bf16[2336,128]{1,0:T(8,128)(2,1)S(1)} %pad_maximum_fusion.1.near, bf16[2336,128]{1,0:T(8,128)(2,1)S(1)} %collective-permute-done.5.far), custom_call_target="tpu_custom_call" | custom-call | tf_op jit(solution)/shard_map/own_gram/pallas_call | solution.py:225
  62.2 0.0 collective-permute-done.3.later_far
  62.2 4.5 %collective-permute-done.4.later_near = bf16[2336,128]{1,0:T(8,128)(2,1)S(1)} collective-permute-done((bf16[2336,128]{1,0:T(8,128)(2,1)S(1)}, bf16[2336,128]{1,0:T(8,128)(2,1)S(1)}, u32[]{:S(2)}, u32[]{:S(2)}) %collective-permute-start.4) | collective-permute-done | bytes 598048 | tf_op jit(solution)/shard_map/ppermute | solution.py:314
  66.7 5.0 %gram.1 = f32[36,256,128]{2,1,0:T(8,128)} custom-call(bf16[2336,128]{1,0:T(8,128)(2,1)S(1)} %collective-permute-done.3.later_far, bf16[2336,128]{1,0:T(8,128)(2,1)S(1)} %collective-permute-done.4.later_near, bf16[2336,128]{1,0:T(8,128)(2,1)S(1)} %pad_maximum_fusion.1.near, bf16[2336,128]{1,0:T(8,128)(2,1)S(1)} %collective-permute-done.5.far, ...), custom_call_target="tpu_custom_call" | custom-call | tf_op jit(solution)/shard_map/gram/pallas_call | solution.py:281
  (3 shorter events, 0.1 us)
Async XLA Ops:
  0.0 1.9 %copy-start.1 = (bf16[288,2048]{1,0:T(8,128)(2,1)S(1)}, bf16[288,2048]{1,0:T(8,128)(2,1)}, u32[]{:S(2)}) copy-start(bf16[288,2048]{1,0:T(8,128)(2,1)} %constant.6.clone.basis) | copy-start | bytes 3538948
  1.9 7.6 %copy-start.3 = (f32[31]{0:T(128)S(1)}, f32[31]{0:T(128)}, u32[]{:S(2)}) copy-start(f32[31]{0:T(128)} %taps.3) | copy-start | bytes 376
  2.7 14.6 %collective-permute-start = (bf16[288,256]{1,0:T(8,128)(2,1)S(1)}, bf16[288,256]{1,0:T(8,128)(2,1)S(1)}, u32[]{:S(2)}, u32[]{:S(2)}) collective-permute-start(bf16[288,256]{1,0:T(8,128)(2,1)S(1)} %get-tuple-element.13), channel_id=1, source_target_pairs={{0,4},{4,8},{8,12},{12,16},{16,20},{20,24},{24,28},{28,32},{32,36}... | collective-permute-start | bytes 442376 | tf_op jit(solution)/shard_map/ppermute | solution.py:297
  7.6 11.4 %collective-permute-start.1 = (bf16[288,256]{1,0:T(8,128)(2,1)S(1)}, bf16[288,256]{1,0:T(8,128)(2,1)S(1)}, u32[]{:S(2)}, u32[]{:S(2)}) collective-permute-start(bf16[288,256]{1,0:T(8,128)(2,1)S(1)} %get-tuple-element.14), channel_id=1, source_target_pairs={{4,0},{8,4},{12,8},{16,12},{20,16},{24,20},{28,24},{32,28},{36,32}... | collective-permute-start | bytes 442376 | tf_op jit(solution)/shard_map/ppermute | solution.py:298
  9.5 3.4 %copy-start = (bf16[16,128,2048]{2,1,0:T(8,128)(2,1)S(1)}, bf16[16,128,2048]{2,1,0:T(8,128)(2,1)}, u32[]{:S(2)}) copy-start(bf16[16,128,2048]{2,1,0:T(8,128)(2,1)} %raw.1) | copy-start | bytes 25165828
  12.9 6.1 %copy-start.2 = (s32[16,128]{1,0:T(8,128)S(1)}, s32[16,128]{1,0:T(8,128)}, u32[]{:S(2)}) copy-start(s32[16,128]{1,0:T(8,128)} %mask.1) | copy-start | bytes 24580
  22.1 2.1 %collective-permute-start.2 = (bf16[2336,128]{1,0:T(8,128)(2,1)S(1)}, bf16[2336,128]{1,0:T(8,128)(2,1)S(1)}, u32[]{:S(2)}, u32[]{:S(2)}) collective-permute-start(bf16[2336,128]{1,0:T(8,128)(2,1)S(1)} %get-tuple-element.16), channel_id=1, source_target_pairs={{0,1},{1,0},{2,3},{3,2},{4,5},{5,4},{6,7},{7,6},{8,9},{9,8},{10,11... | collective-permute-start | bytes 1794056 | tf_op jit(solution)/shard_map/ppermute | solution.py:304
  24.3 36.6 %collective-permute-start.5 = (bf16[2336,128]{1,0:T(8,128)(2,1)S(1)}, bf16[2336,128]{1,0:T(8,128)(2,1)S(1)}, u32[]{:S(2)}, u32[]{:S(2)}) collective-permute-start(bf16[2336,128]{1,0:T(8,128)(2,1)S(1)} %pad_maximum_fusion), channel_id=1, source_target_pairs={{0,2},{1,3},{2,0},{3,1},{4,6},{5,7},{6,4},{7,5},{8,10},{9,11},{10,... | collective-permute-start | bytes 1794056 | tf_op jit(solution)/shard_map/ppermute | solution.py:317
  27.0 35.3 %collective-permute-start.3 = (bf16[2336,128]{1,0:T(8,128)(2,1)S(1)}, bf16[2336,128]{1,0:T(8,128)(2,1)S(1)}, u32[]{:S(2)}, u32[]{:S(2)}) collective-permute-start(bf16[2336,128]{1,0:T(8,128)(2,1)S(1)} %pad_maximum_fusion), channel_id=1, source_target_pairs={{6,0},{7,1},{4,2},{5,3},{10,4},{11,5},{8,6},{9,7},{14,8},{15,9},{1... | collective-permute-start | bytes 1794056 | tf_op jit(solution)/shard_map/ppermute | solution.py:314
  28.9 37.8 %collective-permute-start.4 = (bf16[2336,128]{1,0:T(8,128)(2,1)S(1)}, bf16[2336,128]{1,0:T(8,128)(2,1)S(1)}, u32[]{:S(2)}, u32[]{:S(2)}) collective-permute-start(bf16[2336,128]{1,0:T(8,128)(2,1)S(1)} %pad_maximum_fusion.1.near), channel_id=1, source_target_pairs={{4,0},{5,1},{6,2},{7,3},{8,4},{9,5},{10,6},{11,7},{12,8},{13,9},{1... | collective-permute-start | bytes 1794056 | tf_op jit(solution)/shard_map/ppermute | solution.py:314

commit v5 on v4

--- a/solution.py
+++ b/solution.py
@@ -20,6 +20,7 @@
 water_share = 0.1
 
 GRID = ("fiber", "seg")
+AHEAD = 16
 VMEM = 24 * 1024 * 1024
 STREAM = 50 * 1024 * 1024
 F32 = jnp.float32
@@ -236,57 +237,100 @@
     )(near, far)
 
 
-def gram_kernel(segs, bins, batch, later_far, later_near, near, far, rows, sums, own_count, out, cells, sems):
-    later = (later_near, later_far)
-    channels = near.shape[1]
-    height = near.shape[0] // 2
-    share = rows.shape[0]
+def gram_kernel(segs, batch, first_half, *refs):
+    if first_half:
+        later_near, later_far, near, far, own_count, rows, sums, out, scale, cells, sems = refs
+        begin = 0
+    else:
+        later_near, later_far, scale, rows, sums, _, out, cells, sems = refs
+        begin = out.shape[0] - cells.shape[0]
+    channels = later_near.shape[1]
+    count = cells.shape[0]
+    bins = count
     row = lax.broadcasted_iota(jnp.int32, (channels, channels), 0)
     column = lax.broadcasted_iota(jnp.int32, (channels, channels), 1)
     ahead = column > row
     skew = (row + column + 1) % channels
-    mine = pieces((near, far), height - segs, segs)
-    theirs = pieces(later, height - segs, segs)
-    count = jnp.where(ahead, own_count[...], dot(mine, theirs, TN))
-    scale = 1.0 / jnp.maximum(count, 1.0)
+    near_height = count * 2 * segs
+    far_height = later_far.shape[0] // 2
+
+    def group_rows(ref, height, first, size):
+        return [ref[pl.ds(base + first, size), :] for base in (0, height)]
+
+    if first_half:
+        height = near.shape[0] // 2
+        mine = pieces((near, far), height - segs, segs)
+        theirs = jnp.concatenate(
+            [later_near[2 * near_height :, :]]
+            + group_rows(later_far, far_height, far_height - segs, segs),
+            axis=0,
+        )
+        pairs = jnp.where(ahead, own_count[...], dot(mine, theirs, TN))
+        scale[...] = 1.0 / jnp.maximum(pairs, 1.0)
 
     def group(step, carry):
         for at in range(bins):
-            bin_at = step * bins + at
-            first = pl.multiple_of(bin_at * (2 * segs), 2 * segs)
-            gram = dot(rows[bin_at], pieces(later, first, 2 * segs))
+            here = step * bins + at
+            first = pl.multiple_of(here * (2 * segs), 2 * segs)
+            theirs = jnp.concatenate(
+                group_rows(later_near, near_height, first, 2 * segs)
+                + group_rows(later_far, far_height, first + begin * 2 * segs, 2 * segs),
+                axis=0,
+            )
+            gram = dot(rows[begin + here], theirs)
             for part in range(2):
                 half = slice(part * channels, (part + 1) * channels)
-                band = jnp.where(ahead, sums[bin_at, half, :], gram[half]) * scale
+                band = jnp.where(ahead, sums[begin + here, half, :], gram[half]) * scale[...]
                 band = jnp.take_along_axis(band, skew, axis=1, mode="promise_in_bounds")
-                cells[bin_at, pl.ds(part, channels, stride=2), :] = band
+                cells[here, pl.ds(part, channels, stride=2), :] = band
             if at % batch == batch - 1:
                 done = step * (bins // batch) + at // batch
-                there = pl.ds(done * batch, batch)
-                pltpu.make_async_copy(cells.at[there], out.at[there], sems.at[done]).start()
+                pltpu.make_async_copy(
+                    cells.at[pl.ds(done * batch, batch)],
+                    out.at[pl.ds(begin + done * batch, batch)],
+                    sems.at[done],
+                ).start()
         return carry
 
-    lax.fori_loop(0, share // bins, group, 0)
-    for done in range(share // batch):
-        there = pl.ds(done * batch, batch)
-        pltpu.make_async_copy(cells.at[there], out.at[there], sems.at[done]).wait()
+    lax.fori_loop(0, count // bins, group, 0)
+    for done in range(count // batch):
+        pltpu.make_async_copy(
+            cells.at[pl.ds(done * batch, batch)],
+            out.at[pl.ds(begin + done * batch, batch)],
+            sems.at[done],
+        ).wait()
 
 
 def stacked(parts, segs, near, later_near, far, later_far):
     channels = near.shape[1]
     share = NF // parts
     batch = 4
-    shape = (share, 2 * channels, LAGS)
     rows, sums, count = own_gram(parts, segs, near, far)
-    return pl.pallas_call(
-        functools.partial(gram_kernel, segs, 12, batch),
+    out = jax.ShapeDtypeStruct((share, 2 * channels, LAGS), F32)
+    options = lambda bins: dict(
+        scratch_shapes=[
+            pltpu.VMEM((bins, 2 * channels, LAGS), F32),
+            pltpu.SemaphoreType.DMA((bins // batch,)),
+        ],
+        compiler_params=pltpu.CompilerParams(vmem_limit_bytes=VMEM),
+    )
+    out, scale = pl.pallas_call(
+        functools.partial(gram_kernel, segs, batch, True),
         in_specs=[WHOLE] * 7,
+        out_specs=[ANYWHERE, WHOLE],
+        out_shape=[out, jax.ShapeDtypeStruct((channels, channels), F32)],
+        name="gram",
+        **options(AHEAD),
+    )(later_near[0], later_far, near, far, count, rows, sums)
+    return pl.pallas_call(
+        functools.partial(gram_kernel, segs, batch, False),
+        in_specs=[WHOLE] * 5 + [ANYWHERE],
         out_specs=ANYWHERE,
-        out_shape=jax.ShapeDtypeStruct(shape, F32),
-        scratch_shapes=[pltpu.VMEM(shape, F32), pltpu.SemaphoreType.DMA((share // batch,))],
-        compiler_params=pltpu.CompilerParams(vmem_limit_bytes=VMEM),
-        name="gram",
-    )(later_far, later_near, near, far, rows, sums, count)
+        out_shape=jax.ShapeDtypeStruct(out.shape, F32),
+        input_output_aliases={5: 0},
+        name="gram_last",
+        **options(share - AHEAD),
+    )(later_near[1], later_far, scale, rows, sums, out)
 
 
 def on_device(fibers, parts, raw_strain, fir_taps, good_mask):
@@ -315,7 +359,13 @@
 
     later_far = following(far, 2)
     own_far = lax.ppermute(far, "seg", [(j, j ^ 2) for j in range(parts)])
-    later_near = following(near, 0)
+    middle = AHEAD * 2 * segs
+    cut = lambda begin, stop: [near[begin:stop], near[rows + begin : rows + stop]]
+    flags = cut(rows - segs, rows)
+    later_near = [
+        following(jnp.concatenate(cells, axis=0), 0)
+        for cells in (cut(0, middle) + flags, cut(middle, rows - segs))
+    ]
     out = stacked(parts, segs, near, later_near, own_far, later_far)
     return out.reshape(out.shape[0], channels, 2, LAGS)
 

time: 71.9 us -> 69.8 us (0.971)
  waiting for transfers between devices: 38.1 us -> 31.7 us
  starting transfers between devices: 13.4 us -> 17.1 us
    ppermute x1, waiting for transfers between devices: 30 us -> 26.2 us  [on_device(): own_far = lax.ppermute(far, 'seg', [(j, j ^ 2) for j in range(parts)])]
    ppermute x2 -> x3, starting transfers between devices: 3.83 us -> 7.54 us  [following(): return lax.ppermute(cells, GRID, pairs)]
    ppermute x2 -> x3, waiting for transfers between devices: 4.48 us -> 1.93 us  [following(): return lax.ppermute(cells, GRID, pairs)]
    pallas_call x1 -> x2, Pallas kernels: 4.96 us -> 5.4 us  [the longest x1 2.86 us: stacked(): pl.pallas_call(functools.partial(gram_kernel, segs, batch, False), in_spe...]
  transfers between devices with their start and end apart: 6 -> 7, of which waited for: 4 -> 4; matrix products, arithmetic and copies ran while one was open for 0% -> 0% of each run, Pallas kernels for 8% -> 12%
where the time goes in v5:
time: 69.8 us; the launch traced here: 69.6 us
  waiting for transfers between devices  31.7 us (45%)
  starting transfers between devices  17.1 us (24%)
  Pallas kernels  15.1 us (22%)
  local copies, waits for them, and re-layouts  5.36 us (8%)
    ppermute x1, waiting for transfers between devices, on_device(): own_far = lax.ppermute(far, 'seg', [(j, j ^ 2) for j in range(parts)])  26.2 us
    ppermute x3, starting transfers between devices, following(): return lax.ppermute(cells, GRID, pairs)  7.54 us
    ppermute x1, starting transfers between devices, on_device(): left = lax.ppermute(tail, 'fiber', [(i, i + 1) for i in range(fibers - 1)])  4.84 us
    pallas_call x1, Pallas kernels, main_spectra(): pl.pallas_call(functools.partial(main_kernel, 4, taps.shape[0]), in_specs...  4.41 us
    unnamed x8, local copies, waits for them, and re-layouts  3.39 us
    pallas_call x1, Pallas kernels, whitened_parts(): pl.pallas_call(functools.partial(whiten_kernel, parts, taps.shape[0]), in...  3.1 us
    pallas_call x1, Pallas kernels, stacked(): pl.pallas_call(functools.partial(gram_kernel, segs, batch, False), in_spe...  2.86 us
    ppermute x1, starting transfers between devices, on_device(): own_far = lax.ppermute(far, 'seg', [(j, j ^ 2) for j in range(parts)])  2.68 us
  transfers between devices with their start and end apart: 7, of which 4 were waited for; matrix products, arithmetic and copies ran while one was open for 0% of the time, Pallas kernels for 12%

profile of v5, /device:TPU:110, one launch (start us, length us, event | category | flops | bytes accessed | tf_op | source)
XLA Modules:
  0.0 69.6 jit_solution(4323447468876471504)
XLA Ops:
  0.0 0.0 copy-start.1
  0.0 1.9 %fusion = (bf16[16,16,2048]{2,1,0:T(8,128)(2,1)S(1)}, bf16[16,16,2048]{2,1,0:T(8,128)(2,1)S(1)}) fusion(bf16[16,128,2048]{2,1,0:T(8,128)(2,1)} %raw.1), kind=kLoop, calls=%fused_computation.4 | loop fusion | bytes 4194304 | tf_op jit(solution)/shard_map/slice | solution.py:77
  1.9 0.0 copy-start.3
  1.9 0.0 copy-done.1
  1.9 0.8 %edge_spectra.1 = (bf16[288,256]{1,0:T(8,128)(2,1)S(1)}, bf16[288,256]{1,0:T(8,128)(2,1)S(1)}) custom-call(bf16[16,16,2048]{2,1,0:T(8,128)(2,1)S(1)} %get-tuple-element.26.first, bf16[16,16,2048]{2,1,0:T(8,128)(2,1)S(1)} %get-tuple-element.25.last, bf16[288,2048]{1,0:T(8,128)(2,1)S(1)} %copy-done.1), custom_call_target="tpu_custom_call" | custom-call | flops 1 | bytes 1 | tf_op jit(solution)/shard_map/edge_spectra/pallas_call | solution.py:69
  2.7 4.8 %collective-permute-start = (bf16[288,256]{1,0:T(8,128)(2,1)S(1)}, bf16[288,256]{1,0:T(8,128)(2,1)S(1)}, u32[]{:S(2)}, u32[]{:S(2)}) collective-permute-start(bf16[288,256]{1,0:T(8,128)(2,1)S(1)} %get-tuple-element.15), channel_id=1, source_target_pairs={{0,4},{4,8},{8,12},{12,16},{16,20},{20,24},{24,28},{28,32},{32,36}... | collective-permute-start | bytes 442376 | tf_op jit(solution)/shard_map/ppermute | solution.py:341
  7.6 1.9 %collective-permute-start.1 = (bf16[288,256]{1,0:T(8,128)(2,1)S(1)}, bf16[288,256]{1,0:T(8,128)(2,1)S(1)}, u32[]{:S(2)}, u32[]{:S(2)}) collective-permute-start(bf16[288,256]{1,0:T(8,128)(2,1)S(1)} %get-tuple-element.16), channel_id=1, source_target_pairs={{4,0},{8,4},{12,8},{16,12},{20,16},{24,20},{28,24},{32,28},{36,32}... | collective-permute-start | bytes 442376 | tf_op jit(solution)/shard_map/ppermute | solution.py:342
  9.5 0.0 copy-done.3
  9.5 0.0 copy-start
  9.5 3.4 %copy-done = bf16[16,128,2048]{2,1,0:T(8,128)(2,1)S(1)} copy-done((bf16[16,128,2048]{2,1,0:T(8,128)(2,1)S(1)}, bf16[16,128,2048]{2,1,0:T(8,128)(2,1)}, u32[]{:S(2)}) %copy-start) | copy-done | bytes 8388632
  12.9 0.0 copy-start.2
  12.9 4.4 %main_spectra.1.filtered = f32[4608,128]{1,0:T(8,128)S(1)} custom-call(bf16[16,128,2048]{2,1,0:T(8,128)(2,1)S(1)} %copy-done, bf16[288,2048]{1,0:T(8,128)(2,1)S(1)} %copy-done.1, f32[31]{0:T(128)S(1)} %copy-done.3), custom_call_target="tpu_custom_call" | custom-call | tf_op jit(solution)/shard_map/main_spectra/pallas_call | solution.py:106
  17.3 0.0 collective-permute-done.left
  17.3 1.7 %collective-permute-done.1.right = bf16[288,256]{1,0:T(8,128)(2,1)S(1)} collective-permute-done((bf16[288,256]{1,0:T(8,128)(2,1)S(1)}, bf16[288,256]{1,0:T(8,128)(2,1)S(1)}, u32[]{:S(2)}, u32[]{:S(2)}) %collective-permute-start.1) | collective-permute-done | bytes 147488 | tf_op jit(solution)/shard_map/ppermute | solution.py:342
  19.0 0.0 copy-done.2
  19.0 3.1 %whiten.1 = (bf16[1168,128]{1,0:T(8,128)(2,1)S(1)}, bf16[1168,128]{1,0:T(8,128)(2,1)S(1)}, bf16[2336,128]{1,0:T(8,128)(2,1)S(1)}) custom-call(s32[1]{0:T(128)} %bitcast.me, f32[31]{0:T(128)S(1)} %copy-done.3, f32[4608,128]{1,0:T(8,128)S(1)} %main_spectra.1.filtered, bf16[288,256]{1,0:T(8,128)(2,1)S(1)} %collective-permute-done.left, ...), custom_call_target="tpu_custom_call" | custom-call | tf_op jit(solution)/shard_map/whiten/pallas_call | solution.py:180
  22.1 0.1 collective-permute-start.2
  22.2 2.0 %collective-permute-done.2 = bf16[2336,128]{1,0:T(8,128)(2,1)S(1)} collective-permute-done((bf16[2336,128]{1,0:T(8,128)(2,1)S(1)}, bf16[2336,128]{1,0:T(8,128)(2,1)S(1)}, u32[]{:S(2)}, u32[]{:S(2)}) %collective-permute-start.2) | collective-permute-done | bytes 598048 | tf_op jit(solution)/shard_map/ppermute | solution.py:348
  24.3 2.7 %collective-permute-start.6 = (bf16[2336,128]{1,0:T(8,128)(2,1)S(1)}, bf16[2336,128]{1,0:T(8,128)(2,1)S(1)}, u32[]{:S(2)}, u32[]{:S(2)}) collective-permute-start(bf16[2336,128]{1,0:T(8,128)(2,1)S(1)} %pad_maximum_fusion), channel_id=1, source_target_pairs={{0,2},{1,3},{2,0},{3,1},{4,6},{5,7},{6,4},{7,5},{8,10},{9,11},{10,... | collective-permute-start | bytes 1794056 | tf_op jit(solution)/shard_map/ppermute | solution.py:361
  27.0 1.9 %collective-permute-start.4 = (bf16[2336,128]{1,0:T(8,128)(2,1)S(1)}, bf16[2336,128]{1,0:T(8,128)(2,1)S(1)}, u32[]{:S(2)}, u32[]{:S(2)}) collective-permute-start(bf16[2336,128]{1,0:T(8,128)(2,1)S(1)} %pad_maximum_fusion), channel_id=1, source_target_pairs={{6,0},{7,1},{4,2},{5,3},{10,4},{11,5},{8,6},{9,7},{14,8},{15,9},{1... | collective-permute-start | bytes 1794056 | tf_op jit(solution)/shard_map/ppermute | solution.py:358
  28.9 1.9 %collective-permute-start.5 = (bf16[1056,128]{1,0:T(8,128)(2,1)S(1)}, bf16[1056,128]{1,0:T(8,128)(2,1)S(1)}, u32[]{:S(2)}, u32[]{:S(2)}) collective-permute-start(bf16[1056,128]{1,0:T(8,128)(2,1)S(1)} %pad_maximum_fusion.3), channel_id=1, source_target_pairs={{4,0},{5,1},{6,2},{7,3},{8,4},{9,5},{10,6},{11,7},{12,8},{13,9},{1... | collective-permute-start | bytes 811016 | tf_op jit(solution)/shard_map/ppermute | solution.py:358
  30.9 3.7 %collective-permute-start.3 = (bf16[1280,128]{1,0:T(8,128)(2,1)S(1)}, bf16[1280,128]{1,0:T(8,128)(2,1)S(1)}, u32[]{:S(2)}, u32[]{:S(2)}) collective-permute-start(bf16[1280,128]{1,0:T(8,128)(2,1)S(1)} %pad_maximum_fusion.2), channel_id=1, source_target_pairs={{4,0},{5,1},{6,2},{7,3},{8,4},{9,5},{10,6},{11,7},{12,8},{13,9},{1... | collective-permute-start | bytes 983048 | tf_op jit(solution)/shard_map/ppermute | solution.py:358
  34.7 26.2 %collective-permute-done.6.far.refs_3_ = bf16[2336,128]{1,0:T(8,128)(2,1)S(1)} collective-permute-done((bf16[2336,128]{1,0:T(8,128)(2,1)S(1)}, bf16[2336,128]{1,0:T(8,128)(2,1)S(1)}, u32[]{:S(2)}, u32[]{:S(2)}) %collective-permute-start.6) | collective-permute-done | bytes 598048 | tf_op jit(solution)/shard_map/ppermute | solution.py:361
  60.9 1.4 %own_gram.1 = (bf16[36,256,128]{2,1,0:T(8,128)(2,1)S(1)}, f32[36,256,128]{2,1,0:T(8,128)S(1)}, f32[128,128]{1,0:T(8,128)S(1)}) custom-call(bf16[2336,128]{1,0:T(8,128)(2,1)S(1)} %pad_maximum_fusion.1.near.refs_2_, bf16[2336,128]{1,0:T(8,128)(2,1)S(1)} %collective-permute-done.6.far.refs_3_), custom_call_target="tpu_custom_call" | custom-call | tf_op jit(solution)/shard_map/own_gram/pallas_call | solution.py:226
  62.2 0.0 collective-permute-done.5.refs_0_
  62.2 0.0 collective-permute-done.4.refs_1_
  62.3 2.5 %gram.1 = (f32[36,256,128]{2,1,0:T(8,128)}, f32[128,128]{1,0:T(8,128)S(1)}) custom-call(bf16[1056,128]{1,0:T(8,128)(2,1)S(1)} %collective-permute-done.5.refs_0_, bf16[2336,128]{1,0:T(8,128)(2,1)S(1)} %collective-permute-done.4.refs_1_, bf16[2336,128]{1,0:T(8,128)(2,1)S(1)} %pad_maximum_fusion.1.near.refs_2_, ...), custom_call_target="tpu_custom_call" | custom-call | tf_op jit(solution)/shard_map/gram/pallas_call | solution.py:317
  64.8 1.9 %collective-permute-done.3.refs_0_ = bf16[1280,128]{1,0:T(8,128)(2,1)S(1)} collective-permute-done((bf16[1280,128]{1,0:T(8,128)(2,1)S(1)}, bf16[1280,128]{1,0:T(8,128)(2,1)S(1)}, u32[]{:S(2)}, u32[]{:S(2)}) %collective-permute-start.3) | collective-permute-done | bytes 327712 | tf_op jit(solution)/shard_map/ppermute | solution.py:358
  66.7 2.9 %gram_last.1 = f32[36,256,128]{2,1,0:T(8,128)} custom-call(bf16[1280,128]{1,0:T(8,128)(2,1)S(1)} %collective-permute-done.3.refs_0_, bf16[2336,128]{1,0:T(8,128)(2,1)S(1)} %collective-permute-done.4.refs_1_, f32[128,128]{1,0:T(8,128)S(1)} %get-tuple-element.23.refs_2_, ...), custom_call_target="tpu_custom_call", output_to_operand_aliasing={{}: (5, {})} | custom-call | tf_op jit(solution)/shard_map/gram_last/pallas_call | solution.py:325
  (11 shorter events, 0.2 us)
Async XLA Ops:
  0.0 1.9 %copy-start.1 = (bf16[288,2048]{1,0:T(8,128)(2,1)S(1)}, bf16[288,2048]{1,0:T(8,128)(2,1)}, u32[]{:S(2)}) copy-start(bf16[288,2048]{1,0:T(8,128)(2,1)} %constant.6.clone.basis) | copy-start | bytes 3538948
  1.9 7.6 %copy-start.3 = (f32[31]{0:T(128)S(1)}, f32[31]{0:T(128)}, u32[]{:S(2)}) copy-start(f32[31]{0:T(128)} %taps.3) | copy-start | bytes 376
  2.7 14.6 %collective-permute-start = (bf16[288,256]{1,0:T(8,128)(2,1)S(1)}, bf16[288,256]{1,0:T(8,128)(2,1)S(1)}, u32[]{:S(2)}, u32[]{:S(2)}) collective-permute-start(bf16[288,256]{1,0:T(8,128)(2,1)S(1)} %get-tuple-element.15), channel_id=1, source_target_pairs={{0,4},{4,8},{8,12},{12,16},{16,20},{20,24},{24,28},{28,32},{32,36}... | collective-permute-start | bytes 442376 | tf_op jit(solution)/shard_map/ppermute | solution.py:341
  7.6 11.4 %collective-permute-start.1 = (bf16[288,256]{1,0:T(8,128)(2,1)S(1)}, bf16[288,256]{1,0:T(8,128)(2,1)S(1)}, u32[]{:S(2)}, u32[]{:S(2)}) collective-permute-start(bf16[288,256]{1,0:T(8,128)(2,1)S(1)} %get-tuple-element.16), channel_id=1, source_target_pairs={{4,0},{8,4},{12,8},{16,12},{20,16},{24,20},{28,24},{32,28},{36,32}... | collective-permute-start | bytes 442376 | tf_op jit(solution)/shard_map/ppermute | solution.py:342
  9.5 3.4 %copy-start = (bf16[16,128,2048]{2,1,0:T(8,128)(2,1)S(1)}, bf16[16,128,2048]{2,1,0:T(8,128)(2,1)}, u32[]{:S(2)}) copy-start(bf16[16,128,2048]{2,1,0:T(8,128)(2,1)} %raw.1) | copy-start | bytes 25165828
  12.9 6.1 %copy-start.2 = (s32[16,128]{1,0:T(8,128)S(1)}, s32[16,128]{1,0:T(8,128)}, u32[]{:S(2)}) copy-start(s32[16,128]{1,0:T(8,128)} %mask.1) | copy-start | bytes 24580
  22.1 2.1 %collective-permute-start.2 = (bf16[2336,128]{1,0:T(8,128)(2,1)S(1)}, bf16[2336,128]{1,0:T(8,128)(2,1)S(1)}, u32[]{:S(2)}, u32[]{:S(2)}) collective-permute-start(bf16[2336,128]{1,0:T(8,128)(2,1)S(1)} %get-tuple-element.18), channel_id=1, source_target_pairs={{0,1},{1,0},{2,3},{3,2},{4,5},{5,4},{6,7},{7,6},{8,9},{9,8},{10,11... | collective-permute-start | bytes 1794056 | tf_op jit(solution)/shard_map/ppermute | solution.py:348
  24.3 36.6 %collective-permute-start.6 = (bf16[2336,128]{1,0:T(8,128)(2,1)S(1)}, bf16[2336,128]{1,0:T(8,128)(2,1)S(1)}, u32[]{:S(2)}, u32[]{:S(2)}) collective-permute-start(bf16[2336,128]{1,0:T(8,128)(2,1)S(1)} %pad_maximum_fusion), channel_id=1, source_target_pairs={{0,2},{1,3},{2,0},{3,1},{4,6},{5,7},{6,4},{7,5},{8,10},{9,11},{10,... | collective-permute-start | bytes 1794056 | tf_op jit(solution)/shard_map/ppermute | solution.py:361
  27.0 35.3 %collective-permute-start.4 = (bf16[2336,128]{1,0:T(8,128)(2,1)S(1)}, bf16[2336,128]{1,0:T(8,128)(2,1)S(1)}, u32[]{:S(2)}, u32[]{:S(2)}) collective-permute-start(bf16[2336,128]{1,0:T(8,128)(2,1)S(1)} %pad_maximum_fusion), channel_id=1, source_target_pairs={{6,0},{7,1},{4,2},{5,3},{10,4},{11,5},{8,6},{9,7},{14,8},{15,9},{1... | collective-permute-start | bytes 1794056 | tf_op jit(solution)/shard_map/ppermute | solution.py:358
  28.9 33.3 %collective-permute-start.5 = (bf16[1056,128]{1,0:T(8,128)(2,1)S(1)}, bf16[1056,128]{1,0:T(8,128)(2,1)S(1)}, u32[]{:S(2)}, u32[]{:S(2)}) collective-permute-start(bf16[1056,128]{1,0:T(8,128)(2,1)S(1)} %pad_maximum_fusion.3), channel_id=1, source_target_pairs={{4,0},{5,1},{6,2},{7,3},{8,4},{9,5},{10,6},{11,7},{12,8},{13,9},{1... | collective-permute-start | bytes 811016 | tf_op jit(solution)/shard_map/ppermute | solution.py:358
  30.9 35.8 %collective-permute-start.3 = (bf16[1280,128]{1,0:T(8,128)(2,1)S(1)}, bf16[1280,128]{1,0:T(8,128)(2,1)S(1)}, u32[]{:S(2)}, u32[]{:S(2)}) collective-permute-start(bf16[1280,128]{1,0:T(8,128)(2,1)S(1)} %pad_maximum_fusion.2), channel_id=1, source_target_pairs={{4,0},{5,1},{6,2},{7,3},{8,4},{9,5},{10,6},{11,7},{12,8},{13,9},{1... | collective-permute-start | bytes 983048 | tf_op jit(solution)/shard_map/ppermute | solution.py:358

commit v6 on v5

--- a/solution.py
+++ b/solution.py
@@ -191,25 +191,27 @@
     )(me, taps, filtered, left, right, mask)
 
 
-def pieces(arrays, first, size):
-    height = arrays[0].shape[0] // 2
-    rows = [ref[pl.ds(base + first, size), :] for ref in arrays for base in (0, height)]
+def pieces(arrays, height, first, size):
+    rows = [
+        ref[pl.ds(base + first, size), :]
+        for ref in arrays
+        for base in range(0, ref.shape[0], height)
+    ]
     return jnp.concatenate(rows, axis=0)
 
 
-def own_kernel(segs, bins, near, far, rows, sums, count):
-    own = (near, far)
-    channels = near.shape[1]
-    height = near.shape[0] // 2
+def own_kernel(segs, bins, near, far, far_other, rows, sums, count):
+    own = (near, far, far_other)
+    height, channels = far.shape
     share = rows.shape[0]
-    flags = pieces(own, height - segs, segs)
+    flags = pieces(own, height, height - segs, segs)
     count[...] = dot(flags, flags, TN)
 
     def group(step, carry):
         for at in range(bins):
             bin_at = step * bins + at
             first = pl.multiple_of(bin_at * (2 * segs), 2 * segs)
-            mine = pieces(own, first, 2 * segs)
+            mine = pieces(own, height, first, 2 * segs)
             split = mine.reshape(mine.shape[0] // (2 * segs), 2, segs, channels)
             turned = jnp.concatenate([-split[:, 1:], split[:, :1]], axis=1).reshape(mine.shape)
             both = jnp.concatenate([mine.T, turned.T], axis=0)
@@ -220,12 +222,12 @@
     lax.fori_loop(0, share // bins, group, 0)
 
 
-def own_gram(parts, segs, near, far):
+def own_gram(parts, segs, near, far, far_other):
     channels = near.shape[1]
     share = NF // parts
     return pl.pallas_call(
         functools.partial(own_kernel, segs, 12),
-        in_specs=[WHOLE] * 2,
+        in_specs=[WHOLE] * 3,
         out_specs=[WHOLE] * 3,
         out_shape=[
             jax.ShapeDtypeStruct((share, 2 * channels, 2 * parts * segs), BF16),
@@ -234,12 +236,12 @@
         ],
         compiler_params=pltpu.CompilerParams(vmem_limit_bytes=VMEM),
         name="own_gram",
-    )(near, far)
+    )(near, far, far_other)
 
 
 def gram_kernel(segs, batch, first_half, *refs):
     if first_half:
-        later_near, later_far, near, far, own_count, rows, sums, out, scale, cells, sems = refs
+        later_near, later_far, near, far, far_other, own_count, rows, sums, out, scale, cells, sems = refs
         begin = 0
     else:
         later_near, later_far, scale, rows, sums, _, out, cells, sems = refs
@@ -258,8 +260,8 @@
         return [ref[pl.ds(base + first, size), :] for base in (0, height)]
 
     if first_half:
-        height = near.shape[0] // 2
-        mine = pieces((near, far), height - segs, segs)
+        height = far.shape[0]
+        mine = pieces((near, far, far_other), height, height - segs, segs)
         theirs = jnp.concatenate(
             [later_near[2 * near_height :, :]]
             + group_rows(later_far, far_height, far_height - segs, segs),
@@ -305,7 +307,7 @@
     channels = near.shape[1]
     share = NF // parts
     batch = 4
-    rows, sums, count = own_gram(parts, segs, near, far)
+    rows, sums, count = own_gram(parts, segs, near, *far)
     out = jax.ShapeDtypeStruct((share, 2 * channels, LAGS), F32)
     options = lambda bins: dict(
         scratch_shapes=[
@@ -316,12 +318,12 @@
     )
     out, scale = pl.pallas_call(
         functools.partial(gram_kernel, segs, batch, True),
-        in_specs=[WHOLE] * 7,
+        in_specs=[WHOLE] * 8,
         out_specs=[ANYWHERE, WHOLE],
         out_shape=[out, jax.ShapeDtypeStruct((channels, channels), F32)],
         name="gram",
         **options(AHEAD),
-    )(later_near[0], later_far, near, far, count, rows, sums)
+    )(later_near[0], later_far, near, *far, count, rows, sums)
     return pl.pallas_call(
         functools.partial(gram_kernel, segs, batch, False),
         in_specs=[WHOLE] * 5 + [ANYWHERE],
@@ -346,6 +348,8 @@
     )
     rows = near.shape[0]
     swapped = lax.ppermute(other, "seg", [(j, j ^ 1) for j in range(parts)])
+    across = [(j, j ^ 2) for j in range(parts)]
+    own_far = [lax.ppermute(cells, "seg", across) for cells in (far, swapped[rows:])]
     near = jnp.concatenate([near, swapped[:rows]], axis=0)
     far = jnp.concatenate([far, swapped[rows:]], axis=0)
 
@@ -358,7 +362,6 @@
         return lax.ppermute(cells, GRID, pairs)
 
     later_far = following(far, 2)
-    own_far = lax.ppermute(far, "seg", [(j, j ^ 2) for j in range(parts)])
     middle = AHEAD * 2 * segs
     cut = lambda begin, stop: [near[begin:stop], near[rows + begin : rows + stop]]
     flags = cut(rows - segs, rows)

time: 69.8 us -> 68.9 us (0.987)
  waiting for transfers between devices: 31.7 us -> 28.4 us
  starting transfers between devices: 17.1 us -> 19.4 us
    ppermute x1 -> x2, waiting for transfers between devices: 26.2 us -> 11.5 us  [on_device(): lax.ppermute(cells, 'seg', across)]
    ppermute x3, waiting for transfers between devices: 1.93 us -> 15.2 us  [following(): return lax.ppermute(cells, GRID, pairs)]
    ppermute x1, waiting for transfers between devices: 1.95 us -> 0.01 us  [on_device(): swapped = lax.ppermute(other, 'seg', [(j, j ^ 1) for j in range(parts)])]
    ppermute x1 -> x2, starting transfers between devices: 2.68 us -> 4.63 us  [on_device(): lax.ppermute(cells, 'seg', across)]
  transfers between devices with their start and end apart: 7 -> 8, of which waited for: 4 -> 4; matrix products, arithmetic and copies ran while one was open for 0% -> 0% of each run, Pallas kernels for 12% -> 12%
where the time goes in v6:
time: 68.9 us; the launch traced here: 68.7 us
  waiting for transfers between devices  28.4 us (41%)
  starting transfers between devices  19.4 us (28%)
  Pallas kernels  15.1 us (22%)
  local copies, waits for them, and re-layouts  5.36 us (8%)
    ppermute x3, waiting for transfers between devices, following(): return lax.ppermute(cells, GRID, pairs)  15.2 us
    ppermute x2, waiting for transfers between devices, on_device(): lax.ppermute(cells, 'seg', across)  11.5 us
    ppermute x3, starting transfers between devices, following(): return lax.ppermute(cells, GRID, pairs)  7.97 us
    ppermute x1, starting transfers between devices, on_device(): left = lax.ppermute(tail, 'fiber', [(i, i + 1) for i in range(fibers - 1)])  4.84 us
    ppermute x2, starting transfers between devices, on_device(): lax.ppermute(cells, 'seg', across)  4.63 us
    pallas_call x1, Pallas kernels, main_spectra(): pl.pallas_call(functools.partial(main_kernel, 4, taps.shape[0]), in_specs...  4.41 us
    unnamed x8, local copies, waits for them, and re-layouts  3.39 us
    pallas_call x1, Pallas kernels, whitened_parts(): pl.pallas_call(functools.partial(whiten_kernel, parts, taps.shape[0]), in...  3.1 us
  transfers between devices with their start and end apart: 8, of which 4 were waited for; matrix products, arithmetic and copies ran while one was open for 0% of the time, Pallas kernels for 12%

profile of v6, /device:TPU:110, one launch (start us, length us, event | category | flops | bytes accessed | tf_op | source)
XLA Modules:
  0.0 68.7 jit_solution(9086225489952586701)
XLA Ops:
  0.0 0.0 copy-start.1
  0.0 1.9 %fusion = (bf16[16,16,2048]{2,1,0:T(8,128)(2,1)S(1)}, bf16[16,16,2048]{2,1,0:T(8,128)(2,1)S(1)}) fusion(bf16[16,128,2048]{2,1,0:T(8,128)(2,1)} %raw.1), kind=kLoop, calls=%fused_computation.4 | loop fusion | bytes 4194304 | tf_op jit(solution)/shard_map/slice | solution.py:77
  1.9 0.0 copy-start.3
  1.9 0.0 copy-done.1
  1.9 0.8 %edge_spectra.1 = (bf16[288,256]{1,0:T(8,128)(2,1)S(1)}, bf16[288,256]{1,0:T(8,128)(2,1)S(1)}) custom-call(bf16[16,16,2048]{2,1,0:T(8,128)(2,1)S(1)} %get-tuple-element.26.first, bf16[16,16,2048]{2,1,0:T(8,128)(2,1)S(1)} %get-tuple-element.25.last, bf16[288,2048]{1,0:T(8,128)(2,1)S(1)} %copy-done.1), custom_call_target="tpu_custom_call" | custom-call | flops 1 | bytes 1 | tf_op jit(solution)/shard_map/edge_spectra/pallas_call | solution.py:69
  2.7 4.8 %collective-permute-start = (bf16[288,256]{1,0:T(8,128)(2,1)S(1)}, bf16[288,256]{1,0:T(8,128)(2,1)S(1)}, u32[]{:S(2)}, u32[]{:S(2)}) collective-permute-start(bf16[288,256]{1,0:T(8,128)(2,1)S(1)} %get-tuple-element.15), channel_id=1, source_target_pairs={{0,4},{4,8},{8,12},{12,16},{16,20},{20,24},{24,28},{28,32},{32,36}... | collective-permute-start | bytes 442376 | tf_op jit(solution)/shard_map/ppermute | solution.py:343
  7.6 1.9 %collective-permute-start.1 = (bf16[288,256]{1,0:T(8,128)(2,1)S(1)}, bf16[288,256]{1,0:T(8,128)(2,1)S(1)}, u32[]{:S(2)}, u32[]{:S(2)}) collective-permute-start(bf16[288,256]{1,0:T(8,128)(2,1)S(1)} %get-tuple-element.16), channel_id=1, source_target_pairs={{4,0},{8,4},{12,8},{16,12},{20,16},{24,20},{28,24},{32,28},{36,32}... | collective-permute-start | bytes 442376 | tf_op jit(solution)/shard_map/ppermute | solution.py:344
  9.5 0.0 copy-done.3
  9.5 0.0 copy-start
  9.5 3.4 %copy-done = bf16[16,128,2048]{2,1,0:T(8,128)(2,1)S(1)} copy-done((bf16[16,128,2048]{2,1,0:T(8,128)(2,1)S(1)}, bf16[16,128,2048]{2,1,0:T(8,128)(2,1)}, u32[]{:S(2)}) %copy-start) | copy-done | bytes 8388632
  12.9 0.0 copy-start.2
  12.9 4.4 %main_spectra.1.filtered = f32[4608,128]{1,0:T(8,128)S(1)} custom-call(bf16[16,128,2048]{2,1,0:T(8,128)(2,1)S(1)} %copy-done, bf16[288,2048]{1,0:T(8,128)(2,1)S(1)} %copy-done.1, f32[31]{0:T(128)S(1)} %copy-done.3), custom_call_target="tpu_custom_call" | custom-call | tf_op jit(solution)/shard_map/main_spectra/pallas_call | solution.py:106
  17.3 0.0 collective-permute-done.left
  17.3 1.7 %collective-permute-done.1.right = bf16[288,256]{1,0:T(8,128)(2,1)S(1)} collective-permute-done((bf16[288,256]{1,0:T(8,128)(2,1)S(1)}, bf16[288,256]{1,0:T(8,128)(2,1)S(1)}, u32[]{:S(2)}, u32[]{:S(2)}) %collective-permute-start.1) | collective-permute-done | bytes 147488 | tf_op jit(solution)/shard_map/ppermute | solution.py:344
  19.0 0.0 copy-done.2
  19.0 3.1 %whiten.1 = (bf16[1168,128]{1,0:T(8,128)(2,1)S(1)}, bf16[1168,128]{1,0:T(8,128)(2,1)S(1)}, bf16[2336,128]{1,0:T(8,128)(2,1)S(1)}) custom-call(s32[1]{0:T(128)} %bitcast.me, f32[31]{0:T(128)S(1)} %copy-done.3, f32[4608,128]{1,0:T(8,128)S(1)} %main_spectra.1.filtered, bf16[288,256]{1,0:T(8,128)(2,1)S(1)} %collective-permute-done.left, ...), custom_call_target="tpu_custom_call" | custom-call | tf_op jit(solution)/shard_map/whiten/pallas_call | solution.py:180
  22.1 0.1 collective-permute-start.2
  22.2 2.7 %collective-permute-start.6 = (bf16[1168,128]{1,0:T(8,128)(2,1)S(1)}, bf16[1168,128]{1,0:T(8,128)(2,1)S(1)}, u32[]{:S(2)}, u32[]{:S(2)}) collective-permute-start(bf16[1168,128]{1,0:T(8,128)(2,1)S(1)} %get-tuple-element.19), channel_id=1, source_target_pairs={{0,2},{1,3},{2,0},{3,1},{4,6},{5,7},{6,4},{7,5},{8,10},{9,11},{10,... | collective-permute-start | bytes 897032 | tf_op jit(solution)/shard_map/ppermute | solution.py:352
  24.9 0.0 collective-permute-done.2
  25.0 1.9 %collective-permute-start.7 = (bf16[1168,128]{1,0:T(8,128)(2,1)S(1)}, bf16[1168,128]{1,0:T(8,128)(2,1)S(1)}, u32[]{:S(2)}, u32[]{:S(2)}) collective-permute-start(bf16[1168,128]{1,0:T(8,128)(2,1)S(1)} %get-tuple-element.28), channel_id=1, source_target_pairs={{0,2},{1,3},{2,0},{3,1},{4,6},{5,7},{6,4},{7,5},{8,10},{9,11},{10,... | collective-permute-start | bytes 897032 | tf_op jit(solution)/shard_map/ppermute | solution.py:352
  27.0 1.9 %collective-permute-start.4 = (bf16[2336,128]{1,0:T(8,128)(2,1)S(1)}, bf16[2336,128]{1,0:T(8,128)(2,1)S(1)}, u32[]{:S(2)}, u32[]{:S(2)}) collective-permute-start(bf16[2336,128]{1,0:T(8,128)(2,1)S(1)} %pad_maximum_fusion), channel_id=1, source_target_pairs={{6,0},{7,1},{4,2},{5,3},{10,4},{11,5},{8,6},{9,7},{14,8},{15,9},{1... | collective-permute-start | bytes 1794056 | tf_op jit(solution)/shard_map/ppermute | solution.py:362
  28.9 1.9 %collective-permute-start.5 = (bf16[1056,128]{1,0:T(8,128)(2,1)S(1)}, bf16[1056,128]{1,0:T(8,128)(2,1)S(1)}, u32[]{:S(2)}, u32[]{:S(2)}) collective-permute-start(bf16[1056,128]{1,0:T(8,128)(2,1)S(1)} %pad_maximum_fusion.3), channel_id=1, source_target_pairs={{4,0},{5,1},{6,2},{7,3},{8,4},{9,5},{10,6},{11,7},{12,8},{13,9},{1... | collective-permute-start | bytes 811016 | tf_op jit(solution)/shard_map/ppermute | solution.py:362
  30.9 4.1 %collective-permute-start.3 = (bf16[1280,128]{1,0:T(8,128)(2,1)S(1)}, bf16[1280,128]{1,0:T(8,128)(2,1)S(1)}, u32[]{:S(2)}, u32[]{:S(2)}) collective-permute-start(bf16[1280,128]{1,0:T(8,128)(2,1)S(1)} %pad_maximum_fusion.2), channel_id=1, source_target_pairs={{4,0},{5,1},{6,2},{7,3},{8,4},{9,5},{10,6},{11,7},{12,8},{13,9},{1... | collective-permute-start | bytes 983048 | tf_op jit(solution)/shard_map/ppermute | solution.py:362
  35.1 0.0 collective-permute-done.6.far.refs_3_
  35.1 11.5 %collective-permute-done.7.far_other.refs_4_ = bf16[1168,128]{1,0:T(8,128)(2,1)S(1)} collective-permute-done((bf16[1168,128]{1,0:T(8,128)(2,1)S(1)}, bf16[1168,128]{1,0:T(8,128)(2,1)S(1)}, u32[]{:S(2)}, u32[]{:S(2)}) %collective-permute-start.7) | collective-permute-done | bytes 299040 | tf_op jit(solution)/shard_map/ppermute | solution.py:352
  46.7 1.4 %own_gram.1 = (bf16[36,256,128]{2,1,0:T(8,128)(2,1)S(1)}, f32[36,256,128]{2,1,0:T(8,128)S(1)}, f32[128,128]{1,0:T(8,128)S(1)}) custom-call(bf16[2336,128]{1,0:T(8,128)(2,1)S(1)} %pad_maximum_fusion.1.near.refs_2_, bf16[1168,128]{1,0:T(8,128)(2,1)S(1)} %collective-permute-done.6.far.refs_3_, bf16[1168,128]{1,0:T(8,128)(2,1)S(1)} %collective-permute-done.7.far_other.refs_4_), custom_call_target="tpu_custom_call" | custom-call | tf_op jit(solution)/shard_map/own_gram/pallas_call | solution.py:228
  48.1 11.8 %collective-permute-done.5.refs_0_ = bf16[1056,128]{1,0:T(8,128)(2,1)S(1)} collective-permute-done((bf16[1056,128]{1,0:T(8,128)(2,1)S(1)}, bf16[1056,128]{1,0:T(8,128)(2,1)S(1)}, u32[]{:S(2)}, u32[]{:S(2)}) %collective-permute-start.5) | collective-permute-done | bytes 270368 | tf_op jit(solution)/shard_map/ppermute | solution.py:362
  59.9 0.0 collective-permute-done.4.refs_1_
  59.9 2.5 %gram.1 = (f32[36,256,128]{2,1,0:T(8,128)}, f32[128,128]{1,0:T(8,128)S(1)}) custom-call(bf16[1056,128]{1,0:T(8,128)(2,1)S(1)} %collective-permute-done.5.refs_0_, bf16[2336,128]{1,0:T(8,128)(2,1)S(1)} %collective-permute-done.4.refs_1_, bf16[2336,128]{1,0:T(8,128)(2,1)S(1)} %pad_maximum_fusion.1.near.refs_2_, ...), custom_call_target="tpu_custom_call" | custom-call | tf_op jit(solution)/shard_map/gram/pallas_call | solution.py:319
  62.4 3.4 %collective-permute-done.3.refs_0_ = bf16[1280,128]{1,0:T(8,128)(2,1)S(1)} collective-permute-done((bf16[1280,128]{1,0:T(8,128)(2,1)S(1)}, bf16[1280,128]{1,0:T(8,128)(2,1)S(1)}, u32[]{:S(2)}, u32[]{:S(2)}) %collective-permute-start.3) | collective-permute-done | bytes 327712 | tf_op jit(solution)/shard_map/ppermute | solution.py:362
  65.8 2.9 %gram_last.1 = f32[36,256,128]{2,1,0:T(8,128)} custom-call(bf16[1280,128]{1,0:T(8,128)(2,1)S(1)} %collective-permute-done.3.refs_0_, bf16[2336,128]{1,0:T(8,128)(2,1)S(1)} %collective-permute-done.4.refs_1_, f32[128,128]{1,0:T(8,128)S(1)} %get-tuple-element.23.refs_2_, ...), custom_call_target="tpu_custom_call", output_to_operand_aliasing={{}: (5, {})} | custom-call | tf_op jit(solution)/shard_map/gram_last/pallas_call | solution.py:327
  (11 shorter events, 0.2 us)
Async XLA Ops:
  0.0 1.9 %copy-start.1 = (bf16[288,2048]{1,0:T(8,128)(2,1)S(1)}, bf16[288,2048]{1,0:T(8,128)(2,1)}, u32[]{:S(2)}) copy-start(bf16[288,2048]{1,0:T(8,128)(2,1)} %constant.6.clone.basis) | copy-start | bytes 3538948
  1.9 7.6 %copy-start.3 = (f32[31]{0:T(128)S(1)}, f32[31]{0:T(128)}, u32[]{:S(2)}) copy-start(f32[31]{0:T(128)} %taps.3) | copy-start | bytes 376
  2.7 14.6 %collective-permute-start = (bf16[288,256]{1,0:T(8,128)(2,1)S(1)}, bf16[288,256]{1,0:T(8,128)(2,1)S(1)}, u32[]{:S(2)}, u32[]{:S(2)}) collective-permute-start(bf16[288,256]{1,0:T(8,128)(2,1)S(1)} %get-tuple-element.15), channel_id=1, source_target_pairs={{0,4},{4,8},{8,12},{12,16},{16,20},{20,24},{24,28},{28,32},{32,36}... | collective-permute-start | bytes 442376 | tf_op jit(solution)/shard_map/ppermute | solution.py:343
  7.6 11.4 %collective-permute-start.1 = (bf16[288,256]{1,0:T(8,128)(2,1)S(1)}, bf16[288,256]{1,0:T(8,128)(2,1)S(1)}, u32[]{:S(2)}, u32[]{:S(2)}) collective-permute-start(bf16[288,256]{1,0:T(8,128)(2,1)S(1)} %get-tuple-element.16), channel_id=1, source_target_pairs={{4,0},{8,4},{12,8},{16,12},{20,16},{24,20},{28,24},{32,28},{36,32}... | collective-permute-start | bytes 442376 | tf_op jit(solution)/shard_map/ppermute | solution.py:344
  9.5 3.4 %copy-start = (bf16[16,128,2048]{2,1,0:T(8,128)(2,1)S(1)}, bf16[16,128,2048]{2,1,0:T(8,128)(2,1)}, u32[]{:S(2)}) copy-start(bf16[16,128,2048]{2,1,0:T(8,128)(2,1)} %raw.1) | copy-start | bytes 25165828
  12.9 6.1 %copy-start.2 = (s32[16,128]{1,0:T(8,128)S(1)}, s32[16,128]{1,0:T(8,128)}, u32[]{:S(2)}) copy-start(s32[16,128]{1,0:T(8,128)} %mask.1) | copy-start | bytes 24580
  22.1 2.8 %collective-permute-start.2 = (bf16[2336,128]{1,0:T(8,128)(2,1)S(1)}, bf16[2336,128]{1,0:T(8,128)(2,1)S(1)}, u32[]{:S(2)}, u32[]{:S(2)}) collective-permute-start(bf16[2336,128]{1,0:T(8,128)(2,1)S(1)} %get-tuple-element.18), channel_id=1, source_target_pairs={{0,1},{1,0},{2,3},{3,2},{4,5},{5,4},{6,7},{7,6},{8,9},{9,8},{10,11... | collective-permute-start | bytes 1794056 | tf_op jit(solution)/shard_map/ppermute | solution.py:350
  22.2 12.9 %collective-permute-start.6 = (bf16[1168,128]{1,0:T(8,128)(2,1)S(1)}, bf16[1168,128]{1,0:T(8,128)(2,1)S(1)}, u32[]{:S(2)}, u32[]{:S(2)}) collective-permute-start(bf16[1168,128]{1,0:T(8,128)(2,1)S(1)} %get-tuple-element.19), channel_id=1, source_target_pairs={{0,2},{1,3},{2,0},{3,1},{4,6},{5,7},{6,4},{7,5},{8,10},{9,11},{10,... | collective-permute-start | bytes 897032 | tf_op jit(solution)/shard_map/ppermute | solution.py:352
  25.0 21.7 %collective-permute-start.7 = (bf16[1168,128]{1,0:T(8,128)(2,1)S(1)}, bf16[1168,128]{1,0:T(8,128)(2,1)S(1)}, u32[]{:S(2)}, u32[]{:S(2)}) collective-permute-start(bf16[1168,128]{1,0:T(8,128)(2,1)S(1)} %get-tuple-element.28), channel_id=1, source_target_pairs={{0,2},{1,3},{2,0},{3,1},{4,6},{5,7},{6,4},{7,5},{8,10},{9,11},{10,... | collective-permute-start | bytes 897032 | tf_op jit(solution)/shard_map/ppermute | solution.py:352
  27.0 32.9 %collective-permute-start.4 = (bf16[2336,128]{1,0:T(8,128)(2,1)S(1)}, bf16[2336,128]{1,0:T(8,128)(2,1)S(1)}, u32[]{:S(2)}, u32[]{:S(2)}) collective-permute-start(bf16[2336,128]{1,0:T(8,128)(2,1)S(1)} %pad_maximum_fusion), channel_id=1, source_target_pairs={{6,0},{7,1},{4,2},{5,3},{10,4},{11,5},{8,6},{9,7},{14,8},{15,9},{1... | collective-permute-start | bytes 1794056 | tf_op jit(solution)/shard_map/ppermute | solution.py:362
  28.9 30.9 %collective-permute-start.5 = (bf16[1056,128]{1,0:T(8,128)(2,1)S(1)}, bf16[1056,128]{1,0:T(8,128)(2,1)S(1)}, u32[]{:S(2)}, u32[]{:S(2)}) collective-permute-start(bf16[1056,128]{1,0:T(8,128)(2,1)S(1)} %pad_maximum_fusion.3), channel_id=1, source_target_pairs={{4,0},{5,1},{6,2},{7,3},{8,4},{9,5},{10,6},{11,7},{12,8},{13,9},{1... | collective-permute-start | bytes 811016 | tf_op jit(solution)/shard_map/ppermute | solution.py:362
  30.9 34.9 %collective-permute-start.3 = (bf16[1280,128]{1,0:T(8,128)(2,1)S(1)}, bf16[1280,128]{1,0:T(8,128)(2,1)S(1)}, u32[]{:S(2)}, u32[]{:S(2)}) collective-permute-start(bf16[1280,128]{1,0:T(8,128)(2,1)S(1)} %pad_maximum_fusion.2), channel_id=1, source_target_pairs={{4,0},{5,1},{6,2},{7,3},{8,4},{9,5},{10,6},{11,7},{12,8},{13,9},{1... | collective-permute-start | bytes 983048 | tf_op jit(solution)/shard_map/ppermute | solution.py:362

commit v7 on v6

--- a/solution.py
+++ b/solution.py
@@ -20,7 +20,7 @@
 water_share = 0.1
 
 GRID = ("fiber", "seg")
-AHEAD = 16
+CUTS = (0, 10, 22, 36)
 VMEM = 24 * 1024 * 1024
 STREAM = 50 * 1024 * 1024
 F32 = jnp.float32
@@ -239,13 +239,11 @@
     )(near, far, far_other)
 
 
-def gram_kernel(segs, batch, first_half, *refs):
+def gram_kernel(segs, batch, begin, first_half, *refs):
     if first_half:
         later_near, later_far, near, far, far_other, own_count, rows, sums, out, scale, cells, sems = refs
-        begin = 0
     else:
         later_near, later_far, scale, rows, sums, _, out, cells, sems = refs
-        begin = out.shape[0] - cells.shape[0]
     channels = later_near.shape[1]
     count = cells.shape[0]
     bins = count
@@ -306,7 +304,7 @@
 def stacked(parts, segs, near, later_near, far, later_far):
     channels = near.shape[1]
     share = NF // parts
-    batch = 4
+    batch = 2
     rows, sums, count = own_gram(parts, segs, near, *far)
     out = jax.ShapeDtypeStruct((share, 2 * channels, LAGS), F32)
     options = lambda bins: dict(
@@ -317,22 +315,24 @@
         compiler_params=pltpu.CompilerParams(vmem_limit_bytes=VMEM),
     )
     out, scale = pl.pallas_call(
-        functools.partial(gram_kernel, segs, batch, True),
+        functools.partial(gram_kernel, segs, batch, 0, True),
         in_specs=[WHOLE] * 8,
         out_specs=[ANYWHERE, WHOLE],
         out_shape=[out, jax.ShapeDtypeStruct((channels, channels), F32)],
         name="gram",
-        **options(AHEAD),
+        **options(CUTS[1]),
     )(later_near[0], later_far, near, *far, count, rows, sums)
-    return pl.pallas_call(
-        functools.partial(gram_kernel, segs, batch, False),
-        in_specs=[WHOLE] * 5 + [ANYWHERE],
-        out_specs=ANYWHERE,
-        out_shape=jax.ShapeDtypeStruct(out.shape, F32),
-        input_output_aliases={5: 0},
-        name="gram_last",
-        **options(share - AHEAD),
-    )(later_near[1], later_far, scale, rows, sums, out)
+    for at in range(1, len(CUTS) - 1):
+        out = pl.pallas_call(
+            functools.partial(gram_kernel, segs, batch, CUTS[at], False),
+            in_specs=[WHOLE] * 5 + [ANYWHERE],
+            out_specs=ANYWHERE,
+            out_shape=jax.ShapeDtypeStruct(out.shape, F32),
+            input_output_aliases={5: 0},
+            name="gram_more",
+            **options(CUTS[at + 1] - CUTS[at]),
+        )(later_near[at], later_far, scale, rows, sums, out)
+    return out
 
 
 def on_device(fibers, parts, raw_strain, fir_taps, good_mask):
@@ -362,13 +362,13 @@
         return lax.ppermute(cells, GRID, pairs)
 
     later_far = following(far, 2)
-    middle = AHEAD * 2 * segs
     cut = lambda begin, stop: [near[begin:stop], near[rows + begin : rows + stop]]
-    flags = cut(rows - segs, rows)
-    later_near = [
-        following(jnp.concatenate(cells, axis=0), 0)
-        for cells in (cut(0, middle) + flags, cut(middle, rows - segs))
-    ]
+    later_near = []
+    for begin, stop in zip(CUTS, CUTS[1:]):
+        cells = cut(begin * 2 * segs, stop * 2 * segs)
+        if begin == 0:
+            cells += cut(rows - segs, rows)
+        later_near.append(following(jnp.concatenate(cells, axis=0), 0))
     out = stacked(parts, segs, near, later_near, own_far, later_far)
     return out.reshape(out.shape[0], channels, 2, LAGS)
 

time: 68.9 us -> 68.3 us (level)
  waiting for transfers between devices: 28.4 us -> 25.1 us
  starting transfers between devices: 19.4 us -> 21.4 us
  Pallas kernels: 15.1 us -> 15.9 us
    ppermute x2, waiting for transfers between devices: 11.5 us -> 9.61 us  [on_device(): lax.ppermute(cells, 'seg', across)]
    ppermute x3 -> x4, starting transfers between devices: 7.97 us -> 9.9 us  [following(): return lax.ppermute(cells, GRID, pairs)]
    ppermute x3 -> x4, waiting for transfers between devices: 15.2 us -> 13.8 us  [following(): return lax.ppermute(cells, GRID, pairs)]
    pallas_call x2 -> x3, Pallas kernels: 5.39 us -> 6.16 us  [the longest x2 4.26 us: stacked(): pl.pallas_call(functools.partial(gram_kernel, segs, batch, CUTS[at], Fals...]
  transfers between devices with their start and end apart: 8 -> 9, of which waited for: 4 -> 5; matrix products, arithmetic and copies ran while one was open for 0% -> 0% of each run, Pallas kernels for 12% -> 14%
where the time goes in v7:
time: 68.3 us; the launch traced here: 68.1 us
  waiting for transfers between devices  25.1 us (37%)
  starting transfers between devices  21.4 us (31%)
  Pallas kernels  15.9 us (23%)
  local copies, waits for them, and re-layouts  5.36 us (8%)
    ppermute x4, waiting for transfers between devices, following(): return lax.ppermute(cells, GRID, pairs)  13.8 us
    ppermute x4, starting transfers between devices, following(): return lax.ppermute(cells, GRID, pairs)  9.9 us
    ppermute x2, waiting for transfers between devices, on_device(): lax.ppermute(cells, 'seg', across)  9.61 us
    ppermute x1, starting transfers between devices, on_device(): left = lax.ppermute(tail, 'fiber', [(i, i + 1) for i in range(fibers - 1)])  4.84 us
    ppermute x2, starting transfers between devices, on_device(): lax.ppermute(cells, 'seg', across)  4.62 us
    pallas_call x1, Pallas kernels, main_spectra(): pl.pallas_call(functools.partial(main_kernel, 4, taps.shape[0]), in_specs...  4.41 us
    pallas_call x2, Pallas kernels, stacked(): pl.pallas_call(functools.partial(gram_kernel, segs, batch, CUTS[at], Fals...  4.26 us
    unnamed x8, local copies, waits for them, and re-layouts  3.39 us
  transfers between devices with their start and end apart: 9, of which 5 were waited for; matrix products, arithmetic and copies ran while one was open for 0% of the time, Pallas kernels for 14%

profile of v7, /device:TPU:110, one launch (start us, length us, event | category | flops | bytes accessed | tf_op | source)
XLA Modules:
  0.0 68.1 jit_solution(946921465437562434)
XLA Ops:
  0.0 0.0 copy-start.1
  0.0 1.9 %fusion = (bf16[16,16,2048]{2,1,0:T(8,128)(2,1)S(1)}, bf16[16,16,2048]{2,1,0:T(8,128)(2,1)S(1)}) fusion(bf16[16,128,2048]{2,1,0:T(8,128)(2,1)} %raw.1), kind=kLoop, calls=%fused_computation.5 | loop fusion | bytes 4194304 | tf_op jit(solution)/shard_map/slice | solution.py:77
  1.9 0.0 copy-start.3
  1.9 0.0 copy-done.1
  1.9 0.8 %edge_spectra.1 = (bf16[288,256]{1,0:T(8,128)(2,1)S(1)}, bf16[288,256]{1,0:T(8,128)(2,1)S(1)}) custom-call(bf16[16,16,2048]{2,1,0:T(8,128)(2,1)S(1)} %get-tuple-element.26.first, bf16[16,16,2048]{2,1,0:T(8,128)(2,1)S(1)} %get-tuple-element.25.last, bf16[288,2048]{1,0:T(8,128)(2,1)S(1)} %copy-done.1), custom_call_target="tpu_custom_call" | custom-call | flops 1 | bytes 1 | tf_op jit(solution)/shard_map/edge_spectra/pallas_call | solution.py:69
  2.7 4.8 %collective-permute-start = (bf16[288,256]{1,0:T(8,128)(2,1)S(1)}, bf16[288,256]{1,0:T(8,128)(2,1)S(1)}, u32[]{:S(2)}, u32[]{:S(2)}) collective-permute-start(bf16[288,256]{1,0:T(8,128)(2,1)S(1)} %get-tuple-element.15), channel_id=1, source_target_pairs={{0,4},{4,8},{8,12},{12,16},{16,20},{20,24},{24,28},{28,32},{32,36}... | collective-permute-start | bytes 442376 | tf_op jit(solution)/shard_map/ppermute | solution.py:343
  7.6 1.9 %collective-permute-start.1 = (bf16[288,256]{1,0:T(8,128)(2,1)S(1)}, bf16[288,256]{1,0:T(8,128)(2,1)S(1)}, u32[]{:S(2)}, u32[]{:S(2)}) collective-permute-start(bf16[288,256]{1,0:T(8,128)(2,1)S(1)} %get-tuple-element.16), channel_id=1, source_target_pairs={{4,0},{8,4},{12,8},{16,12},{20,16},{24,20},{28,24},{32,28},{36,32}... | collective-permute-start | bytes 442376 | tf_op jit(solution)/shard_map/ppermute | solution.py:344
  9.5 0.0 copy-done.3
  9.5 0.0 copy-start
  9.5 3.4 %copy-done = bf16[16,128,2048]{2,1,0:T(8,128)(2,1)S(1)} copy-done((bf16[16,128,2048]{2,1,0:T(8,128)(2,1)S(1)}, bf16[16,128,2048]{2,1,0:T(8,128)(2,1)}, u32[]{:S(2)}) %copy-start) | copy-done | bytes 8388632
  12.9 0.0 copy-start.2
  12.9 4.4 %main_spectra.1.filtered = f32[4608,128]{1,0:T(8,128)S(1)} custom-call(bf16[16,128,2048]{2,1,0:T(8,128)(2,1)S(1)} %copy-done, bf16[288,2048]{1,0:T(8,128)(2,1)S(1)} %copy-done.1, f32[31]{0:T(128)S(1)} %copy-done.3), custom_call_target="tpu_custom_call" | custom-call | tf_op jit(solution)/shard_map/main_spectra/pallas_call | solution.py:106
  17.3 0.0 collective-permute-done.left
  17.3 1.7 %collective-permute-done.1.right = bf16[288,256]{1,0:T(8,128)(2,1)S(1)} collective-permute-done((bf16[288,256]{1,0:T(8,128)(2,1)S(1)}, bf16[288,256]{1,0:T(8,128)(2,1)S(1)}, u32[]{:S(2)}, u32[]{:S(2)}) %collective-permute-start.1) | collective-permute-done | bytes 147488 | tf_op jit(solution)/shard_map/ppermute | solution.py:344
  19.0 0.0 copy-done.2
  19.0 3.1 %whiten.1 = (bf16[1168,128]{1,0:T(8,128)(2,1)S(1)}, bf16[1168,128]{1,0:T(8,128)(2,1)S(1)}, bf16[2336,128]{1,0:T(8,128)(2,1)S(1)}) custom-call(s32[1]{0:T(128)} %bitcast.me, f32[31]{0:T(128)S(1)} %copy-done.3, f32[4608,128]{1,0:T(8,128)S(1)} %main_spectra.1.filtered, bf16[288,256]{1,0:T(8,128)(2,1)S(1)} %collective-permute-done.left, ...), custom_call_target="tpu_custom_call" | custom-call | tf_op jit(solution)/shard_map/whiten/pallas_call | solution.py:180
  22.1 0.1 collective-permute-start.2
  22.3 2.7 %collective-permute-start.6 = (bf16[1168,128]{1,0:T(8,128)(2,1)S(1)}, bf16[1168,128]{1,0:T(8,128)(2,1)S(1)}, u32[]{:S(2)}, u32[]{:S(2)}) collective-permute-start(bf16[1168,128]{1,0:T(8,128)(2,1)S(1)} %get-tuple-element.19), channel_id=1, source_target_pairs={{0,2},{1,3},{2,0},{3,1},{4,6},{5,7},{6,4},{7,5},{8,10},{9,11},{10,... | collective-permute-start | bytes 897032 | tf_op jit(solution)/shard_map/ppermute | solution.py:352
  24.9 0.0 collective-permute-done.2
  25.0 1.9 %collective-permute-start.7 = (bf16[1168,128]{1,0:T(8,128)(2,1)S(1)}, bf16[1168,128]{1,0:T(8,128)(2,1)S(1)}, u32[]{:S(2)}, u32[]{:S(2)}) collective-permute-start(bf16[1168,128]{1,0:T(8,128)(2,1)S(1)} %get-tuple-element.28), channel_id=1, source_target_pairs={{0,2},{1,3},{2,0},{3,1},{4,6},{5,7},{6,4},{7,5},{8,10},{9,11},{10,... | collective-permute-start | bytes 897032 | tf_op jit(solution)/shard_map/ppermute | solution.py:352
  27.0 1.9 %collective-permute-start.4 = (bf16[2336,128]{1,0:T(8,128)(2,1)S(1)}, bf16[2336,128]{1,0:T(8,128)(2,1)S(1)}, u32[]{:S(2)}, u32[]{:S(2)}) collective-permute-start(bf16[2336,128]{1,0:T(8,128)(2,1)S(1)} %pad_maximum_fusion), channel_id=1, source_target_pairs={{6,0},{7,1},{4,2},{5,3},{10,4},{11,5},{8,6},{9,7},{14,8},{15,9},{1... | collective-permute-start | bytes 1794056 | tf_op jit(solution)/shard_map/ppermute | solution.py:362
  28.9 1.9 %collective-permute-start.5 = (bf16[672,128]{1,0:T(8,128)(2,1)S(1)}, bf16[672,128]{1,0:T(8,128)(2,1)S(1)}, u32[]{:S(2)}, u32[]{:S(2)}) collective-permute-start(bf16[672,128]{1,0:T(8,128)(2,1)S(1)} %pad_maximum_fusion.4), channel_id=1, source_target_pairs={{4,0},{5,1},{6,2},{7,3},{8,4},{9,5},{10,6},{11,7},{12,8},{13,9},{1... | collective-permute-start | bytes 516104 | tf_op jit(solution)/shard_map/ppermute | solution.py:362
  30.9 4.2 %collective-permute-start.8 = (bf16[768,128]{1,0:T(8,128)(2,1)S(1)}, bf16[768,128]{1,0:T(8,128)(2,1)S(1)}, u32[]{:S(2)}, u32[]{:S(2)}) collective-permute-start(bf16[768,128]{1,0:T(8,128)(2,1)S(1)} %pad_maximum_fusion.3), channel_id=1, source_target_pairs={{4,0},{5,1},{6,2},{7,3},{8,4},{9,5},{10,6},{11,7},{12,8},{13,9},{1... | collective-permute-start | bytes 589832 | tf_op jit(solution)/shard_map/ppermute | solution.py:362
  35.1 0.0 collective-permute-done.6.far.refs_3_
  35.1 1.9 %collective-permute-start.3 = (bf16[896,128]{1,0:T(8,128)(2,1)S(1)}, bf16[896,128]{1,0:T(8,128)(2,1)S(1)}, u32[]{:S(2)}, u32[]{:S(2)}) collective-permute-start(bf16[896,128]{1,0:T(8,128)(2,1)S(1)} %pad_maximum_fusion.2), channel_id=1, source_target_pairs={{4,0},{5,1},{6,2},{7,3},{8,4},{9,5},{10,6},{11,7},{12,8},{13,9},{1... | collective-permute-start | bytes 688136 | tf_op jit(solution)/shard_map/ppermute | solution.py:362
  37.1 9.6 %collective-permute-done.7.far_other.refs_4_ = bf16[1168,128]{1,0:T(8,128)(2,1)S(1)} collective-permute-done((bf16[1168,128]{1,0:T(8,128)(2,1)S(1)}, bf16[1168,128]{1,0:T(8,128)(2,1)S(1)}, u32[]{:S(2)}, u32[]{:S(2)}) %collective-permute-start.7) | collective-permute-done | bytes 299040 | tf_op jit(solution)/shard_map/ppermute | solution.py:352
  46.7 1.4 %own_gram.1 = (bf16[36,256,128]{2,1,0:T(8,128)(2,1)S(1)}, f32[36,256,128]{2,1,0:T(8,128)S(1)}, f32[128,128]{1,0:T(8,128)S(1)}) custom-call(bf16[2336,128]{1,0:T(8,128)(2,1)S(1)} %pad_maximum_fusion.1.near.refs_2_, bf16[1168,128]{1,0:T(8,128)(2,1)S(1)} %collective-permute-done.6.far.refs_3_, bf16[1168,128]{1,0:T(8,128)(2,1)S(1)} %collective-permute-done.7.far_other.refs_4_), custom_call_target="tpu_custom_call" | custom-call | tf_op jit(solution)/shard_map/own_gram/pallas_call | solution.py:228
  48.1 9.7 %collective-permute-done.5.refs_0_ = bf16[672,128]{1,0:T(8,128)(2,1)S(1)} collective-permute-done((bf16[672,128]{1,0:T(8,128)(2,1)S(1)}, bf16[672,128]{1,0:T(8,128)(2,1)S(1)}, u32[]{:S(2)}, u32[]{:S(2)}) %collective-permute-start.5) | collective-permute-done | bytes 172064 | tf_op jit(solution)/shard_map/ppermute | solution.py:362
  57.8 0.0 collective-permute-done.4.refs_1_
  57.8 1.9 %gram.1 = (f32[36,256,128]{2,1,0:T(8,128)}, f32[128,128]{1,0:T(8,128)S(1)}) custom-call(bf16[672,128]{1,0:T(8,128)(2,1)S(1)} %collective-permute-done.5.refs_0_, bf16[2336,128]{1,0:T(8,128)(2,1)S(1)} %collective-permute-done.4.refs_1_, bf16[2336,128]{1,0:T(8,128)(2,1)S(1)} %pad_maximum_fusion.1.near.refs_2_, ...), custom_call_target="tpu_custom_call" | custom-call | tf_op jit(solution)/shard_map/gram/pallas_call | solution.py:317
  59.7 2.3 %collective-permute-done.8.refs_0_ = bf16[768,128]{1,0:T(8,128)(2,1)S(1)} collective-permute-done((bf16[768,128]{1,0:T(8,128)(2,1)S(1)}, bf16[768,128]{1,0:T(8,128)(2,1)S(1)}, u32[]{:S(2)}, u32[]{:S(2)}) %collective-permute-start.8) | collective-permute-done | bytes 196640 | tf_op jit(solution)/shard_map/ppermute | solution.py:362
  62.0 2.0 %gram_more.2.refs_5_ = f32[36,256,128]{2,1,0:T(8,128)} custom-call(bf16[768,128]{1,0:T(8,128)(2,1)S(1)} %collective-permute-done.8.refs_0_, bf16[2336,128]{1,0:T(8,128)(2,1)S(1)} %collective-permute-done.4.refs_1_, f32[128,128]{1,0:T(8,128)S(1)} %get-tuple-element.23.refs_2_, ...), custom_call_target="tpu_custom_call", output_to_operand_aliasing={{}: (5, {})} | custom-call | tf_op jit(solution)/shard_map/gram_more/pallas_call | solution.py:326
  64.0 1.8 %collective-permute-done.3.refs_0_ = bf16[896,128]{1,0:T(8,128)(2,1)S(1)} collective-permute-done((bf16[896,128]{1,0:T(8,128)(2,1)S(1)}, bf16[896,128]{1,0:T(8,128)(2,1)S(1)}, u32[]{:S(2)}, u32[]{:S(2)}) %collective-permute-start.3) | collective-permute-done | bytes 229408 | tf_op jit(solution)/shard_map/ppermute | solution.py:362
  65.8 2.2 %gram_more.3 = f32[36,256,128]{2,1,0:T(8,128)} custom-call(bf16[896,128]{1,0:T(8,128)(2,1)S(1)} %collective-permute-done.3.refs_0_, bf16[2336,128]{1,0:T(8,128)(2,1)S(1)} %collective-permute-done.4.refs_1_, f32[128,128]{1,0:T(8,128)S(1)} %get-tuple-element.23.refs_2_, ...), custom_call_target="tpu_custom_call", output_to_operand_aliasing={{}: (5, {})} | custom-call | tf_op jit(solution)/shard_map/gram_more/pallas_call | solution.py:326
  (14 shorter events, 0.2 us)
Async XLA Ops:
  0.0 1.9 %copy-start.1 = (bf16[288,2048]{1,0:T(8,128)(2,1)S(1)}, bf16[288,2048]{1,0:T(8,128)(2,1)}, u32[]{:S(2)}) copy-start(bf16[288,2048]{1,0:T(8,128)(2,1)} %constant.6.clone.basis) | copy-start | bytes 3538948
  1.9 7.6 %copy-start.3 = (f32[31]{0:T(128)S(1)}, f32[31]{0:T(128)}, u32[]{:S(2)}) copy-start(f32[31]{0:T(128)} %taps.3) | copy-start | bytes 376
  2.7 14.6 %collective-permute-start = (bf16[288,256]{1,0:T(8,128)(2,1)S(1)}, bf16[288,256]{1,0:T(8,128)(2,1)S(1)}, u32[]{:S(2)}, u32[]{:S(2)}) collective-permute-start(bf16[288,256]{1,0:T(8,128)(2,1)S(1)} %get-tuple-element.15), channel_id=1, source_target_pairs={{0,4},{4,8},{8,12},{12,16},{16,20},{20,24},{24,28},{28,32},{32,36}... | collective-permute-start | bytes 442376 | tf_op jit(solution)/shard_map/ppermute | solution.py:343
  7.6 11.4 %collective-permute-start.1 = (bf16[288,256]{1,0:T(8,128)(2,1)S(1)}, bf16[288,256]{1,0:T(8,128)(2,1)S(1)}, u32[]{:S(2)}, u32[]{:S(2)}) collective-permute-start(bf16[288,256]{1,0:T(8,128)(2,1)S(1)} %get-tuple-element.16), channel_id=1, source_target_pairs={{4,0},{8,4},{12,8},{16,12},{20,16},{24,20},{28,24},{32,28},{36,32}... | collective-permute-start | bytes 442376 | tf_op jit(solution)/shard_map/ppermute | solution.py:344
  9.5 3.4 %copy-start = (bf16[16,128,2048]{2,1,0:T(8,128)(2,1)S(1)}, bf16[16,128,2048]{2,1,0:T(8,128)(2,1)}, u32[]{:S(2)}) copy-start(bf16[16,128,2048]{2,1,0:T(8,128)(2,1)} %raw.1) | copy-start | bytes 25165828
  12.9 6.1 %copy-start.2 = (s32[16,128]{1,0:T(8,128)S(1)}, s32[16,128]{1,0:T(8,128)}, u32[]{:S(2)}) copy-start(s32[16,128]{1,0:T(8,128)} %mask.1) | copy-start | bytes 24580
  22.1 2.8 %collective-permute-start.2 = (bf16[2336,128]{1,0:T(8,128)(2,1)S(1)}, bf16[2336,128]{1,0:T(8,128)(2,1)S(1)}, u32[]{:S(2)}, u32[]{:S(2)}) collective-permute-start(bf16[2336,128]{1,0:T(8,128)(2,1)S(1)} %get-tuple-element.18), channel_id=1, source_target_pairs={{0,1},{1,0},{2,3},{3,2},{4,5},{5,4},{6,7},{7,6},{8,9},{9,8},{10,11... | collective-permute-start | bytes 1794056 | tf_op jit(solution)/shard_map/ppermute | solution.py:350
  22.3 12.9 %collective-permute-start.6 = (bf16[1168,128]{1,0:T(8,128)(2,1)S(1)}, bf16[1168,128]{1,0:T(8,128)(2,1)S(1)}, u32[]{:S(2)}, u32[]{:S(2)}) collective-permute-start(bf16[1168,128]{1,0:T(8,128)(2,1)S(1)} %get-tuple-element.19), channel_id=1, source_target_pairs={{0,2},{1,3},{2,0},{3,1},{4,6},{5,7},{6,4},{7,5},{8,10},{9,11},{10,... | collective-permute-start | bytes 897032 | tf_op jit(solution)/shard_map/ppermute | solution.py:352
  25.0 21.7 %collective-permute-start.7 = (bf16[1168,128]{1,0:T(8,128)(2,1)S(1)}, bf16[1168,128]{1,0:T(8,128)(2,1)S(1)}, u32[]{:S(2)}, u32[]{:S(2)}) collective-permute-start(bf16[1168,128]{1,0:T(8,128)(2,1)S(1)} %get-tuple-element.28), channel_id=1, source_target_pairs={{0,2},{1,3},{2,0},{3,1},{4,6},{5,7},{6,4},{7,5},{8,10},{9,11},{10,... | collective-permute-start | bytes 897032 | tf_op jit(solution)/shard_map/ppermute | solution.py:352
  27.0 30.8 %collective-permute-start.4 = (bf16[2336,128]{1,0:T(8,128)(2,1)S(1)}, bf16[2336,128]{1,0:T(8,128)(2,1)S(1)}, u32[]{:S(2)}, u32[]{:S(2)}) collective-permute-start(bf16[2336,128]{1,0:T(8,128)(2,1)S(1)} %pad_maximum_fusion), channel_id=1, source_target_pairs={{6,0},{7,1},{4,2},{5,3},{10,4},{11,5},{8,6},{9,7},{14,8},{15,9},{1... | collective-permute-start | bytes 1794056 | tf_op jit(solution)/shard_map/ppermute | solution.py:362
  28.9 28.8 %collective-permute-start.5 = (bf16[672,128]{1,0:T(8,128)(2,1)S(1)}, bf16[672,128]{1,0:T(8,128)(2,1)S(1)}, u32[]{:S(2)}, u32[]{:S(2)}) collective-permute-start(bf16[672,128]{1,0:T(8,128)(2,1)S(1)} %pad_maximum_fusion.4), channel_id=1, source_target_pairs={{4,0},{5,1},{6,2},{7,3},{8,4},{9,5},{10,6},{11,7},{12,8},{13,9},{1... | collective-permute-start | bytes 516104 | tf_op jit(solution)/shard_map/ppermute | solution.py:362
  30.9 31.1 %collective-permute-start.8 = (bf16[768,128]{1,0:T(8,128)(2,1)S(1)}, bf16[768,128]{1,0:T(8,128)(2,1)S(1)}, u32[]{:S(2)}, u32[]{:S(2)}) collective-permute-start(bf16[768,128]{1,0:T(8,128)(2,1)S(1)} %pad_maximum_fusion.3), channel_id=1, source_target_pairs={{4,0},{5,1},{6,2},{7,3},{8,4},{9,5},{10,6},{11,7},{12,8},{13,9},{1... | collective-permute-start | bytes 589832 | tf_op jit(solution)/shard_map/ppermute | solution.py:362
  35.1 30.7 %collective-permute-start.3 = (bf16[896,128]{1,0:T(8,128)(2,1)S(1)}, bf16[896,128]{1,0:T(8,128)(2,1)S(1)}, u32[]{:S(2)}, u32[]{:S(2)}) collective-permute-start(bf16[896,128]{1,0:T(8,128)(2,1)S(1)} %pad_maximum_fusion.2), channel_id=1, source_target_pairs={{4,0},{5,1},{6,2},{7,3},{8,4},{9,5},{10,6},{11,7},{12,8},{13,9},{1... | collective-permute-start | bytes 688136 | tf_op jit(solution)/shard_map/ppermute | solution.py:362
